TPU v7x, 32 devices: a whole 2x2x4 slice. The times are simulated.
32 devices in a mesh: px: 8 (over z, y), py: 4 (over x, core).
Axes of the slice: x: 2, y: 2, z: 4, core: 2. Of those that a mesh axis runs over, the one named last changes fastest.
Arguments:
- eta_boxes: float32 [128, 32, 32, 128], P(('px', 'py')), may hold values from 0 to 1
- corners: int32 [128, 2], P(('px', 'py')), may hold values from 0 to 95, as said below
- grain_ids: int32 [128], P(('px', 'py')), may hold values from 0 to 23
- misfit: float32 [24], replicated, may hold values from -1 to 1
- green: float32 [128, 768, 512], P('px', 'py'), may hold values from 0.25 to 2.5
Outputs:
- eta_next: float32 [128, 32, 32, 128], P(('px', 'py'))
- potential: float32 [768, 512, 128], P('px', 'py')
Inputs may be any that keep to these rules, and one draw needn't show every extreme that they name: Box b lies with device d = b // 4 (px index p = d // 4, py index q = d % 4): 8 corners[b,0] lies in [p * 96, (p + 1) * 96) and 8 corners[b,1] in [q * 128, (q + 1) * 128). Among each device's boxes one has its corner at the last tile grid position of that device's cells in both columns.
All inputs are finite; a program needn't handle non-finite values.
Results may differ from a plain program's by a relative error of at most 0.000075.
Values sent between devices are 32-bit elements; how exact they have to be, the bound alone decides.
No kernel may reach another device: no remote copies, remote signals or barrier semaphores. Data moves between devices by JAX's collectives and lax.ppermute only.
A program may use at most 192 MiB of HBM per device.

v0:
```python
import math

import jax
import jax.numpy as jnp
from jax import lax
from jax.sharding import PartitionSpec as P

NX = 768
NY = 512
NZ = 128
BX = 32
BY = 32
STEP = 8


rate_step = 0.2
gradient_coef = 0.1
coupling = 1.5
precise_mode = lax.Precision.HIGHEST


def from_behind(shard, axis, by):
    peers = lax.axis_size(axis)
    return lax.ppermute(shard, axis, [(i, (i + by) % peers) for i in range(peers)])


def laplace(values):
    padded = jnp.pad(values, ((1, 1), (1, 1), (0, 0)))
    beside_all = padded[2:, 1:-1] + padded[:-2, 1:-1] + padded[1:-1, 2:] + padded[1:-1, :-2]
    beside_all = beside_all + jnp.roll(values, 1, axis=2) + jnp.roll(values, -1, axis=2)
    return beside_all - 6.0 * values


def advance(order_param, weight, field_mu, occupancy):
    square = order_param * order_param
    force = order_param * square - order_param + 2.0 * coupling * order_param * (occupancy - square)
    force = force - gradient_coef * laplace(order_param) + 2.0 * weight * order_param * field_mu
    return order_param - rate_step * force


def spectra(length):
    counter = jnp.arange(length, dtype=jnp.int32)
    phase_index = counter[:, None] * counter[None, :] % length
    angles = phase_index.astype(jnp.float32) * (2.0 * math.pi / length)
    return (jnp.cos(angles), jnp.sin(angles))


def product(pattern, operand, table_mat):
    return jnp.einsum(pattern, operand, table_mat, precision=precise_mode)


def on_device(eta_boxes, corners, grain_ids, misfit, green):
    rows_dev = NX // lax.axis_size("px")
    cols_dev = NY // lax.axis_size("py")
    over_x = BX - STEP
    over_y = BY - STEP
    start_x = corners[:, 0] * STEP - lax.axis_index("px") * rows_dev
    start_y = corners[:, 1] * STEP - lax.axis_index("py") * cols_dev
    variant = jnp.arange(misfit.shape[0], dtype=jnp.int32)
    weights = jnp.sum(
        jnp.where(grain_ids[:, None] == variant[None, :], misfit[None, :], 0.0), axis=1
    )
    squares = eta_boxes * eta_boxes
    anchor_zero = jnp.zeros((), jnp.int32)
    box_count = eta_boxes.shape[0]
    box_patch = jnp.zeros((2, rows_dev + over_x, cols_dev + over_y, NZ), jnp.float32)
    for box_slot in range(box_count):
        contrib = jnp.stack([weights[box_slot] * squares[box_slot], squares[box_slot]])
        position = (anchor_zero, start_x[box_slot], start_y[box_slot], anchor_zero)
        current = lax.dynamic_slice(box_patch, position, contrib.shape)
        box_patch = lax.dynamic_update_slice(box_patch, current + contrib, position)
    beside_x = from_behind(box_patch[:, rows_dev:, :cols_dev], "px", 1)
    beside_y = from_behind(box_patch[:, :rows_dev, cols_dev:], "py", 1)
    first_leg = from_behind(box_patch[:, rows_dev:, cols_dev:], "px", 1)
    diagonal = from_behind(first_leg, "py", 1)
    grid_field = box_patch[:, :rows_dev, :cols_dev]
    grid_field = grid_field.at[:, :over_x].add(beside_x)
    grid_field = grid_field.at[:, :, :over_y].add(beside_y)
    grid_field = grid_field.at[:, :over_x, :over_y].add(diagonal)
    cosine_depth, sine_depth = spectra(NZ)
    cosine_rows, sine_rows = spectra(NX)
    cosine_cols, sine_cols = spectra(NY)
    eigen_field = grid_field[0]
    depth_real = product("xyz,zk->kyx", eigen_field, cosine_depth)
    depth_imag = -product("xyz,zk->kyx", eigen_field, sine_depth)
    pieces = lax.all_to_all(
        jnp.stack([depth_real, depth_imag]), "px", split_axis=1, concat_axis=3, tiled=True
    )
    real_part = product("zyx,xk->zyk", pieces[0], cosine_rows) + product(
        "zyx,xk->zyk", pieces[1], sine_rows
    )
    imag_part = product("zyx,xk->zyk", pieces[1], cosine_rows) - product(
        "zyx,xk->zyk", pieces[0], sine_rows
    )
    along_x = jnp.stack([real_part, imag_part])
    along_y = lax.all_to_all(along_x, "py", split_axis=3, concat_axis=2, tiled=True)
    spec_real = (
        product("zyx,yk->zxk", along_y[0], cosine_cols)
        + product("zyx,yk->zxk", along_y[1], sine_cols)
    ) * green
    spec_imag = (
        product("zyx,yk->zxk", along_y[1], cosine_cols)
        - product("zyx,yk->zxk", along_y[0], sine_cols)
    ) * green
    back_real = product("zxk,ky->zyx", spec_real, cosine_cols) - product(
        "zxk,ky->zyx", spec_imag, sine_cols
    )
    back_imag = product("zxk,ky->zyx", spec_imag, cosine_cols) + product(
        "zxk,ky->zyx", spec_real, sine_cols
    )
    returned = lax.all_to_all(
        jnp.stack([back_real, back_imag]), "py", split_axis=2, concat_axis=3, tiled=True
    )
    rows_real = product("zyk,kx->zyx", returned[0], cosine_rows) - product(
        "zyk,kx->zyx", returned[1], sine_rows
    )
    rows_imag = product("zyk,kx->zyx", returned[1], cosine_rows) + product(
        "zyk,kx->zyx", returned[0], sine_rows
    )
    inverse_scale = 1.0 / (NX * NY * NZ)
    pieces = lax.all_to_all(
        jnp.stack([rows_real, rows_imag]), "px", split_axis=3, concat_axis=1, tiled=True
    )
    summed = product("kyx,kz->xyz", pieces[0], cosine_depth) - product(
        "kyx,kz->xyz", pieces[1], sine_depth
    )
    potential = summed * inverse_scale
    handed = jnp.stack([potential, grid_field[1]])
    upper_tile = from_behind(handed[:, :, :over_y], "py", -1)
    column_pair = jnp.concatenate([handed, upper_tile], axis=2)
    next_column = from_behind(column_pair[:, :over_x], "px", -1)
    window_all = jnp.concatenate([column_pair, next_column], axis=1)
    results = []
    for box_slot in range(box_count):
        position = (anchor_zero, start_x[box_slot], start_y[box_slot], anchor_zero)
        window_vals = lax.dynamic_slice(window_all, position, (2,) + eta_boxes.shape[1:])
        results.append(
            advance(eta_boxes[box_slot], weights[box_slot], window_vals[0], window_vals[1])
        )
    return (jnp.stack(results), potential)


def solution(mesh):
    in_specs = (
        P(("px", "py"), None, None, None),
        P(("px", "py"), None),
        P(("px", "py")),
        P(),
        P("px", "py", None),
    )
    out_specs = (P(("px", "py"), None, None, None), P("px", "py", None))
    return jax.shard_map(
        on_device, mesh=mesh, in_specs=in_specs, out_specs=out_specs, check_vma=False
    )
```

profile of v0, /device:TPU:5, one launch (start us, length us, event | category | flops | bytes accessed | tf_op | source)
XLA Modules:
  0.0 1982.1 jit_solution(10456744515258738720)
XLA Ops:
  16.4 4.0 broadcast_multiply_fusion
  22.9 7.6 broadcast_in_dim.14
  30.5 6.3 dynamic_update_slice.12
  38.6 5.8 dynamic_update_slice.13
  47.1 6.4 dynamic_update_slice.14
  56.3 5.7 dynamic_update_slice.15
  66.0 3.2 slice.458
  74.3 11.3 slice.454
  85.6 59.9 %collective-permute-done.2 = f32[2,24,24,128]{3,2,1,0:T(8,128)} collective-permute-done((f32[2,24,24,128]{3,2,1,0:T(8,128)}, f32[2,24,24,128]{3,2,1,0:T(8,128)}, u32[]{:S(2)}, u32[]{:S(2)}) %collective-permute-start.2) | collective-permute-done | bytes 589856 | tf_op jit(solution)/shard_map/ppermute | solution.py:24
  145.5 4.1 collective-permute-start.3
  149.6 4.0 fusion.6
  153.7 4.2 constant_dynamic-update-slice_fusion
  158.7 8.9 fusion.7
  167.6 8.2 negate_bitcast_fusion
  175.8 9.0 pad_maximum_fusion.1
  184.8 16.4 copy.89
  201.2 282.3 %all_to_all.60 = f32[2,128,128,96]{2,3,0,1:T(8,128)} all-to-all(f32[2,128,128,96]{2,3,0,1:T(8,128)} %copy.89), channel_id=1, replica_groups=mesh['px'=8,'py'=4] {'px'}, dimensions={1} | all-to-all | bytes 25165824 | tf_op jit(solution)/shard_map/all_to_all | solution.py:86
  483.5 10.7 copy.90
  494.1 8.6 fusion.253
  502.7 3.2 copy.93
  505.9 54.1 %fusion.18 = f32[16,128,768]{2,1,0:T(8,128)S(1)} fusion(f32[16,128,768]{1,2,0:T(8,128)S(1)} %bitcast.214), kind=kOutput, calls=%fused_computation.38 | convolution fusion | flops 14500823040 | bytes 12582912 | tf_op jit(solution)/shard_map/zyx,xk->zyk/dot_general | solution.py:49
  560.7 44.3 %fusion.16 = f32[16,128,768]{2,1,0:T(8,128)S(1)} fusion(f32[16,128,768]{1,2,0:T(8,128)S(1)} %bitcast.222), kind=kOutput, calls=%fused_computation.36 | convolution fusion | flops 14500823040 | bytes 12582912 | tf_op jit(solution)/shard_map/zyx,xk->zyk/dot_general | solution.py:49
  605.0 44.3 %add_bitcast_fusion.2 = f32[1,16,128,768]{3,2,1,0:T(8,128)S(1)} fusion(f32[16,128,768]{2,1,0:T(8,128)S(1)} %fusion.18, f32[16,128,768]{1,2,0:T(8,128)S(1)} %bitcast.223), kind=kOutput, calls=%fused_computation.18 | convolution fusion | flops 14502395904 | bytes 18874368 | tf_op jit(solution)/shard_map/zyx,xk->zyk/dot_general | solution.py:49
  649.3 42.1 %subtract_bitcast_fusion.2 = f32[1,16,128,768]{3,2,1,0:T(8,128)} fusion(f32[16,128,768]{2,1,0:T(8,128)S(1)} %fusion.16, f32[16,128,768]{1,2,0:T(8,128)S(1)} %bitcast.215), kind=kOutput, calls=%fused_computation.17 | convolution fusion | flops 14502395904 | bytes 18874368 | tf_op jit(solution)/shard_map/zyx,xk->zyk/dot_general | solution.py:49
  691.4 8.9 pad_maximum_fusion.2
  700.3 12.7 copy.97
  713.0 147.3 %all_to_all.61 = f32[2,16,128,768]{2,1,0,3:T(8,128)} all-to-all(f32[2,16,128,768]{2,1,0,3:T(8,128)} %copy.97), channel_id=1, replica_groups=mesh['px'=8,'py'=4] {'py'}, dimensions={3} | all-to-all | bytes 25165824 | tf_op jit(solution)/shard_map/all_to_all | solution.py:96
  860.3 16.4 copy.98
  876.7 8.5 fusion.252
  885.2 7.1 copy.99
  892.3 8.0 squeeze.139
  900.3 19.1 fusion.86
  919.4 6.9 copy.100
  926.3 7.9 squeeze.140
  934.2 18.7 fusion.82
  952.9 23.4 %add_multiply_fusion = f32[16,192,512]{2,1,0:T(8,128)S(1)} fusion(f32[16,192,512]{2,1,0:T(8,128)} %param.15, f32[16,192,512]{2,1,0:T(8,128)} %fusion.86, f32[16,512,192]{1,2,0:T(8,128)S(1)} %copy-done.2), kind=kOutput, calls=%fused_computation.16 | convolution fusion | flops 9670492160 | bytes 25165824 | tf_op jit(solution)/shard_map/zyx,yk->zxk/dot_general | solution.py:49
  976.3 16.0 fusion.84
  992.4 23.7 %subtract_multiply_fusion.1 = f32[16,192,512]{2,1,0:T(8,128)S(1)} fusion(f32[16,192,512]{2,1,0:T(8,128)} %param.15, f32[16,192,512]{2,1,0:T(8,128)} %fusion.82, f32[16,512,192]{1,2,0:T(8,128)S(1)} %bitcast.208), kind=kOutput, calls=%fused_computation.15 | convolution fusion | flops 9670492160 | bytes 25165824 | tf_op jit(solution)/shard_map/zyx,yk->zxk/dot_general | solution.py:49
  1016.1 14.1 fusion.80
  1030.3 16.2 subtract_bitcast_fusion.1
  1046.5 16.5 add_bitcast_fusion.1
  1063.0 11.6 pad_maximum_fusion.3
  1074.7 18.1 copy.101
  1092.7 194.1 %all_to_all.62 = f32[2,16,512,192]{3,1,0,2:T(8,128)} all-to-all(f32[2,16,512,192]{3,1,0,2:T(8,128)} %copy.101), channel_id=1, replica_groups=mesh['px'=8,'py'=4] {'py'}, dimensions={2} | all-to-all | bytes 25165824 | tf_op jit(solution)/shard_map/all_to_all | solution.py:111
  1286.8 14.0 copy.127
  1300.9 10.6 fusion.251
  1311.5 3.8 copy.105
  1315.4 44.1 %fusion.14 = f32[16,128,768]{2,1,0:T(8,128)S(1)} fusion(f32[16,128,768]{1,2,0:T(8,128)S(1)} %bitcast.216), kind=kOutput, calls=%fused_computation.34 | convolution fusion | flops 14500823040 | bytes 12582912 | tf_op jit(solution)/shard_map/zyk,kx->zyx/dot_general | solution.py:49
  1360.4 44.3 %fusion.12 = f32[16,128,768]{2,1,0:T(8,128)S(1)} fusion(f32[16,128,768]{1,2,0:T(8,128)S(1)} %bitcast.224), kind=kOutput, calls=%fused_computation.32 | convolution fusion | flops 14500823040 | bytes 12582912 | tf_op jit(solution)/shard_map/zyk,kx->zyx/dot_general | solution.py:49
  1404.7 44.3 %subtract_bitcast_fusion = f32[1,16,128,768]{3,2,1,0:T(8,128)S(1)} fusion(f32[16,128,768]{2,1,0:T(8,128)S(1)} %fusion.14, f32[16,128,768]{1,2,0:T(8,128)S(1)} %bitcast.225), kind=kOutput, calls=%fused_computation.12 | convolution fusion | flops 14502395904 | bytes 18874368 | tf_op jit(solution)/shard_map/zyk,kx->zyx/dot_general | solution.py:49
  1449.0 42.1 %add_bitcast_fusion = f32[1,16,128,768]{3,2,1,0:T(8,128)} fusion(f32[16,128,768]{2,1,0:T(8,128)S(1)} %fusion.12, f32[16,128,768]{1,2,0:T(8,128)S(1)} %bitcast.217), kind=kOutput, calls=%fused_computation.11 | convolution fusion | flops 14502395904 | bytes 18874368 | tf_op jit(solution)/shard_map/zyk,kx->zyx/dot_general | solution.py:49
  1491.1 8.9 pad_maximum_fusion.4
  1500.0 12.7 copy.109
  1512.7 5.5 all-to-all-start.3
  1518.2 6.3 slice.470
  1524.5 266.0 %all-to-all-done.3 = f32[2,16,128,768]{2,1,0,3:T(8,128)} async-done(((f32[2,16,128,768]{2,1,0,3:T(8,128)}), f32[2,16,128,768]{2,1,0,3:T(8,128)}, u32[]{:S(2)}, u32[]{:S(2)}) %all-to-all-start.3) | async-done | bytes 12582944 | tf_op jit(solution)/shard_map/all_to_all | solution.py:121
  1790.5 16.4 copy.110
  1806.9 8.8 fusion.250
  1815.7 3.2 copy.113
  1818.9 13.2 fusion
  1832.8 13.2 subtract_multiply_fusion
  1847.9 26.9 %collective-permute-done.4 = f32[2,96,24,128]{3,2,1,0:T(8,128)S(1)} collective-permute-done((f32[2,96,24,128]{3,2,1,0:T(8,128)S(1)}, f32[2,96,24,128]{3,2,1,0:T(8,128)S(1)}, u32[]{:S(2)}, u32[]{:S(2)}) %collective-permute-start.4) | collective-permute-done | bytes 2359328 | tf_op jit(solution)/shard_map/ppermute | solution.py:24
  1883.8 77.5 %collective-permute-done.5 = f32[2,24,152,128]{3,2,1,0:T(8,128)} collective-permute-done((f32[2,24,152,128]{3,2,1,0:T(8,128)}, f32[2,24,152,128]{3,2,1,0:T(8,128)}, u32[]{:S(2)}, u32[]{:S(2)}) %collective-permute-start.5) | collective-permute-done | bytes 3735584 | tf_op jit(solution)/shard_map/ppermute | solution.py:24
  1961.4 11.1 pad_maximum_fusion
  (77 shorter events, 40.2 us)
Async XLA Ops:
  64.1 85.5 %collective-permute-start = (f32[2,24,128,128]{3,2,1,0:T(8,128)S(1)}, f32[2,24,128,128]{3,2,1,0:T(8,128)S(1)}, u32[]{:S(2)}, u32[]{:S(2)}) collective-permute-start(f32[2,24,128,128]{3,2,1,0:T(8,128)S(1)} %slice.456), channel_id=1, source_target_pairs={{0,4},{4,8},{8,12},{12,16},{16,20},{20,24},{24,28},{28,0},{1,5},{5... | collective-permute-start | bytes 9437192 | tf_op jit(solution)/shard_map/ppermute | solution.py:24
  69.3 84.4 %collective-permute-start.1 = (f32[2,96,24,128]{3,2,1,0:T(8,128)}, f32[2,96,24,128]{3,2,1,0:T(8,128)}, u32[]{:S(2)}, u32[]{:S(2)}) collective-permute-start(f32[2,96,24,128]{3,2,1,0:T(8,128)} %slice.458), channel_id=1, source_target_pairs={{0,1},{1,2},{2,3},{3,0},{4,5},{5,6},{6,7},{7,4},{8,9},{9,10},{10,1... | collective-permute-start | bytes 7077896 | tf_op jit(solution)/shard_map/ppermute | solution.py:24
  73.3 72.2 %collective-permute-start.2 = (f32[2,24,24,128]{3,2,1,0:T(8,128)}, f32[2,24,24,128]{3,2,1,0:T(8,128)}, u32[]{:S(2)}, u32[]{:S(2)}) collective-permute-start(f32[2,24,24,128]{3,2,1,0:T(8,128)} %slice.460), channel_id=1, source_target_pairs={{0,4},{4,8},{8,12},{12,16},{16,20},{20,24},{24,28},{28,0},{1,5},{5... | collective-permute-start | bytes 1769480 | tf_op jit(solution)/shard_map/ppermute | solution.py:24
  145.5 12.3 collective-permute-start.3
  158.7 8.9 copy-start.1
  892.3 27.1 %slice-start.8 = ((s8[6291456]{0:T(1024)(128)(4,1)}), s8[2097152]{0:T(1024)(128)(4,1)S(1)}, s32[]{:S(2)}) async-start(s8[6291456]{0:T(1024)(128)(4,1)} %bitcast.218), calls=%async_computation.12 | async-start | bytes 4194304
  900.3 19.1 slice-start.9
  934.2 18.7 copy-start.2
  934.2 58.2 %slice-start.6 = ((s8[6291456]{0:T(1024)(128)(4,1)}), s8[4194304]{0:T(1024)(128)(4,1)S(1)}, s32[]{:S(2)}) async-start(s8[6291456]{0:T(1024)(128)(4,1)} %bitcast.207), calls=%async_computation.10 | async-start | bytes 8388608
  952.9 39.5 %slice-start.7 = ((s8[6291456]{0:T(1024)(128)(4,1)}), s8[2097152]{0:T(1024)(128)(4,1)S(1)}, s32[]{:S(2)}) async-start(s8[6291456]{0:T(1024)(128)(4,1)} %bitcast.207), calls=%async_computation.11 | async-start | bytes 4194304
  1016.1 14.2 copy-start.3
  1311.5 48.0 %slice-start.10 = ((s8[6291456]{0:T(1024)(128)(4,1)}), s8[4194304]{0:T(1024)(128)(4,1)S(1)}, s32[]{:S(2)}) async-start(s8[6291456]{0:T(1024)(128)(4,1)} %bitcast.220), calls=%async_computation.14 | async-start | bytes 8388608
  1315.3 44.1 %slice-start.11 = ((s8[6291456]{0:T(1024)(128)(4,1)}), s8[2097152]{0:T(1024)(128)(4,1)S(1)}, s32[]{:S(2)}) async-start(s8[6291456]{0:T(1024)(128)(4,1)} %bitcast.220), calls=%async_computation.15 | async-start | bytes 4194304
  1512.7 277.8 %all-to-all-start.3 = ((f32[2,16,128,768]{2,1,0,3:T(8,128)}), f32[2,16,128,768]{2,1,0,3:T(8,128)}, u32[]{:S(2)}, u32[]{:S(2)}) async-start(f32[2,16,128,768]{2,1,0,3:T(8,128)} %copy.109), calls=%async_computation.3 | async-start | bytes 25165824 | tf_op jit(solution)/shard_map/all_to_all | solution.py:121
  1832.1 13.9 slice-start.2
  1832.8 13.3 slice-start.3
  1846.0 28.8 %copy-start = (f32[128,128,96]{0,1,2:T(8,128)}, f32[128,128,96]{0,1,2:T(8,128)S(1)}, u32[]{:S(2)}) copy-start(f32[128,128,96]{0,1,2:T(8,128)S(1)} %subtract_multiply_fusion) | copy-start | bytes 18874372
  1846.3 28.4 %collective-permute-start.4 = (f32[2,96,24,128]{3,2,1,0:T(8,128)S(1)}, f32[2,96,24,128]{3,2,1,0:T(8,128)S(1)}, u32[]{:S(2)}, u32[]{:S(2)}) collective-permute-start(f32[2,96,24,128]{3,2,1,0:T(8,128)S(1)} %pad_maximum_fusion.7), channel_id=1, source_target_pairs={{0,3},{1,0},{2,1},{3,2},{4,7},{5,4},{6,5},{7,6},{8,11},{9,8},{10,9... | collective-permute-start | bytes 7077896 | tf_op jit(solution)/shard_map/ppermute | solution.py:24
  1874.8 2.8 copy-start.4
  1874.8 86.6 %slice-start.4 = ((s8[6291456]{0:T(1024)(128)(4,1)}), s8[2097152]{0:T(1024)(128)(4,1)S(1)}, s32[]{:S(2)}) async-start(s8[6291456]{0:T(1024)(128)(4,1)} %bitcast.204), calls=%async_computation.8 | async-start | bytes 4194304
  1877.5 83.8 %collective-permute-start.5 = (f32[2,24,152,128]{3,2,1,0:T(8,128)}, f32[2,24,152,128]{3,2,1,0:T(8,128)}, u32[]{:S(2)}, u32[]{:S(2)}) collective-permute-start(f32[2,24,152,128]{3,2,1,0:T(8,128)} %pad_maximum_fusion.5), channel_id=1, source_target_pairs={{0,28},{4,0},{8,4},{12,8},{16,12},{20,16},{24,20},{28,24},{1,29},{... | collective-permute-start | bytes 11206664 | tf_op jit(solution)/shard_map/ppermute | solution.py:24
  1880.4 81.0 %slice-start.5 = ((s8[6291456]{0:T(1024)(128)(4,1)}), s8[4194304]{0:T(1024)(128)(4,1)S(1)}, s32[]{:S(2)}) async-start(s8[6291456]{0:T(1024)(128)(4,1)} %bitcast.204), calls=%async_computation.9 | async-start | bytes 8388608
  1882.6 78.7 %slice-start = ((s8[6291456]{0:T(1024)(128)(4,1)}), s8[4194304]{0:T(1024)(128)(4,1)S(1)}, s32[]{:S(2)}) async-start(s8[6291456]{0:T(1024)(128)(4,1)} %bitcast.199), calls=%async_computation.4 | async-start | bytes 8388608
  1882.7 78.7 %copy-start.5 = (f32[2,96,24,128]{3,2,1,0:T(8,128)S(1)}, f32[2,96,24,128]{3,2,1,0:T(8,128)}, u32[]{:S(2)}) copy-start(f32[2,96,24,128]{3,2,1,0:T(8,128)} %copy-done.4) | copy-start | bytes 7077892
  1883.0 78.3 %slice-start.1 = ((s8[6291456]{0:T(1024)(128)(4,1)}), s8[2097152]{0:T(1024)(128)(4,1)S(1)}, s32[]{:S(2)}) async-start(s8[6291456]{0:T(1024)(128)(4,1)} %bitcast.199), calls=%async_computation.5 | async-start | bytes 4194304
where the time goes:
time: 1990 us; the launch traced here: 1980 us
  blocking collectives  624 us (31%)
  matrix products  551 us (28%)
  waiting for transfers between devices  430 us (22%)
  local copies, waits for them, and re-layouts  258 us (13%)
  other arithmetic  83.5 us (4%)
    dot_general x20, matrix products, product(): return jnp.einsum(pattern, operand, table_mat, precision=precise_mode)  551 us
    all_to_all x1, blocking collectives, on_device(): lax.all_to_all(jnp.stack([depth_real, depth_imag]), 'px', split_axis=1, c...  282 us
    all_to_all x1, waiting for transfers between devices, on_device(): lax.all_to_all(jnp.stack([rows_real, rows_imag]), 'px', split_axis=3, con...  266 us
    all_to_all x1, blocking collectives, on_device(): lax.all_to_all(jnp.stack([back_real, back_imag]), 'py', split_axis=2, con...  194 us
    ppermute x6, waiting for transfers between devices, from_behind(): lax.ppermute(shard, axis, [(i, (i + by) % peers) for i in range(peers)])  164 us
    all_to_all x1, blocking collectives, on_device(): lax.all_to_all(along_x, 'py', split_axis=3, concat_axis=2, tiled=True)  147 us
  transfers between devices with their start and end apart: 7, of which 4 were waited for; matrix products, arithmetic and copies ran while one was open for 2% of the time, Pallas kernels for 0%

commit v1 on v0

v1 whole, which is shorter than its diff:
```python
import functools
import math

import jax
import jax.numpy as jnp
import ml_dtypes
import numpy as np
from jax import lax
from jax.experimental import pallas as pl
from jax.experimental.pallas import tpu as pltpu
from jax.sharding import PartitionSpec as P

STEP = 8
LANES = 128
RADIX = 3

rate_step = 0.2
gradient_coef = 0.1
coupling = 1.5

F32 = jnp.float32
BF16 = jnp.bfloat16
MIB = 1 << 20


def from_behind(shard, axis, by):
    peers = lax.axis_size(axis)
    return lax.ppermute(shard, axis, [(i, (i + by) % peers) for i in range(peers)])


def laplace(values):
    padded = jnp.pad(values, ((1, 1), (1, 1), (0, 0)))
    beside_all = padded[2:, 1:-1] + padded[:-2, 1:-1] + padded[1:-1, 2:] + padded[1:-1, :-2]
    beside_all = beside_all + jnp.roll(values, 1, axis=2) + jnp.roll(values, -1, axis=2)
    return beside_all - 6.0 * values


def advance(order_param, weight, field_mu, occupancy):
    square = order_param * order_param
    force = order_param * square - order_param + 2.0 * coupling * order_param * (occupancy - square)
    force = force - gradient_coef * laplace(order_param) + 2.0 * weight * order_param * field_mu
    return order_param - rate_step * force


def pair_of(table):
    high = table.astype(ml_dtypes.bfloat16)
    low = (table - high.astype(np.float64)).astype(ml_dtypes.bfloat16)
    return high, low


def angle_of(index, length):
    return (index % length) * (2.0 * math.pi / length)


def plane_frequencies(depth, owners):
    own = depth // owners
    half = own // 2
    return [[own * p + t + (1 if p < owners // 2 else 0) for t in range(half)] for p in range(owners)]


def depth_tables(depth, owners, scale):
    freqs = plane_frequencies(depth, owners)
    z = np.arange(depth)
    forward, inverse = [], []
    for p in range(owners):
        real, imag, real_inv, imag_inv = [], [], [], []
        for t, freq in enumerate(freqs[p]):
            angles = angle_of(freq * z, depth)
            if p == owners // 2 and t == 0:
                real.append(np.cos(angles))
                imag.append(np.ones(depth))
                real_inv.append(0.5 * scale * np.cos(angles))
                imag_inv.append(np.full(depth, 0.5 * scale))
            else:
                real.append(np.cos(angles))
                imag.append(-np.sin(angles))
                real_inv.append(scale * np.cos(angles))
                imag_inv.append(-scale * np.sin(angles))
        forward += real + imag
        inverse += real_inv + imag_inv
    return pair_of(np.array(forward)), pair_of(np.array(inverse))


def row_tables(length):
    part = length // RADIX
    m = np.arange(part)
    forward, inverse = [], []
    for l in range(RADIX):
        angles = angle_of(m[:, None] * (RADIX * m[None, :] + l), length)
        c, s = np.cos(angles), np.sin(angles)
        forward.append(np.block([[c, s], [-s, c]]))
        c, s = c.T, s.T
        inverse.append(np.block([[c, -s], [s, c]]))
    return pair_of(np.array(forward)), pair_of(np.array(inverse))


def column_tables(length):
    part = length // 2
    m = np.arange(part)
    forward, inverse = [], []
    for parity in range(2):
        angles = angle_of(m[:, None] * (2 * m[None, :] + parity), length)
        c, s = np.cos(angles), np.sin(angles)
        forward.append(np.block([[c, -s], [s, c]]))
        c, s = c.T, s.T
        inverse.append(np.block([[c, s], [-s, c]]))
    return pair_of(np.array(forward)), pair_of(np.array(inverse))


def mirror_tables(rows, length):
    part = length // 2
    m = np.arange(part)
    order = np.concatenate([2 * m, 2 * m + 1])
    straight = np.zeros((length, length))
    straight[order, np.arange(length)] = 1.0
    mirrored = np.zeros((length, length))
    mirrored[(length - order) % length, np.arange(length)] = 1.0
    flip = np.zeros((rows, rows))
    i = np.arange(1, rows)
    flip[i, rows - i] = 1.0
    as_bf16 = lambda table: table.astype(ml_dtypes.bfloat16)
    return as_bf16(straight), as_bf16(mirrored), as_bf16(flip)


def halves(values):
    high = values.astype(BF16)
    return high, (values - high.astype(F32)).astype(BF16)


def dot(a, b):
    return jnp.dot(a, b, preferred_element_type=F32)


def table_first(high, low, values):
    top, rest = halves(values)
    width = values.shape[1]
    if width % LANES == 0:
        both = dot(high, jnp.concatenate([top, rest], axis=1))
        both = both[:, :width] + both[:, width:]
    else:
        both = dot(high, top) + dot(high, rest)
    return both + dot(low, top)


def table_last(values, high, low):
    top, rest = halves(values)
    rows = values.shape[0]
    both = dot(jnp.concatenate([top, rest], axis=0), high)
    return both[:rows] + both[rows:] + dot(top, low)


def params(mib):
    return pltpu.CompilerParams(vmem_limit_bytes=mib * MIB)


def whole(array):
    rank = len(array.shape)
    return pl.BlockSpec(array.shape, lambda *_: (0,) * rank)


def depth_kernel(weights, eta, high, low, out):
    boxes, extent = eta.shape[0], eta.shape[1]
    planes = high.shape[0]
    for i in range(extent):
        rows = []
        for b in range(boxes):
            values = eta[b, i]
            rows.append(weights[b] * (values * values))
        field = jnp.concatenate(rows, axis=0)
        top, rest = halves(field)
        count = field.shape[0]
        dims = (((1,), (1,)), ((), ()))
        both = lax.dot_general(
            high[...], jnp.concatenate([top, rest], axis=0), dims, preferred_element_type=F32
        )
        small = lax.dot_general(low[...], top, dims, preferred_element_type=F32)
        out[pl.ds(i, planes, stride=extent), :] = both[:, :count] + both[:, count:] + small


def box_depth(eta_boxes, weights, tables):
    high, low = tables
    boxes, extent, span, depth = eta_boxes.shape
    planes = high.shape[0]
    return pl.pallas_call(
        depth_kernel,
        out_shape=jax.ShapeDtypeStruct((planes * extent, boxes * span), F32),
        in_specs=[
            pl.BlockSpec(memory_space=pltpu.SMEM),
            whole(eta_boxes),
            whole(high),
            whole(low),
        ],
        out_specs=pl.BlockSpec((planes * extent, boxes * span), lambda: (0, 0)),
        compiler_params=params(24),
        name="box_depth",
    )(weights, eta_boxes, high, low)


def rows_kernel(shape, place, boxes, high, low, out, lines, packed):
    owners, per_owner, half, extent, span, length, cols, over, slots, packs = shape
    step = pl.program_id(0)
    lane = lax.broadcasted_iota(jnp.int32, (extent, LANES), 1)
    side = lines.shape[0]

    @pl.when(step == 0)
    def _():
        packed[...] = jnp.zeros(packed.shape, F32)

    @pl.when((step == 0) | ((step >= 2) & (step <= half)))
    def _():
        lines[...] = jnp.zeros(lines.shape, F32)

        def add_owner(s, carry):
            for b in range(per_owner):
                at = s * per_owner + b
                first = pl.multiple_of(place[2 * at], STEP)
                column = place[2 * at + 1]
                inside = (lane >= b * span) & (lane < (b + 1) * span)
                shift = lax.rem(column + (LANES - b * span), LANES)
                for ri in range(2):
                    moved = pltpu.roll(jnp.where(inside, boxes[s, ri, 0], 0.0), shift, axis=1)
                    where_to = pl.ds(first, extent)
                    lines[0, ri, where_to, :] += jnp.where(lane >= column, moved, 0.0)
                    if side > 1:

                        @pl.when(column + span > LANES)
                        def _():
                            lines[1, ri, where_to, :] += jnp.where(lane < column, moved, 0.0)

            return carry

        lax.fori_loop(0, owners, add_owner, 0)
        lines[:, :, :extent, :] += lines[:, :, length:, :]

    sign = jnp.where(step == 1, -1.0, 1.0).astype(F32)

    for k in range(half + 1):
        slot = half if k == 1 else max(k - 1, 0)

        @pl.when(step == k)
        def _(slot=slot):
            lanes_all = lax.broadcasted_iota(jnp.int32, (length, LANES), 1)
            for ri in range(2):
                beyond = lines[side - 1, ri, :length, :]
                if side == 1:
                    beyond = jnp.where(lanes_all >= cols, beyond, 0.0)
                shift = ((slot % slots) * over - (cols % LANES)) % LANES
                if shift:
                    beyond = pltpu.roll(beyond, shift, axis=1)
                packed[slot // slots, ri] += beyond * (sign if ri else 1.0)

    for k in range(packs):

        @pl.when(step == half + 1 + k)
        def _(k=k):
            lines[0, :, :length, :] = packed[k]

    part = length // RADIX
    terms = []
    for l in range(RADIX):
        take = pl.ds(l, part, stride=RADIX)
        values = jnp.concatenate([lines[0, 0, take, :], lines[0, 1, take, :] * sign], axis=0)
        terms.append(table_first(high[l], low[l], values))
    real, imag = [v[:part] for v in terms], [v[part:] for v in terms]
    root = math.sqrt(0.75)
    sum_re, sum_im = real[1] + real[2], imag[1] + imag[2]
    dif_re, dif_im = root * (real[1] - real[2]), root * (imag[1] - imag[2])
    mid_re, mid_im = real[0] - 0.5 * sum_re, imag[0] - 0.5 * sum_im
    result_re = jnp.concatenate([real[0] + sum_re, mid_re + dif_im, mid_re - dif_im], axis=0)
    result_im = jnp.concatenate([imag[0] + sum_im, mid_im - dif_re, mid_im + dif_re], axis=0)
    block = (out.shape[0], out.shape[3], LANES)
    out[:, 0, 0] = result_re.reshape(block)[:, :, :cols]
    out[:, 1, 0] = result_im.reshape(block)[:, :, :cols]


def box_rows(pieces, place, tables, shape, parts):
    owners, per_owner, half, extent, span, length, cols, over, slots, packs = shape
    high, low = tables
    planes = half + 1 + packs
    rows = length // parts
    side = -(-(cols + over) // LANES)

    def plane_out(k, place):
        return (0, 0, jnp.where(k == 1, half, jnp.where(k > half, k, jnp.maximum(k - 1, 0))), 0, 0)

    return pl.pallas_call(
        functools.partial(rows_kernel, shape),
        out_shape=jax.ShapeDtypeStruct((parts, 2, planes, rows, cols), F32),
        grid_spec=pltpu.PrefetchScalarGridSpec(
            num_scalar_prefetch=1,
            grid=(planes,),
            in_specs=[
                pl.BlockSpec(
                    (owners, 2, 1, extent, LANES),
                    lambda k, place: (0, 0, jnp.clip(k - 1, 0, half - 1), 0, 0),
                ),
                whole(high),
                whole(low),
            ],
            out_specs=pl.BlockSpec((parts, 2, 1, rows, cols), plane_out),
            scratch_shapes=[
                pltpu.VMEM((side, 2, length + extent, LANES), F32),
                pltpu.VMEM((packs, 2, length, LANES), F32),
            ],
        ),
        compiler_params=params(44),
        name="box_rows",
    )(place, pieces, high, low)


def columns_kernel(slots, over, has_packs, main, conj, *rest):
    if has_packs:
        pack, conj_pack = rest[:2]
        rest = rest[2:]
    own, mirror, first_gain, conj_gain, fwd_high, fwd_low, inv_high, inv_low, out, scratch = rest
    step = pl.program_id(0)
    parts, rows, cols = out.shape[0], out.shape[3], out.shape[4]
    half_length = fwd_high.shape[1] // 2

    def gathered(body, overhang, slot):
        pieces = []
        for ri in range(2):
            line = []
            for q in range(parts):
                piece = body[q, ri, 0]
                if has_packs:
                    lane = lax.broadcasted_iota(jnp.int32, piece.shape, 1)
                    shift = lax.rem(cols - over * slot, cols)
                    beyond = pltpu.roll(overhang[(q - 1) % parts, ri, 0], shift, axis=1)
                    piece = piece + jnp.where(lane < over, beyond, 0.0)
                line.append(piece)
            pieces.append(jnp.concatenate(line, axis=1) if parts > 1 else line[0])
        lower = [v[:, :half_length] for v in pieces]
        upper = [v[:, half_length:] for v in pieces]
        even = jnp.concatenate([a + b for a, b in zip(lower, upper)], axis=1)
        odd = jnp.concatenate([a - b for a, b in zip(lower, upper)], axis=1)
        return even, odd

    def forward(body, overhang, slot):
        even, odd = gathered(body, overhang, slot)
        return (
            table_last(even, fwd_high[0], fwd_low[0]),
            table_last(odd, fwd_high[1], fwd_low[1]),
        )

    def scaled(spectrum, gain):
        even, odd = spectrum
        left, right = gain[:, :half_length], gain[:, half_length:]
        left = jnp.concatenate([left, left], axis=1)
        right = jnp.concatenate([right, right], axis=1)
        return even * left, odd * right

    gain = jnp.where(step == 0, first_gain[...], own[0] + mirror[0])
    slot = lax.rem(step, slots)
    even, odd = scaled(forward(main, pack if has_packs else None, slot), gain)
    scratch[0] = even
    scratch[1] = odd

    @pl.when(step == 0)
    def _():
        slot = pl.num_programs(0) % slots
        even, odd = scaled(forward(conj, conj_pack if has_packs else None, slot), conj_gain[...])
        scratch[0] += even
        scratch[1] += odd

    even = table_last(scratch[0], inv_high[0], inv_low[0])
    odd = table_last(scratch[1], inv_high[1], inv_low[1])
    lower, upper = even + odd, even - odd
    for ri in range(2):
        take = slice(ri * half_length, (ri + 1) * half_length)
        line = jnp.concatenate([lower[:, take], upper[:, take]], axis=1)
        for q in range(parts):
            out[q, ri, 0] = line[:, q * cols : (q + 1) * cols]


def grid_columns(arrived, own, mirror, first_gain, conj_gain, forward, inverse, slots, over, packs):
    parts, _, planes, rows, cols = arrived.shape
    half = own.shape[0]
    length = own.shape[2]
    has_packs = packs > 0
    one = (parts, 2, 1, rows, cols)
    operands = [arrived, arrived]
    specs = [
        pl.BlockSpec(one, lambda t: (0, 0, t, 0, 0)),
        pl.BlockSpec(one, lambda t: (0, 0, half, 0, 0)),
    ]
    if has_packs:
        operands += [arrived, arrived]
        specs += [
            pl.BlockSpec(one, lambda t: (0, 0, half + 1 + t // slots, 0, 0)),
            pl.BlockSpec(one, lambda t: (0, 0, half + 1 + half // slots, 0, 0)),
        ]
    gain_spec = pl.BlockSpec((1, rows, length), lambda t: (t, 0, 0))
    tables = [*forward, *inverse]
    return pl.pallas_call(
        functools.partial(columns_kernel, slots, over, has_packs),
        out_shape=jax.ShapeDtypeStruct((parts, 2, half, rows, cols), F32),
        grid=(half,),
        in_specs=specs
        + [gain_spec, gain_spec, whole(first_gain), whole(conj_gain)]
        + [whole(t) for t in tables],
        out_specs=pl.BlockSpec(one, lambda t: (0, 0, t, 0, 0)),
        scratch_shapes=[pltpu.VMEM((2, rows, length), F32)],
        compiler_params=params(44),
        name="grid_columns",
    )(*operands, own, mirror, first_gain, conj_gain, *tables)


def back_rows_kernel(body, high, low, out):
    parts, rows, cols = body.shape[0], body.shape[3], body.shape[4]
    length = parts * rows
    part = length // RADIX
    owners, group = out.shape[0], out.shape[3] // RADIX
    real = body[:, 0, 0].reshape(length, cols)
    imag = body[:, 1, 0].reshape(length, cols)
    real = [real[t * part : (t + 1) * part] for t in range(RADIX)]
    imag = [imag[t * part : (t + 1) * part] for t in range(RADIX)]
    root = math.sqrt(0.75)
    sum_re, sum_im = real[1] + real[2], imag[1] + imag[2]
    dif_re, dif_im = root * (real[1] - real[2]), root * (imag[1] - imag[2])
    mid_re, mid_im = real[0] - 0.5 * sum_re, imag[0] - 0.5 * sum_im
    terms = [
        (real[0] + sum_re, imag[0] + sum_im),
        (mid_re - dif_im, mid_im + dif_re),
        (mid_re + dif_im, mid_im - dif_re),
    ]
    for l in range(RADIX):
        result = table_first(high[l], low[l], jnp.concatenate(terms[l], axis=0))
        for ri in range(2):
            values = result[ri * part : (ri + 1) * part].reshape(owners, group, cols)
            out[:, ri, 0, l * group : (l + 1) * group, :] = values


def back_rows(arrived, tables, owners):
    high, low = tables
    parts, _, half, rows, cols = arrived.shape
    length = parts * rows
    return pl.pallas_call(
        back_rows_kernel,
        out_shape=jax.ShapeDtypeStruct((owners, 2, half, length // owners, cols), F32),
        grid=(half,),
        in_specs=[
            pl.BlockSpec((parts, 2, 1, rows, cols), lambda t: (0, 0, t, 0, 0)),
            whole(high),
            whole(low),
        ],
        out_specs=pl.BlockSpec((owners, 2, 1, length // owners, cols), lambda t: (0, 0, t, 0, 0)),
        compiler_params=params(44),
        name="back_rows",
    )(arrived, high, low)


def back_depth_kernel(rows, body, high, low, out):
    planes = high.shape[0]
    group = out.shape[0]
    dims = (((0,), (0,)), ((), ()))
    for g in range(group):
        for l in range(RADIX):
            values = body[pl.ds(l * group + g, planes, stride=rows), :]
            top, rest = halves(values)
            total = lax.dot_general(top, high[...], dims, preferred_element_type=F32)
            total += lax.dot_general(rest, high[...], dims, preferred_element_type=F32)
            total += lax.dot_general(top, low[...], dims, preferred_element_type=F32)
            out[g, l] = total


def back_depth(arrived, tables):
    high, low = tables
    planes, depth = high.shape
    rows, cols = arrived.shape[-2:]
    body = arrived.reshape(planes * rows, cols)
    group = rows // RADIX
    found = pl.pallas_call(
        functools.partial(back_depth_kernel, rows),
        out_shape=jax.ShapeDtypeStruct((group, RADIX, cols, depth), F32),
        in_specs=[whole(body), whole(high), whole(low)],
        out_specs=pl.BlockSpec((group, RADIX, cols, depth), lambda: (0, 0, 0, 0)),
        compiler_params=params(48),
        name="back_depth",
    )(body, high, low)
    return found.reshape(rows, cols, depth)


def mirror_kernel(index, own, other, edge, straight, mirrored, flip, own_out, mirror_out):
    rows, length = own.shape[1], own.shape[2]
    top, rest = halves(own[0])
    both = dot(jnp.concatenate([top, rest], axis=0), straight[...])
    own_out[0] = both[:rows] + both[rows:]
    top, rest = halves(other[0])
    turned = dot(flip[...], jnp.concatenate([top, rest], axis=1))
    edge_top, edge_rest = halves(edge[0])
    row = lax.broadcasted_iota(jnp.int32, (rows, length), 0)
    top = jnp.where(row == 0, edge_top.astype(F32), turned[:, :length])
    rest = jnp.where(row == 0, edge_rest.astype(F32), turned[:, length:])
    both = dot(jnp.concatenate([top, rest], axis=0).astype(BF16), mirrored[...])
    mirror_out[0] = both[:rows] + both[rows:]


def mirror_planes(green, edge, index, count, tables):
    rows, length = green.shape[1:]
    block = (1, rows, length)
    out = jax.ShapeDtypeStruct((count, rows, length), F32)
    return pl.pallas_call(
        mirror_kernel,
        out_shape=[out, out],
        grid_spec=pltpu.PrefetchScalarGridSpec(
            num_scalar_prefetch=1,
            grid=(count,),
            in_specs=[
                pl.BlockSpec(block, lambda t, index: (index[t], 0, 0)),
                pl.BlockSpec(block, lambda t, index: (index[count + t], 0, 0)),
                pl.BlockSpec((1, 1, length), lambda t, index: (index[count + t], 0, 0)),
            ]
            + [whole(t) for t in tables],
            out_specs=[pl.BlockSpec(block, lambda t, index: (t, 0, 0))] * 2,
        ),
        compiler_params=params(24),
        name="mirror_planes",
    )(index, green, green, edge, *tables)


def multiplier(green, px, py):
    own, rows, length = green.shape
    half = own // 2
    middle = px // 2
    p = lax.axis_index("px")
    tables = mirror_tables(rows, length)
    edge = from_behind(green[:, :1, :], "py", -1)
    zeros = jnp.zeros((2,), jnp.int32)
    own_zero, mirror_zero = mirror_planes(green, edge, zeros, 1, tables)
    mirror_zero = lax.ppermute(mirror_zero, "py", [(i, py - 1 - i) for i in range(py)])
    payload = jnp.where(p == 0, 0.5 * (own_zero + mirror_zero), mirror_zero)
    pairs = [(0, middle)] + [(i, px - i) for i in range(1, middle)]
    from_zero = lax.ppermute(payload, "px", pairs)
    lower = (p < middle).astype(jnp.int32)
    t = jnp.arange(half, dtype=jnp.int32)
    index = jnp.concatenate([t + lower, jnp.minimum(own - 1 - t + lower, own - 1)])
    own_planes, mirror = mirror_planes(green, edge, index, half, tables)
    pairs = [
        (a * py + b, (px - 1 - a) * py + py - 1 - b) for a in range(px) for b in range(py)
    ]
    mirror = lax.ppermute(mirror, ("px", "py"), pairs)
    middle_own = 0.5 * (own_zero + mirror_zero)
    first = own_planes[:1] + jnp.where(p < middle, mirror[:1], from_zero)
    first = jnp.where(p == middle, middle_own + from_zero, first)
    conj = jnp.where(p == middle, middle_own - from_zero, 0.0)
    return first[0], conj[0], own_planes, mirror


def exchange(shard, axis):
    return lax.all_to_all(shard, axis, split_axis=0, concat_axis=0, tiled=True)


def occupancy_window(squares, start_x, start_y, rows_dev, cols_dev, over_x, over_y):
    box_count, _, _, depth = squares.shape
    zero = jnp.zeros((), jnp.int32)
    patch = jnp.zeros((rows_dev + over_x, cols_dev + over_y, depth), F32)
    for b in range(box_count):
        position = (start_x[b], start_y[b], zero)
        current = lax.dynamic_slice(patch, position, squares.shape[1:])
        patch = lax.dynamic_update_slice(patch, current + squares[b], position)
    beside_x = from_behind(patch[rows_dev:], "px", 1)
    patch = patch[:rows_dev].at[:over_x].add(beside_x)
    beside_y = from_behind(patch[:, cols_dev:], "py", 1)
    return patch[:, :cols_dev].at[:, :over_y].add(beside_y)


def extended(field, over_x, over_y):
    px, py = lax.axis_size("px"), lax.axis_size("py")
    right = from_behind(field[:, :over_y], "py", -1)
    below = from_behind(field[:over_x], "px", -1)
    pairs = [
        (a * py + b, ((a - 1) % px) * py + (b - 1) % py) for a in range(px) for b in range(py)
    ]
    corner = lax.ppermute(field[:over_x, :over_y], ("px", "py"), pairs)
    upper = jnp.concatenate([field, right], axis=1)
    lower = jnp.concatenate([below, corner], axis=1)
    return jnp.concatenate([upper, lower], axis=0)


def on_device(eta_boxes, corners, grain_ids, misfit, green):
    px, py = lax.axis_size("px"), lax.axis_size("py")
    box_count, extent, span, depth = eta_boxes.shape
    own, kx_rows, length_y = green.shape
    length_x = kx_rows * py
    rows_dev = length_x // px
    cols_dev = length_y // py
    over_x = extent - STEP
    over_y = span - STEP
    half = own // 2
    slots = cols_dev // over_y
    packs = -(-(half + 1) // slots)
    first_x = corners[:, 0] * STEP
    start_x = first_x - lax.axis_index("px") * rows_dev
    start_y = corners[:, 1] * STEP - lax.axis_index("py") * cols_dev
    variant = jnp.arange(misfit.shape[0], dtype=jnp.int32)
    weights = jnp.sum(
        jnp.where(grain_ids[:, None] == variant[None, :], misfit[None, :], 0.0), axis=1
    )
    place = lax.all_gather(jnp.stack([first_x, start_y], axis=1), "px", tiled=True).reshape(-1)
    scale = 1.0 / (length_x * length_y * depth)
    depth_forward, depth_inverse = depth_tables(depth, px, scale)
    rows_forward, rows_inverse = row_tables(length_x)
    cols_forward, cols_inverse = column_tables(length_y)

    first_gain, conj_gain, own_planes, mirror = multiplier(green, px, py)

    spectra = box_depth(eta_boxes, weights, depth_forward)
    spectra = spectra.reshape(px, 2, half, extent, box_count * span)
    spectra = exchange(spectra, "px")
    shape = (px, box_count, half, extent, span, length_x, cols_dev, over_y, slots, packs)
    along_x = box_rows(spectra, place, rows_forward, shape, py)
    along_x = exchange(along_x, "py")
    if cols_dev % LANES:
        body = along_x[:, :, : half + 1]
        shifted = jnp.roll(along_x[:, :, half + 1 :], 1, axis=0)
        pieces = []
        for k in range(half + 1):
            at = (k % slots) * over_y
            pieces.append(shifted[:, :, k // slots, :, at : at + over_y])
        beyond = jnp.stack(pieces, axis=2)
        body = body.at[..., :over_y].add(beyond)
        body = jnp.transpose(body, (1, 2, 3, 0, 4)).reshape(1, 2, half + 1, kx_rows, length_y)
        back = grid_columns(
            body, own_planes, mirror, first_gain, conj_gain, cols_forward, cols_inverse, slots, over_y, 0
        )
        back = back.reshape(2, half, kx_rows, py, cols_dev)
        back = jnp.transpose(back, (3, 0, 1, 2, 4))
    else:
        back = grid_columns(
            along_x, own_planes, mirror, first_gain, conj_gain, cols_forward, cols_inverse, slots, over_y, packs
        )
    back = exchange(back, "py")
    back = back_rows(back, rows_inverse, px)
    back = exchange(back, "px")
    potential = back_depth(back, depth_inverse)

    occupancy = occupancy_window(
        eta_boxes * eta_boxes, start_x, start_y, rows_dev, cols_dev, over_x, over_y
    )
    occupancy = extended(occupancy, over_x, over_y)
    window = extended(potential, over_x, over_y)
    zero = jnp.zeros((), jnp.int32)
    results = []
    for b in range(box_count):
        position = (start_x[b], start_y[b], zero)
        mu = lax.dynamic_slice(window, position, eta_boxes.shape[1:])
        total = lax.dynamic_slice(occupancy, position, eta_boxes.shape[1:])
        results.append(advance(eta_boxes[b], weights[b], mu, total))
    return (jnp.stack(results), potential)


def solution(mesh):
    in_specs = (
        P(("px", "py"), None, None, None),
        P(("px", "py"), None),
        P(("px", "py")),
        P(),
        P("px", "py", None),
    )
    out_specs = (P(("px", "py"), None, None, None), P("px", "py", None))
    return jax.shard_map(
        on_device, mesh=mesh, in_specs=in_specs, out_specs=out_specs, check_vma=False
    )
```

time: 1990 us -> 818 us (0.41)
  matrix products: 551 us -> 0 us
  blocking collectives: 624 us -> 128 us
  local copies, waits for them, and re-layouts: 258 us -> 61.3 us
  Pallas kernels: 0 us -> 108 us
  starting transfers between devices: 16.5 us -> 106 us
  waiting for transfers between devices: 430 us -> 355 us
  other arithmetic: 83.5 us -> 34.4 us
    dot_general x20 -> x0, matrix products: 551 us -> none  [product(): return jnp.einsum(pattern, operand, table_mat, precision=precise_mode)]
    all_to_all x3 -> x1, blocking collectives: 624 us -> 77.3 us  [exchange(): return lax.all_to_all(shard, axis, split_axis=0, concat_axis=0, tiled=True)]
    all_to_all x1 -> x3, waiting for transfers between devices: 266 us -> 5.75 us  [exchange(): return lax.all_to_all(shard, axis, split_axis=0, concat_axis=0, tiled=True)]
    ppermute x0 -> x5, waiting for transfers between devices: none -> 149 us  [the longest x1 72.1 us: multiplier(): lax.ppermute(mirror_zero, 'py', [(i, py - 1 - i) for i in range(py)])]
    pallas_call x0 -> x7, Pallas kernels: none -> 108 us  [the longest x1 54.6 us: box_rows(): pl.pallas_call(functools.partial(rows_kernel, shape), out_shape=jax.Shape...]
    all_to_all x1 -> x3, starting transfers between devices: 5.53 us -> 80.6 us  [exchange(): return lax.all_to_all(shard, axis, split_axis=0, concat_axis=0, tiled=True)]
    slice x19 -> x12, local copies, waits for them, and re-layouts: 89.1 us -> 15.1 us  [the longest x2 4.33 us: extended(): below = from_behind(field[:over_x], 'px', -1)]
    another operation x4 -> x1, local copies, waits for them, and re-layouts: 59.9 us -> 0.01 us  [the longest x1 18.1 us: on_device(): jnp.stack([back_real, back_imag])]
  transfers between devices with their start and end apart: 7 -> 15, of which waited for: 4 -> 8; matrix products, arithmetic and copies ran while one was open for 2% -> 7% of each run, Pallas kernels for 0% -> 3%
where the time goes in v1:
time: 818 us; the launch traced here: 811 us
  waiting for transfers between devices  355 us (43%)
  blocking collectives  128 us (16%)
  Pallas kernels  108 us (13%)
  starting transfers between devices  106 us (13%)
  local copies, waits for them, and re-layouts  61.3 us (7%)
  other arithmetic  34.4 us (4%)
  between operations  18.8 us (2%)
    ppermute x7, waiting for transfers between devices, from_behind(): lax.ppermute(shard, axis, [(i, (i + by) % peers) for i in range(peers)])  200 us
    all_to_all x3, starting transfers between devices, exchange(): return lax.all_to_all(shard, axis, split_axis=0, concat_axis=0, tiled=True)  80.6 us
    all_to_all x1, blocking collectives, exchange(): return lax.all_to_all(shard, axis, split_axis=0, concat_axis=0, tiled=True)  77.3 us
    ppermute x1, waiting for transfers between devices, multiplier(): lax.ppermute(mirror_zero, 'py', [(i, py - 1 - i) for i in range(py)])  72.1 us
    ppermute x2, waiting for transfers between devices, extended(): corner = lax.ppermute(field[:over_x, :over_y], ('px', 'py'), pairs)  68.9 us
    pallas_call x1, Pallas kernels, box_rows(): pl.pallas_call(functools.partial(rows_kernel, shape), out_shape=jax.Shape...  54.6 us
    all_gather x1, blocking collectives, on_device(): lax.all_gather(jnp.stack([first_x, start_y], axis=1), 'px', tiled=True)  50.9 us
    unnamed x80, local copies, waits for them, and re-layouts  20.2 us
  transfers between devices with their start and end apart: 15, of which 8 were waited for; matrix products, arithmetic and copies ran while one was open for 7% of the time, Pallas kernels for 3%

profile of v1, /device:TPU:5, one launch (start us, length us, event | category | flops | bytes accessed | tf_op | source)
XLA Modules:
  0.0 810.9 jit_solution(10776063765567520490)
XLA Ops:
  1.5 1.6 copy-done.1
  4.6 4.6 box_depth.1
  9.2 5.8 all-to-all-start
  15.0 50.9 %all-gather = s32[8,4,2]{1,2,0:T(2,128)S(1)} all-gather(s32[1,4,2]{1,2,0:T(2,128)S(1)} %add_bitcast_fusion), channel_id=1, replica_groups=mesh['px'=8,'py'=4] {'px'}, dimensions={0}, use_global_device_ids=true | all-gather | bytes 288 | tf_op jit(solution)/shard_map/all_gather | solution.py:600
  66.2 1.4 copy-done.8
  67.6 1.4 copy-done.9
  69.0 54.6 %box_rows.1 = f32[4,2,11,192,128]{4,3,2,1,0:T(8,128)} custom-call(s32[64]{0:T(128)S(1)} %reshape.112.place, f32[8,2,8,32,128]{4,3,2,1,0:T(8,128)S(1)} %all-to-all-done.boxes, bf16[3,512,512]{2,1,0:T(8,128)(2,1)S(1)} %copy-done.8, bf16[3,512,512]{2,1,0:T(8,128)(2,1)S(1)} %copy-done.9), custom_call_target="tpu_custom_call" | custom-call | tf_op jit(solution)/shard_map/box_rows/pallas_call | solution.py:286
  123.6 10.1 %all-to-all-start.1 = ((f32[4,2,11,192,128]{4,3,2,1,0:T(8,128)}), f32[4,2,11,192,128]{4,3,2,1,0:T(8,128)}, u32[]{:S(2)}, u32[]{:S(2)}) async-start(f32[4,2,11,192,128]{4,3,2,1,0:T(8,128)} %box_rows.1), calls=%async_computation.1 | async-start | bytes 17301504 | tf_op jit(solution)/shard_map/all_to_all | solution.py:551
  134.9 94.5 %collective-permute-done.5.edge = f32[16,1,512]{2,1,0:T(1,128)S(1)} collective-permute-done((f32[16,1,512]{2,1,0:T(1,128)S(1)}, f32[16,1,512]{2,1,0:T(1,128)S(1)}, u32[]{:S(2)}, u32[]{:S(2)}) %collective-permute-start.5) | collective-permute-done | bytes 32800 | tf_op jit(solution)/shard_map/ppermute | solution.py:28
  229.4 2.8 copy-done
  234.3 7.1 mirror_planes.2
  241.4 3.3 collective-permute-start.6
  245.5 2.0 mirror_planes.3
  247.5 2.0 collective-permute-start.7
  249.4 72.1 %collective-permute-done.7 = f32[1,192,512]{2,1,0:T(8,128)} collective-permute-done((f32[1,192,512]{2,1,0:T(8,128)}, f32[1,192,512]{2,1,0:T(8,128)}, u32[]{:S(2)}, u32[]{:S(2)}) %collective-permute-start.7) | collective-permute-done | bytes 393248 | tf_op jit(solution)/shard_map/ppermute | solution.py:531
  321.6 1.8 broadcast_select_fusion
  323.4 5.3 collective-permute-start.8
  328.7 8.2 %collective-permute-done.8 = f32[1,192,512]{2,1,0:T(8,128)} collective-permute-done((f32[1,192,512]{2,1,0:T(8,128)}, f32[1,192,512]{2,1,0:T(8,128)}, u32[]{:S(2)}, u32[]{:S(2)}) %collective-permute-start.8) | collective-permute-done | bytes 393248 | tf_op jit(solution)/shard_map/ppermute | solution.py:534
  336.9 2.3 select_bitcast_fusion
  340.2 1.2 copy-done.12
  341.5 1.2 copy-done.13
  342.7 1.2 copy-done.14
  343.9 1.2 copy-done.15
  345.1 17.8 %grid_columns.1 = f32[4,2,8,192,128]{4,3,2,1,0:T(8,128)} custom-call(f32[4,2,11,192,128]{4,3,2,1,0:T(8,128)} %all-to-all-done.1.main.conj.rest_0_.rest_1_, f32[4,2,11,192,128]{4,3,2,1,0:T(8,128)} %all-to-all-done.1.main.conj.rest_0_.rest_1_, f32[4,2,11,192,128]{4,3,2,1,0:T(8,128)} %all-to-all-done.1.main.conj.rest_0_.rest_1_, ...), custom_call_target="tpu_custom_call" | custom-call | tf_op jit(solution)/shard_map/grid_columns/pallas_call | solution.py:395
  363.0 77.3 %all_to_all.20.body = f32[4,2,8,192,128]{4,3,2,1,0:T(8,128)} all-to-all(f32[4,2,8,192,128]{4,3,2,1,0:T(8,128)} %grid_columns.1), channel_id=1, replica_groups=mesh['px'=8,'py'=4] {'py'}, dimensions={0} | all-to-all | bytes 12582912 | tf_op jit(solution)/shard_map/all_to_all | solution.py:551
  440.3 9.8 %back_rows.1 = f32[8,2,8,96,128]{4,3,2,1,0:T(8,128)S(1)} custom-call(f32[4,2,8,192,128]{4,3,2,1,0:T(8,128)} %all_to_all.20.body, bf16[3,512,512]{2,1,0:T(8,128)(2,1)S(1)} %copy-done.10, bf16[3,512,512]{2,1,0:T(8,128)(2,1)S(1)} %copy-done.11), custom_call_target="tpu_custom_call" | custom-call | tf_op jit(solution)/shard_map/back_rows/pallas_call | solution.py:438
  450.1 2.7 copy-done.3
  452.8 64.7 %all-to-all-start.3 = ((f32[8,2,8,96,128]{4,3,2,1,0:T(8,128)}), f32[8,2,8,96,128]{4,3,2,1,0:T(8,128)}, u32[]{:S(2)}, u32[]{:S(2)}) async-start(f32[8,2,8,96,128]{4,3,2,1,0:T(8,128)} %copy-done.3), calls=%async_computation.3 | async-start | bytes 12582912 | tf_op jit(solution)/shard_map/all_to_all | solution.py:551
  517.5 1.8 mul.170
  533.6 4.2 broadcast_in_dim.22
  537.9 3.1 dynamic_update_slice.12
  541.0 1.3 fusion.59
  542.3 3.8 dynamic_update_slice.13
  547.4 1.3 fusion.58
  548.7 3.8 dynamic_update_slice.14
  553.8 1.3 fusion.57
  555.2 3.8 dynamic_update_slice.15
  558.9 1.6 slice.348
  561.8 3.6 slice.346
  565.4 92.8 %collective-permute-done = f32[24,152,128]{2,1,0:T(8,128)S(1)} collective-permute-done((f32[24,152,128]{2,1,0:T(8,128)S(1)}, f32[24,152,128]{2,1,0:T(8,128)S(1)}, u32[]{:S(2)}, u32[]{:S(2)}) %collective-permute-start) | collective-permute-done | bytes 1867808 | tf_op jit(solution)/shard_map/ppermute | solution.py:28
  658.2 1.7 fusion
  660.0 2.7 collective-permute-start.1
  663.5 12.3 %collective-permute-done.1 = f32[96,24,128]{2,1,0:T(8,128)S(1)} collective-permute-done((f32[96,24,128]{2,1,0:T(8,128)S(1)}, f32[96,24,128]{2,1,0:T(8,128)S(1)}, u32[]{:S(2)}, u32[]{:S(2)}) %collective-permute-start.1) | collective-permute-done | bytes 1179680 | tf_op jit(solution)/shard_map/ppermute | solution.py:28
  675.8 1.3 constant_dynamic-update-slice_fusion
  677.1 1.5 slice.352
  678.5 4.5 collective-permute-start.3
  686.3 1.2 slice_bitcast_fusion.7
  687.5 2.4 collective-permute-start.2
  689.9 5.7 all-to-all-done.3
  695.6 11.9 %back_depth.1 = f32[32,3,128,128]{3,2,1,0:T(8,128)} custom-call(f32[12288,128]{1,0:T(8,128)} %bitcast.18.body, bf16[128,128]{1,0:T(8,128)(2,1)S(1)} %copy-done.20, bf16[128,128]{1,0:T(8,128)(2,1)S(1)} %copy-done.21), custom_call_target="tpu_custom_call" | custom-call | tf_op jit(solution)/shard_map/back_depth/pallas_call | solution.py:473
  707.6 2.9 slice.360
  710.4 1.3 fusion.63
  714.1 1.7 fusion.64
  717.4 1.3 fusion.67
  718.7 41.9 %collective-permute-done.4 = f32[24,24,128]{2,1,0:T(8,128)S(1)} collective-permute-done((f32[24,24,128]{2,1,0:T(8,128)S(1)}, f32[24,24,128]{2,1,0:T(8,128)S(1)}, u32[]{:S(2)}, u32[]{:S(2)}) %collective-permute-start.4) | collective-permute-done | bytes 294944 | tf_op jit(solution)/shard_map/ppermute | solution.py:575
  760.6 2.5 collective-permute-start.11
  763.1 4.4 maximum_maximum_fusion
  767.6 27.0 %collective-permute-done.11 = f32[24,24,128]{2,1,0:T(8,128)S(1)} collective-permute-done((f32[24,24,128]{2,1,0:T(8,128)S(1)}, f32[24,24,128]{2,1,0:T(8,128)S(1)}, u32[]{:S(2)}, u32[]{:S(2)}) %collective-permute-start.11) | collective-permute-done | bytes 294944 | tf_op jit(solution)/shard_map/ppermute | solution.py:575
  794.6 7.3 maximum_maximum_fusion.1
  802.0 1.8 fusion.7
  803.9 1.8 fusion.14
  805.7 1.8 fusion.21
  807.5 1.8 fusion.28
  809.3 1.5 pad_maximum_fusion
  (102 shorter events, 16.2 us)
Async XLA Ops:
  0.6 14.3 %copy-start.37 = (s32[4,2]{0,1:T(2,128)S(1)}, s32[4,2]{0,1:T(2,128)}, u32[]{:S(2)}) copy-start(s32[4,2]{0,1:T(2,128)} %param.25) | copy-start | bytes 100
  1.5 1.6 copy-start.1
  3.1 0.8 copy-start.22
  3.9 0.8 copy-start.23
  9.2 56.9 %all-to-all-start = ((f32[8,2,8,32,128]{4,3,2,1,0:T(8,128)}), f32[8,2,8,32,128]{4,3,2,1,0:T(8,128)S(1)}, u32[]{:S(2)}, u32[]{:S(2)}) async-start(f32[8,2,8,32,128]{4,3,2,1,0:T(8,128)} %bitcast.15), calls=%async_computation | async-start | bytes 4194304 | tf_op jit(solution)/shard_map/all_to_all | solution.py:551
  66.1 1.4 copy-start.8
  67.6 1.4 copy-start.9
  123.6 105.8 %copy-start.16 = (bf16[192,192]{1,0:T(8,128)(2,1)S(1)}, bf16[192,192]{1,0:T(8,128)(2,1)}, u32[]{:S(2)}) copy-start(bf16[192,192]{1,0:T(8,128)(2,1)} %constant.129.clone.flip) | copy-start | bytes 221188
  123.6 215.6 %all-to-all-start.1 = ((f32[4,2,11,192,128]{4,3,2,1,0:T(8,128)}), f32[4,2,11,192,128]{4,3,2,1,0:T(8,128)}, u32[]{:S(2)}, u32[]{:S(2)}) async-start(f32[4,2,11,192,128]{4,3,2,1,0:T(8,128)} %box_rows.1), calls=%async_computation.1 | async-start | bytes 17301504 | tf_op jit(solution)/shard_map/all_to_all | solution.py:551
  134.7 94.7 %collective-permute-start.5 = (f32[16,1,512]{2,1,0:T(1,128)S(1)}, f32[16,1,512]{2,1,0:T(1,128)S(1)}, u32[]{:S(2)}, u32[]{:S(2)}) collective-permute-start(f32[16,1,512]{2,1,0:T(1,128)S(1)} %slice.305), channel_id=1, source_target_pairs={{0,3},{1,0},{2,1},{3,2},{4,7},{5,4},{6,5},{7,6},{8,11},{9,8},{10,9... | collective-permute-start | bytes 98312 | tf_op jit(solution)/shard_map/ppermute | solution.py:28
  229.4 2.8 copy-start
  232.2 1.0 copy-start.4
  233.2 1.0 copy-start.5
  234.2 7.1 copy-start.18
  234.2 10.4 %copy-start.17 = (bf16[192,192]{1,0:T(8,128)(2,1)S(1)}, bf16[192,192]{1,0:T(8,128)(2,1)}, u32[]{:S(2)}) copy-start(bf16[192,192]{1,0:T(8,128)(2,1)} %constant.129.clone.flip) | copy-start | bytes 221188
  241.4 95.5 %collective-permute-start.6 = (f32[8,192,512]{2,1,0:T(8,128)}, f32[8,192,512]{2,1,0:T(8,128)}, u32[]{:S(2)}, u32[]{:S(2)}) collective-permute-start(f32[8,192,512]{2,1,0:T(8,128)} %get-tuple-element.31), channel_id=1, source_target_pairs={{0,31},{1,30},{2,29},{3,28},{4,27},{5,26},{6,25},{7,24},{8,23},{9,... | collective-permute-start | bytes 9437192 | tf_op jit(solution)/shard_map/ppermute | solution.py:542
  244.7 0.8 copy-start.19
  247.5 89.5 %copy-start.7 = (f32[1,192,512]{2,1,0:T(8,128)}, f32[1,192,512]{2,1,0:T(8,128)S(1)}, u32[]{:S(2)}) copy-start(f32[1,192,512]{2,1,0:T(8,128)S(1)} %get-tuple-element.32) | copy-start | bytes 1179652
  247.5 74.1 %collective-permute-start.7 = (f32[1,192,512]{2,1,0:T(8,128)}, f32[1,192,512]{2,1,0:T(8,128)}, u32[]{:S(2)}, u32[]{:S(2)}) collective-permute-start(f32[1,192,512]{2,1,0:T(8,128)} %get-tuple-element.33), channel_id=1, source_target_pairs={{0,3},{1,2},{2,1},{3,0},{4,7},{5,6},{6,5},{7,4},{8,11},{9,10},{10,... | collective-permute-start | bytes 1179656 | tf_op jit(solution)/shard_map/ppermute | solution.py:531
  323.4 13.5 %collective-permute-start.8 = (f32[1,192,512]{2,1,0:T(8,128)}, f32[1,192,512]{2,1,0:T(8,128)}, u32[]{:S(2)}, u32[]{:S(2)}) collective-permute-start(f32[1,192,512]{2,1,0:T(8,128)} %broadcast_select_fusion), channel_id=1, source_target_pairs={{0,16},{4,28},{8,24},{12,20},{1,17},{5,29},{9,25},{13,21},{2,18},{... | collective-permute-start | bytes 1179656 | tf_op jit(solution)/shard_map/ppermute | solution.py:534
  339.2 1.0 copy-start.6
  340.2 1.2 copy-start.12
  341.5 1.2 copy-start.13
  342.7 1.2 copy-start.14
  343.9 1.2 copy-start.15
  363.0 77.3 %copy-start.10 = (bf16[3,512,512]{2,1,0:T(8,128)(2,1)S(1)}, bf16[3,512,512]{2,1,0:T(8,128)(2,1)}, u32[]{:S(2)}) copy-start(bf16[3,512,512]{2,1,0:T(8,128)(2,1)} %constant.138.clone.high) | copy-start | bytes 4718596
  363.0 77.3 %copy-start.11 = (bf16[3,512,512]{2,1,0:T(8,128)(2,1)S(1)}, bf16[3,512,512]{2,1,0:T(8,128)(2,1)}, u32[]{:S(2)}) copy-start(bf16[3,512,512]{2,1,0:T(8,128)(2,1)} %constant.139.clone.low) | copy-start | bytes 4718596
  450.1 2.7 copy-start.3
  452.8 64.7 %copy-start.2 = (f32[4,32,32,128]{3,2,1,0:T(8,128)S(1)}, f32[4,32,32,128]{3,2,1,0:T(8,128)}, u32[]{:S(2)}) copy-start(f32[4,32,32,128]{3,2,1,0:T(8,128)} %eta.1) | copy-start | bytes 6291460
  452.8 242.8 %all-to-all-start.3 = ((f32[8,2,8,96,128]{4,3,2,1,0:T(8,128)}), f32[8,2,8,96,128]{4,3,2,1,0:T(8,128)}, u32[]{:S(2)}, u32[]{:S(2)}) async-start(f32[8,2,8,96,128]{4,3,2,1,0:T(8,128)} %copy-done.3), calls=%async_computation.3 | async-start | bytes 12582912 | tf_op jit(solution)/shard_map/all_to_all | solution.py:551
  560.6 97.6 %collective-permute-start = (f32[24,152,128]{2,1,0:T(8,128)S(1)}, f32[24,152,128]{2,1,0:T(8,128)S(1)}, u32[]{:S(2)}, u32[]{:S(2)}) collective-permute-start(f32[24,152,128]{2,1,0:T(8,128)S(1)} %slice.348), channel_id=1, source_target_pairs={{0,4},{4,8},{8,12},{12,16},{16,20},{20,24},{24,28},{28,0},{1,5},{5... | collective-permute-start | bytes 5603336 | tf_op jit(solution)/shard_map/ppermute | solution.py:28
  660.0 15.8 %collective-permute-start.1 = (f32[96,24,128]{2,1,0:T(8,128)S(1)}, f32[96,24,128]{2,1,0:T(8,128)S(1)}, u32[]{:S(2)}, u32[]{:S(2)}) collective-permute-start(f32[96,24,128]{2,1,0:T(8,128)S(1)} %slice.351), channel_id=1, source_target_pairs={{0,1},{1,2},{2,3},{3,0},{4,5},{5,6},{6,7},{7,4},{8,9},{9,10},{10,1... | collective-permute-start | bytes 3538952 | tf_op jit(solution)/shard_map/ppermute | solution.py:28
  663.5 32.1 %copy-start.20 = (bf16[128,128]{1,0:T(8,128)(2,1)S(1)}, bf16[128,128]{1,0:T(8,128)(2,1)}, u32[]{:S(2)}) copy-start(bf16[128,128]{1,0:T(8,128)(2,1)} %constant.140.clone.high) | copy-start | bytes 98308
  663.5 32.1 %copy-start.21 = (bf16[128,128]{1,0:T(8,128)(2,1)S(1)}, bf16[128,128]{1,0:T(8,128)(2,1)}, u32[]{:S(2)}) copy-start(bf16[128,128]{1,0:T(8,128)(2,1)} %constant.141.clone.low) | copy-start | bytes 98308
  677.1 10.5 %copy-start.25 = (f32[96,128,128]{2,1,0:T(8,128)}, f32[96,128,128]{2,1,0:T(8,128)S(1)}, u32[]{:S(2)}) copy-start(f32[96,128,128]{2,1,0:T(8,128)S(1)} %get-tuple-element.34) | copy-start | bytes 18874372
  678.5 84.6 %collective-permute-start.3 = (f32[24,128,128]{2,1,0:T(8,128)}, f32[24,128,128]{2,1,0:T(8,128)}, u32[]{:S(2)}, u32[]{:S(2)}) collective-permute-start(f32[24,128,128]{2,1,0:T(8,128)} %slice.352), channel_id=1, source_target_pairs={{0,28},{4,0},{8,4},{12,8},{16,12},{20,16},{24,20},{28,24},{1,29},{... | collective-permute-start | bytes 4718600 | tf_op jit(solution)/shard_map/ppermute | solution.py:28
  687.5 75.6 %collective-permute-start.2 = (f32[96,24,128]{2,1,0:T(8,128)}, f32[96,24,128]{2,1,0:T(8,128)}, u32[]{:S(2)}, u32[]{:S(2)}) collective-permute-start(f32[96,24,128]{2,1,0:T(8,128)} %get-tuple-element.35), channel_id=1, source_target_pairs={{0,3},{1,0},{2,1},{3,2},{4,7},{5,4},{6,5},{7,6},{8,11},{9,8},{10,9... | collective-permute-start | bytes 3538952 | tf_op jit(solution)/shard_map/ppermute | solution.py:28
  695.6 14.8 %copy-start.26 = (f32[32,32,128]{2,1,0:T(8,128)S(1)}, f32[32,32,128]{2,1,0:T(8,128)}, u32[]{:S(2)}) copy-start(f32[32,32,128]{2,1,0:T(8,128)} %get-tuple-element.37) | copy-start | bytes 1572868
  695.6 14.8 %copy-start.27 = (f32[32,32,128]{2,1,0:T(8,128)S(1)}, f32[32,32,128]{2,1,0:T(8,128)}, u32[]{:S(2)}) copy-start(f32[32,32,128]{2,1,0:T(8,128)} %get-tuple-element.36) | copy-start | bytes 1572868
  707.6 4.2 copy-start.24
  710.4 84.2 %collective-permute-start.10 = (f32[24,128,128]{2,1,0:T(8,128)}, f32[24,128,128]{2,1,0:T(8,128)}, u32[]{:S(2)}, u32[]{:S(2)}) collective-permute-start(f32[24,128,128]{2,1,0:T(8,128)} %bitcast.20), channel_id=1, source_target_pairs={{0,28},{4,0},{8,4},{12,8},{16,12},{20,16},{24,20},{28,24},{1,29},{... | collective-permute-start | bytes 4718600 | tf_op jit(solution)/shard_map/ppermute | solution.py:28
  712.9 50.2 %slice-start = ((s8[6291456]{0:T(1024)(128)(4,1)}), s8[4194304]{0:T(1024)(128)(4,1)S(1)}, s32[]{:S(2)}) async-start(s8[6291456]{0:T(1024)(128)(4,1)} %bitcast.56), calls=%async_computation.4 | async-start | bytes 8388608
  712.9 81.7 %collective-permute-start.9 = (f32[96,24,128]{2,1,0:T(8,128)}, f32[96,24,128]{2,1,0:T(8,128)}, u32[]{:S(2)}, u32[]{:S(2)}) collective-permute-start(f32[96,24,128]{2,1,0:T(8,128)} %slice.359), channel_id=1, source_target_pairs={{0,3},{1,0},{2,1},{3,2},{4,7},{5,4},{6,5},{7,6},{8,11},{9,8},{10,9... | collective-permute-start | bytes 3538952 | tf_op jit(solution)/shard_map/ppermute | solution.py:28
  715.8 47.4 %slice-start.1 = ((s8[6291456]{0:T(1024)(128)(4,1)}), s8[2097152]{0:T(1024)(128)(4,1)S(1)}, s32[]{:S(2)}) async-start(s8[6291456]{0:T(1024)(128)(4,1)} %bitcast.56), calls=%async_computation.5 | async-start | bytes 4194304
  717.3 43.3 %collective-permute-start.4 = (f32[24,24,128]{2,1,0:T(8,128)S(1)}, f32[24,24,128]{2,1,0:T(8,128)S(1)}, u32[]{:S(2)}, u32[]{:S(2)}) collective-permute-start(f32[24,24,128]{2,1,0:T(8,128)S(1)} %slice.353), channel_id=1, source_target_pairs={{0,31},{1,28},{2,29},{3,30},{4,3},{5,0},{6,1},{7,2},{8,7},{9,4},{1... | collective-permute-start | bytes 884744 | tf_op jit(solution)/shard_map/ppermute | solution.py:575
  760.6 2.5 copy-start.36
  760.6 34.0 %collective-permute-start.11 = (f32[24,24,128]{2,1,0:T(8,128)S(1)}, f32[24,24,128]{2,1,0:T(8,128)S(1)}, u32[]{:S(2)}, u32[]{:S(2)}) collective-permute-start(f32[24,24,128]{2,1,0:T(8,128)S(1)} %slice.361), channel_id=1, source_target_pairs={{0,31},{1,28},{2,29},{3,30},{4,3},{5,0},{6,1},{7,2},{8,7},{9,4},{1... | collective-permute-start | bytes 884744 | tf_op jit(solution)/shard_map/ppermute | solution.py:575
  767.6 34.4 %copy-start.28 = (f32[32,32,127]{2,1,0:T(8,128)S(1)}, f32[32,32,127]{2,1,0:T(8,128)}, u32[]{:S(2)}) copy-start(f32[32,32,127]{2,1,0:T(8,128)} %get-tuple-element.42) | copy-start | bytes 1560580
  767.6 34.4 %copy-start.29 = (f32[32,32,127]{2,1,0:T(8,128)S(1)}, f32[32,32,127]{2,1,0:T(8,128)}, u32[]{:S(2)}) copy-start(f32[32,32,127]{2,1,0:T(8,128)} %get-tuple-element.43) | copy-start | bytes 1560580
  767.6 34.4 %copy-start.34 = (f32[32,32,1]{2,1,0:T(8,128)S(1)}, f32[32,32,1]{2,1,0:T(8,128)}, u32[]{:S(2)}) copy-start(f32[32,32,1]{2,1,0:T(8,128)} %get-tuple-element.44) | copy-start | bytes 12292
  767.6 34.4 %copy-start.35 = (f32[32,32,1]{2,1,0:T(8,128)S(1)}, f32[32,32,1]{2,1,0:T(8,128)}, u32[]{:S(2)}) copy-start(f32[32,32,1]{2,1,0:T(8,128)} %get-tuple-element.45) | copy-start | bytes 12292
  767.6 36.2 %copy-start.30 = (f32[32,32,1]{2,1,0:T(8,128)S(1)}, f32[32,32,1]{2,1,0:T(8,128)}, u32[]{:S(2)}) copy-start(f32[32,32,1]{2,1,0:T(8,128)} %get-tuple-element.75) | copy-start | bytes 12292
  767.6 36.2 %copy-start.31 = (f32[32,32,1]{2,1,0:T(8,128)S(1)}, f32[32,32,1]{2,1,0:T(8,128)}, u32[]{:S(2)}) copy-start(f32[32,32,1]{2,1,0:T(8,128)} %get-tuple-element.76) | copy-start | bytes 12292
  802.0 3.7 copy-start.32
  802.0 3.7 copy-start.33

commit v2 on v1

v2 whole, which is shorter than its diff:
```python
import functools
import math

import jax
import jax.numpy as jnp
import ml_dtypes
import numpy as np
from jax import lax
from jax.experimental import pallas as pl
from jax.experimental.pallas import tpu as pltpu
from jax.sharding import PartitionSpec as P

STEP = 8
LANES = 128
RADIX = 3

rate_step = 0.2
gradient_coef = 0.1
coupling = 1.5

F32 = jnp.float32
BF16 = jnp.bfloat16
MIB = 1 << 20


def from_behind(shard, axis, by):
    peers = lax.axis_size(axis)
    return lax.ppermute(shard, axis, [(i, (i + by) % peers) for i in range(peers)])


def laplace(values):
    padded = jnp.pad(values, ((1, 1), (1, 1), (0, 0)))
    beside_all = padded[2:, 1:-1] + padded[:-2, 1:-1] + padded[1:-1, 2:] + padded[1:-1, :-2]
    beside_all = beside_all + jnp.roll(values, 1, axis=2) + jnp.roll(values, -1, axis=2)
    return beside_all - 6.0 * values


def advance(order_param, occupancy):
    square = order_param * order_param
    force = order_param * square - order_param + 2.0 * coupling * order_param * (occupancy - square)
    force = force - gradient_coef * laplace(order_param)
    return order_param - rate_step * force


def pair_of(table):
    high = table.astype(ml_dtypes.bfloat16)
    low = (table - high.astype(np.float64)).astype(ml_dtypes.bfloat16)
    return high, low


def angle_of(index, length):
    return (index % length) * (2.0 * math.pi / length)


def depth_tables(depth, owners, chunks, scale):
    own = depth // owners
    half = own // 2
    z = np.arange(depth)

    def rows_of(p, planes):
        forward, inverse = ([], []), ([], [])
        for t in planes:
            angles = angle_of((own * p + t + (1 if p < owners // 2 else 0)) * z, depth)
            c, s, factor = np.cos(angles), np.sin(angles), scale
            if p == owners // 2 and t == 0:
                s, factor = -np.ones(depth), 0.5 * scale
            forward[0].append(c)
            forward[1].append(-s)
            inverse[0].append(factor * c)
            inverse[1].append(-factor * s)
        return forward[0] + forward[1], inverse[0] + inverse[1]

    out = []
    for p in range(owners):
        out += rows_of(p, range(half))[0]
    back = []
    size = half // chunks
    for k in range(chunks):
        for p in range(owners):
            back += rows_of(p, range(k * size, (k + 1) * size))[1]
    return pair_of(np.array(out)), pair_of(np.array(back))


def row_tables(length):
    part = length // RADIX
    m = np.arange(part)
    forward, inverse = [], []
    for l in range(RADIX):
        angles = angle_of(m[:, None] * (RADIX * m[None, :] + l), length)
        c, s = np.cos(angles), np.sin(angles)
        forward.append(np.block([[c, s], [-s, c]]))
        c, s = c.T, s.T
        inverse.append(np.block([[c, -s], [s, c]]))
    return pair_of(np.array(forward)), pair_of(np.array(inverse))


def column_tables(length):
    part = length // 2
    m = np.arange(part)
    forward, inverse = [], []
    for parity in range(2):
        angles = angle_of(m[:, None] * (2 * m[None, :] + parity), length)
        c, s = np.cos(angles), np.sin(angles)
        forward.append(np.block([[c, -s], [s, c]]))
        c, s = c.T, s.T
        inverse.append(np.block([[c, s], [-s, c]]))
    return pair_of(np.array(forward)), pair_of(np.array(inverse))


def mirror_tables(rows, length):
    part = length // 2
    m = np.arange(part)
    order = np.concatenate([2 * m, 2 * m + 1])
    straight = np.zeros((length, length))
    straight[order, np.arange(length)] = 1.0
    mirrored = np.zeros((length, length))
    mirrored[(length - order) % length, np.arange(length)] = 1.0
    flip = np.zeros((rows, rows))
    i = np.arange(1, rows)
    flip[i, rows - i] = 1.0
    as_bf16 = lambda table: table.astype(ml_dtypes.bfloat16)
    return as_bf16(straight), as_bf16(mirrored), as_bf16(flip)


def halves(values):
    high = values.astype(BF16)
    return high, (values - high.astype(F32)).astype(BF16)


def dot(a, b):
    return jnp.dot(a, b, preferred_element_type=F32)


def table_first(high, low, values):
    top, rest = halves(values)
    width = values.shape[1]
    if width % LANES == 0:
        both = dot(high, jnp.concatenate([top, rest], axis=1))
        both = both[:, :width] + both[:, width:]
    else:
        both = dot(high, top) + dot(high, rest)
    return both + dot(low, top)


def table_last(values, high, low):
    top, rest = halves(values)
    rows = values.shape[0]
    both = dot(jnp.concatenate([top, rest], axis=0), high)
    return both[:rows] + both[rows:] + dot(top, low)


def cost(*arrays):
    size = sum(math.prod(array.shape) * 4 for array in arrays)
    return pl.CostEstimate(flops=0, bytes_accessed=5 * size, transcendentals=0)


def params(mib):
    return pltpu.CompilerParams(vmem_limit_bytes=mib * MIB)


ANYWHERE = pl.BlockSpec(memory_space=pl.ANY)


def waiting(kernel, before, after):
    def body(*refs):
        kernel(*refs[:before], *refs[before + len(after) :])

    return body


def whole(array):
    rank = len(array.shape)
    return pl.BlockSpec(array.shape, lambda *_: (0,) * rank)


def depth_kernel(weights, place, eta, high, low, out):
    boxes, extent, span = eta.shape[0], eta.shape[1], eta.shape[2]
    owners = out.shape[0]
    planes = high.shape[0] // owners
    dims = (((1,), (1,)), ((), ()))
    for i in range(extent):
        rows = []
        for b in range(boxes):
            values = eta[b, i]
            rows.append(weights[b] * (values * values))
        field = jnp.concatenate(rows, axis=0)
        top, rest = halves(field)
        count = field.shape[0]
        both = lax.dot_general(
            high[...], jnp.concatenate([top, rest], axis=0), dims, preferred_element_type=F32
        )
        small = lax.dot_general(low[...], top, dims, preferred_element_type=F32)
        result = both[:, :count] + both[:, count:] + small
        for p in range(owners):
            out[p, pl.ds(i, planes, stride=extent), :] = result[p * planes : (p + 1) * planes]
    lane = lax.broadcasted_iota(jnp.int32, (STEP, boxes * span), 1)
    where_to = jnp.zeros(lane.shape, jnp.int32)
    for k in range(2 * boxes):
        where_to = jnp.where(lane == k, place[k], where_to)
    for p in range(owners):
        out[p, planes * extent :, :] = where_to.astype(F32)


def box_depth(eta_boxes, weights, place, tables, owners, after):
    high, low = tables
    boxes, extent, span, depth = eta_boxes.shape
    shape = (owners, high.shape[0] // owners * extent + STEP, boxes * span)
    return pl.pallas_call(
        waiting(depth_kernel, 5, after),
        out_shape=jax.ShapeDtypeStruct(shape, F32),
        in_specs=[
            pl.BlockSpec(memory_space=pltpu.SMEM),
            pl.BlockSpec(memory_space=pltpu.SMEM),
            whole(eta_boxes),
            whole(high),
            whole(low),
            *([ANYWHERE] * len(after)),
        ],
        out_specs=pl.BlockSpec(shape, lambda: (0, 0, 0)),
        compiler_params=params(24),
        cost_estimate=cost(eta_boxes, eta_boxes),
        name="box_depth",
    )(weights, place, eta_boxes, high, low, *after)


def rows_kernel(shape, place, boxes_re, boxes_im, high, low, out, lines, packed):
    owners, per_owner, half, extent, span, length, cols, over, slots, packs = shape
    step = pl.program_id(0)
    lane = lax.broadcasted_iota(jnp.int32, (extent, LANES), 1)
    side = lines.shape[0]

    @pl.when(step == 0)
    def _():
        packed[...] = jnp.zeros(packed.shape, F32)

    @pl.when((step <= half) & (step != 1))
    def _():
        lines[...] = jnp.zeros(lines.shape, F32)

        def add_owner(s, carry):
            values = (boxes_re[s], boxes_im[s])
            moved = []
            for b in range(per_owner):
                column = place[2 * (s * per_owner + b) + 1]
                inside = (lane >= b * span) & (lane < (b + 1) * span)
                shift = lax.rem(column + (LANES - b * span), LANES)
                for v in values:
                    moved.append(pltpu.roll(jnp.where(inside, v, 0.0), shift, axis=1))
            for b in range(per_owner):
                at = 2 * (s * per_owner + b)
                where_to = pl.ds(pl.multiple_of(place[at], STEP), extent)
                here = lane >= place[at + 1]
                for ri in range(2):
                    value = moved[2 * b + ri]
                    lines[0, ri, where_to, :] += jnp.where(here, value, 0.0)
                    if side > 1:
                        lines[1, ri, where_to, :] += jnp.where(here, 0.0, value)
            return carry

        lax.fori_loop(0, owners, add_owner, 0, unroll=4)
        lines[:, :, :extent, :] += lines[:, :, length:, :]

    sign = jnp.where(step == 1, -1.0, 1.0).astype(F32)

    for k in range(half + 1):
        slot = half if k == 1 else max(k - 1, 0)

        @pl.when(step == k)
        def _(slot=slot):
            lanes_all = lax.broadcasted_iota(jnp.int32, (length, LANES), 1)
            for ri in range(2):
                beyond = lines[side - 1, ri, :length, :]
                if side == 1:
                    beyond = jnp.where(lanes_all >= cols, beyond, 0.0)
                shift = ((slot % slots) * over - (cols % LANES)) % LANES
                if shift:
                    beyond = pltpu.roll(beyond, shift, axis=1)
                packed[slot // slots, ri] += beyond * (sign if ri else 1.0)

    for k in range(packs):

        @pl.when(step == half + 1 + k)
        def _(k=k):
            lines[0, :, :length, :] = packed[k]

    part = length // RADIX
    terms = []
    for l in range(RADIX):
        take = pl.ds(l, part, stride=RADIX)
        values = jnp.concatenate([lines[0, 0, take, :], lines[0, 1, take, :] * sign], axis=0)
        terms.append(table_first(high[l], low[l], values))
    real, imag = [v[:part] for v in terms], [v[part:] for v in terms]
    root = math.sqrt(0.75)
    sum_re, sum_im = real[1] + real[2], imag[1] + imag[2]
    dif_re, dif_im = root * (real[1] - real[2]), root * (imag[1] - imag[2])
    mid_re, mid_im = real[0] - 0.5 * sum_re, imag[0] - 0.5 * sum_im
    result_re = jnp.concatenate([real[0] + sum_re, mid_re + dif_im, mid_re - dif_im], axis=0)
    result_im = jnp.concatenate([imag[0] + sum_im, mid_im - dif_re, mid_im + dif_re], axis=0)
    block = (out.shape[0], out.shape[3], LANES)
    out[:, 0, 0] = result_re.reshape(block)[:, :, :cols]
    out[:, 1, 0] = result_im.reshape(block)[:, :, :cols]


def box_rows(pieces, place, tables, shape, parts, after):
    owners, per_owner, half, extent, span, length, cols, over, slots, packs = shape
    high, low = tables
    planes = half + 1 + packs
    rows = length // parts
    side = -(-(cols + over) // LANES)

    def plane_in(k):
        return jnp.clip(k - 1, 0, half - 1)

    def plane_out(k, place):
        return (0, 0, jnp.where(k == 1, half, jnp.where(k > half, k, jnp.maximum(k - 1, 0))), 0, 0)

    return pl.pallas_call(
        waiting(functools.partial(rows_kernel, shape), 5, after),
        out_shape=jax.ShapeDtypeStruct((parts, 2, planes, rows, cols), F32),
        grid_spec=pltpu.PrefetchScalarGridSpec(
            num_scalar_prefetch=1,
            grid=(planes,),
            in_specs=[
                pl.BlockSpec((owners, extent, LANES), lambda k, place: (0, plane_in(k), 0)),
                pl.BlockSpec((owners, extent, LANES), lambda k, place: (0, half + plane_in(k), 0)),
                whole(high),
                whole(low),
                *([ANYWHERE] * len(after)),
            ],
            out_specs=pl.BlockSpec((parts, 2, 1, rows, cols), plane_out),
            scratch_shapes=[
                pltpu.VMEM((side, 2, length + extent, LANES), F32),
                pltpu.VMEM((packs, 2, length, LANES), F32),
            ],
        ),
        compiler_params=params(56),
        cost_estimate=cost(pieces, jax.ShapeDtypeStruct((parts, 2, planes, rows, cols), F32)),
        name="box_rows",
    )(place, pieces, pieces, high, low, *after)


def columns_kernel(slots, over, has_packs, has_conj, begin, half, *refs):
    refs = list(refs)
    me = refs.pop(0)[0]
    main = refs.pop(0)
    pack = refs.pop(0) if has_packs else None
    conj = refs.pop(0) if has_conj else None
    conj_pack = refs.pop(0) if has_conj and has_packs else None
    own, mirror = refs.pop(0), refs.pop(0)
    first_gain, conj_gain = (refs.pop(0), refs.pop(0)) if has_conj else (None, None)
    fwd_high, fwd_low, inv_high, inv_low = refs[:4]
    out, scratch = refs[-2:]
    step = pl.program_id(0)
    parts, rows, cols = out.shape[0], out.shape[3], out.shape[4]
    half_length = fwd_high.shape[1] // 2

    def gathered(body, overhang, slot):
        pieces = []
        for ri in range(2):
            line = []
            for q in range(parts):
                piece = body[q, ri, 0]
                if has_packs:
                    lane = lax.broadcasted_iota(jnp.int32, piece.shape, 1)
                    shift = lax.rem(cols - over * slot, cols)
                    beyond = pltpu.roll(overhang[(q - 1) % parts, ri, 0], shift, axis=1)
                    piece = piece + jnp.where(lane < over, beyond, 0.0)
                line.append(piece)
            pieces.append(jnp.concatenate(line, axis=1) if parts > 1 else line[0])
        lower = [v[:, :half_length] for v in pieces]
        upper = [v[:, half_length:] for v in pieces]
        even = jnp.concatenate([a + b for a, b in zip(lower, upper)], axis=1)
        odd = jnp.concatenate([a - b for a, b in zip(lower, upper)], axis=1)
        return even, odd

    def forward(body, overhang, slot):
        even, odd = gathered(body, overhang, slot)
        return (
            table_last(even, fwd_high[0], fwd_low[0]),
            table_last(odd, fwd_high[1], fwd_low[1]),
        )

    def scaled(spectrum, gain):
        even, odd = spectrum
        left, right = gain[:, :half_length], gain[:, half_length:]
        left = jnp.concatenate([left, left], axis=1)
        right = jnp.concatenate([right, right], axis=1)
        return even * left, odd * right

    gain = own[0] + mirror[0]
    if has_conj:
        gain = jnp.where(step == 0, first_gain[...], gain)
    even, odd = scaled(forward(main, pack, lax.rem(step + begin, slots)), gain)
    scratch[0] = even
    scratch[1] = odd

    if has_conj:

        @pl.when(step == 0)
        def _():
            even, odd = scaled(forward(conj, conj_pack, half % slots), conj_gain[...])
            scratch[0] += even
            scratch[1] += odd

    even = table_last(scratch[0], inv_high[0], inv_low[0])
    odd = table_last(scratch[1], inv_high[1], inv_low[1])
    lower, upper = even + odd, even - odd
    for ri in range(2):
        take = slice(ri * half_length, (ri + 1) * half_length)
        line = jnp.concatenate([lower[:, take], upper[:, take]], axis=1)
        for q in range(parts):
            out[lax.rem(q - me + parts, parts), ri, 0] = line[:, q * cols : (q + 1) * cols]


def grid_columns(me, arrived, count, half, own, begin, mirror, gains, forward, inverse, slots, over, packs, after):
    parts, _, planes, rows, cols = arrived.shape
    length = own.shape[2]
    has_packs, has_conj = packs > 0, gains is not None
    one = (parts, 2, 1, rows, cols)
    operands = [me, arrived]
    specs = [
        pl.BlockSpec(memory_space=pltpu.SMEM),
        pl.BlockSpec(one, lambda t: (0, 0, begin + t, 0, 0)),
    ]
    if has_packs:
        operands += [arrived]
        specs += [pl.BlockSpec(one, lambda t: (0, 0, half + 1 + (begin + t) // slots, 0, 0))]
    if has_conj:
        operands += [arrived]
        specs += [pl.BlockSpec(one, lambda t: (0, 0, half, 0, 0))]
        if has_packs:
            operands += [arrived]
            specs += [pl.BlockSpec(one, lambda t: (0, 0, half + 1 + half // slots, 0, 0))]
    operands += [own, mirror]
    specs += [
        pl.BlockSpec((1, rows, length), lambda t: (begin + t, 0, 0)),
        pl.BlockSpec((1, rows, length), lambda t: (t, 0, 0)),
    ]
    fixed = [*(gains or ()), *forward, *inverse]
    return pl.pallas_call(
        functools.partial(columns_kernel, slots, over, has_packs, has_conj, begin, half),
        out_shape=jax.ShapeDtypeStruct((parts, 2, count, rows, cols), F32),
        grid=(count,),
        in_specs=specs + [whole(t) for t in fixed] + [ANYWHERE] * len(after),
        out_specs=pl.BlockSpec(one, lambda t: (0, 0, t, 0, 0)),
        scratch_shapes=[pltpu.VMEM((2, rows, length), F32)],
        compiler_params=params(56),
        cost_estimate=cost(jax.ShapeDtypeStruct((parts, 6, count, rows, cols), F32)),
        name="grid_columns",
    )(*operands, *fixed, *after)


def back_rows_kernel(count, *refs):
    me = refs[0][0]
    bodies = refs[1 : 1 + count]
    high, low, out, lines = refs[1 + count :]
    parts, rows, cols = lines.shape[0], lines.shape[2], lines.shape[3]
    length = parts * rows
    part = length // RADIX
    owners, group = out.shape[0], out.shape[3] // RADIX
    if count == 1:
        lines[...] = bodies[0][:, :, 0]
    else:
        for r, body in enumerate(bodies):
            lines[lax.rem(me - r + parts, parts)] = body[:, 0]
    real = lines[:, 0].reshape(length, cols)
    imag = lines[:, 1].reshape(length, cols)
    real = [real[t * part : (t + 1) * part] for t in range(RADIX)]
    imag = [imag[t * part : (t + 1) * part] for t in range(RADIX)]
    root = math.sqrt(0.75)
    sum_re, sum_im = real[1] + real[2], imag[1] + imag[2]
    dif_re, dif_im = root * (real[1] - real[2]), root * (imag[1] - imag[2])
    mid_re, mid_im = real[0] - 0.5 * sum_re, imag[0] - 0.5 * sum_im
    terms = [
        (real[0] + sum_re, imag[0] + sum_im),
        (mid_re - dif_im, mid_im + dif_re),
        (mid_re + dif_im, mid_im - dif_re),
    ]
    for l in range(RADIX):
        result = table_first(high[l], low[l], jnp.concatenate(terms[l], axis=0))
        for ri in range(2):
            values = result[ri * part : (ri + 1) * part].reshape(owners, group, cols)
            out[:, ri, 0, l * group : (l + 1) * group, :] = values


def back_rows(me, bodies, tables, owners, after):
    high, low = tables
    half, rows, cols = bodies[0].shape[-3:]
    if len(bodies) == 1:
        parts = bodies[0].shape[0]
        spec = pl.BlockSpec((parts, 2, 1, rows, cols), lambda t: (0, 0, t, 0, 0))
    else:
        parts = len(bodies)
        spec = pl.BlockSpec((2, 1, rows, cols), lambda t: (0, t, 0, 0))
    length = parts * rows
    out = jax.ShapeDtypeStruct((owners, 2, half, length // owners, cols), F32)
    return pl.pallas_call(
        waiting(functools.partial(back_rows_kernel, len(bodies)), len(bodies) + 3, after),
        out_shape=out,
        grid=(half,),
        in_specs=[pl.BlockSpec(memory_space=pltpu.SMEM)]
        + [spec] * len(bodies)
        + [whole(high), whole(low)]
        + [ANYWHERE] * len(after),
        out_specs=pl.BlockSpec((owners, 2, 1, length // owners, cols), lambda t: (0, 0, t, 0, 0)),
        scratch_shapes=[pltpu.VMEM((parts, 2, rows, cols), F32)],
        compiler_params=params(56),
        cost_estimate=cost(out, out),
        name="back_rows",
    )(me, *bodies, high, low, *after)


def back_depth_kernel(chunks, *refs):
    bodies = refs[:chunks]
    high, low = refs[chunks : chunks + 2]
    out = refs[-1]
    group = out.shape[0]
    planes = bodies[0].shape[0]
    dims = (((0,), (0,)), ((), ()))
    for g in range(group):
        for l in range(RADIX):
            lines = [body[:, l, g, :] for body in bodies]
            values = jnp.concatenate(lines, axis=0) if chunks > 1 else lines[0]
            top, rest = halves(values)
            total = lax.dot_general(top, high[...], dims, preferred_element_type=F32)
            total += lax.dot_general(rest, high[...], dims, preferred_element_type=F32)
            total += lax.dot_general(top, low[...], dims, preferred_element_type=F32)
            out[g, l] = total


def back_depth(arrived, tables, after, only=None):
    high, low = tables
    chunks = len(arrived)
    depth = high.shape[1]
    planes = high.shape[0] // chunks
    rows, cols = arrived[0].shape[-2:]
    group = rows // RADIX
    take = group if only is None else only // RADIX
    bodies = [piece.reshape(planes, RADIX, group, cols) for piece in arrived]
    block = (planes, RADIX, STEP, cols)
    found = pl.pallas_call(
        functools.partial(back_depth_kernel, chunks),
        out_shape=jax.ShapeDtypeStruct((take, RADIX, cols, depth), F32),
        grid=(take // STEP,),
        in_specs=[pl.BlockSpec(block, lambda g: (0, 0, g, 0)) for _ in bodies]
        + [whole(high), whole(low)]
        + [ANYWHERE] * len(after),
        out_specs=pl.BlockSpec((STEP, RADIX, cols, depth), lambda g: (g, 0, 0, 0)),
        compiler_params=params(56),
        cost_estimate=cost(*bodies, *bodies),
        name="back_depth",
    )(*bodies, high, low, *after)
    return found.reshape(take * RADIX, cols, depth)


def mirror_kernel(index, other, edge, mirrored, flip, out):
    rows, length = other.shape[1], other.shape[2]
    top, rest = halves(other[0])
    turned = dot(flip[...], jnp.concatenate([top, rest], axis=1))
    edge_top, edge_rest = halves(edge[0])
    row = lax.broadcasted_iota(jnp.int32, (rows, length), 0)
    top = jnp.where(row == 0, edge_top.astype(F32), turned[:, :length])
    rest = jnp.where(row == 0, edge_rest.astype(F32), turned[:, length:])
    both = dot(jnp.concatenate([top, rest], axis=0).astype(BF16), mirrored[...])
    out[0] = both[:rows] + both[rows:]


def mirror_planes(green, edge, index, mirrored, flip, after):
    rows, length = green.shape[1:]
    block = (1, rows, length)
    count = index.shape[0]
    return pl.pallas_call(
        waiting(mirror_kernel, 5, after),
        out_shape=jax.ShapeDtypeStruct((count, rows, length), F32),
        grid_spec=pltpu.PrefetchScalarGridSpec(
            num_scalar_prefetch=1,
            grid=(count,),
            in_specs=[
                pl.BlockSpec(block, lambda t, index: (index[t], 0, 0)),
                pl.BlockSpec((1, 1, length), lambda t, index: (index[t], 0, 0)),
                whole(mirrored),
                whole(flip),
                *([ANYWHERE] * len(after)),
            ],
            out_specs=pl.BlockSpec(block, lambda t, index: (t, 0, 0)),
        ),
        compiler_params=params(16),
        cost_estimate=cost(jax.ShapeDtypeStruct((count, rows, length), F32)),
        name="mirror_planes",
    )(index, green, edge, mirrored, flip, *after)


def order_kernel(index, own, straight, out):
    rows = own.shape[1]
    top, rest = halves(own[0])
    both = dot(jnp.concatenate([top, rest], axis=0), straight[...])
    out[0] = both[:rows] + both[rows:]


def order_planes(green, index, straight, after):
    rows, length = green.shape[1:]
    block = (1, rows, length)
    count = index.shape[0]
    return pl.pallas_call(
        waiting(order_kernel, 3, after),
        out_shape=jax.ShapeDtypeStruct((count, rows, length), F32),
        grid_spec=pltpu.PrefetchScalarGridSpec(
            num_scalar_prefetch=1,
            grid=(count,),
            in_specs=[
                pl.BlockSpec(block, lambda t, index: (index[t], 0, 0)),
                whole(straight),
                *([ANYWHERE] * len(after)),
            ],
            out_specs=pl.BlockSpec(block, lambda t, index: (t, 0, 0)),
        ),
        compiler_params=params(16),
        cost_estimate=cost(jax.ShapeDtypeStruct((count, rows, length), F32)),
        name="order_planes",
    )(index, green, straight, *after)


def edges_of(body, axis, first, last):
    over = first.shape[axis]
    if axis == 0:
        first[...] = body[:over]
        last[...] = body[body.shape[0] - over :]
    else:
        first[...] = body[:, :over, :]
        last[...] = body[:, body.shape[1] - over :, :]


def patch_kernel(place, eta, out, first, last):
    boxes, extent, span = eta.shape[0], eta.shape[1], eta.shape[2]
    out[...] = jnp.zeros(out.shape, F32)
    for b in range(boxes):
        row = place[2 * b]
        columns = pl.ds(pl.multiple_of(place[2 * b + 1], STEP), span)

        def add_row(i, carry, b=b, row=row, columns=columns):
            values = eta[b, i]
            out[row + i, columns, :] += values * values
            return carry

        lax.fori_loop(0, extent, add_row, 0, unroll=4)
    edges_of(out, 0, first, last)


def occupancy_patch(eta_boxes, place, rows, cols, over, after):
    depth = eta_boxes.shape[3]
    shapes = [(rows, cols, depth), (over, cols, depth), (over, cols, depth)]
    return pl.pallas_call(
        waiting(patch_kernel, 2, after),
        out_shape=[jax.ShapeDtypeStruct(shape, F32) for shape in shapes],
        in_specs=[pl.BlockSpec(memory_space=pltpu.SMEM), whole(eta_boxes)]
        + [ANYWHERE] * len(after),
        out_specs=[pl.BlockSpec(shape, lambda: (0, 0, 0)) for shape in shapes],
        compiler_params=params(32),
        cost_estimate=cost(eta_boxes),
        name="occupancy_patch",
    )(place, eta_boxes, *after)


def join_rows_kernel(body, behind, ahead, out, first, last):
    step, steps = pl.program_id(0), pl.num_programs(0)
    near = behind.shape[0] // out.shape[0]
    out[...] = body[...]
    count = out.shape[0]

    @pl.when(step < near)
    def _():
        out[...] += behind[pl.ds(step * count, count)]

    @pl.when(step >= steps - near)
    def _():
        out[...] += ahead[pl.ds((step - steps + near) * count, count)]

    edges_of(out, 1, first, last)


def join_rows(patch, behind, ahead, over, after):
    rows, cols, depth = patch.shape
    spec = pl.BlockSpec((STEP, cols, depth), lambda r: (r, 0, 0))
    side = pl.BlockSpec((STEP, over, depth), lambda r: (r, 0, 0))
    edge = jax.ShapeDtypeStruct((rows, over, depth), F32)
    return pl.pallas_call(
        waiting(join_rows_kernel, 3, after),
        out_shape=[jax.ShapeDtypeStruct(patch.shape, F32), edge, edge],
        grid=(rows // STEP,),
        in_specs=[spec, whole(behind), whole(ahead)] + [ANYWHERE] * len(after),
        out_specs=[spec, side, side],
        compiler_params=params(24),
        cost_estimate=cost(patch),
        name="join_rows",
    )(patch, behind, ahead, *after)


def apply_kernel(place, weights, base, eta, main, right, below, corner, out):
    boxes, extent, span = eta.shape[0], eta.shape[1], eta.shape[2]
    rows, cols = main.shape[0], main.shape[1]

    def one_box(b, carry):
        first, column = place[2 * b], place[2 * b + 1]
        factor = (-2.0 * rate_step) * weights[b]
        for i in range(0, extent, STEP):
            x = first + i
            for j in range(0, span, STEP):
                y = pl.multiple_of(column + j, STEP)
                for source, take in (
                    (main, (x < rows) & (y < cols)),
                    (right, (x < rows) & (y >= cols)),
                    (below, (x >= rows) & (y < cols)),
                    (corner, (x >= rows) & (y >= cols)),
                ):

                    @pl.when(take)
                    def _(source=source, i=i, j=j, x=x, y=y):
                        low = source is below or source is corner
                        side = source is right or source is corner
                        at_x = x - rows if low else x
                        at_y = pl.multiple_of(y - cols if side else y, STEP)
                        mu = source[pl.ds(at_x, STEP), pl.ds(at_y, STEP), :]
                        here = (b, pl.ds(i, STEP), pl.ds(j, STEP), slice(None))
                        out[here] = base[here] + factor * eta[here] * mu

        return carry

    lax.fori_loop(0, boxes, one_box, 0)


def apply_potential(place, weights, base, eta_boxes, pieces):
    arrays = [base, eta_boxes, *pieces]
    smem = pl.BlockSpec(memory_space=pltpu.SMEM)
    return pl.pallas_call(
        apply_kernel,
        out_shape=jax.ShapeDtypeStruct(eta_boxes.shape, F32),
        in_specs=[smem, smem] + [whole(v) for v in arrays],
        out_specs=whole(eta_boxes),
        compiler_params=params(36),
        cost_estimate=cost(eta_boxes, eta_boxes),
        name="apply_potential",
    )(place, weights, *arrays)


def exchange(shard, axis):
    return lax.all_to_all(shard, axis, split_axis=0, concat_axis=0, tiled=True)


def send_round(lines, axis):
    count = lines.shape[0]
    return [lines[0]] + [from_behind(lines[r], axis, r) for r in range(1, count)]


def potential_pieces(field, rows, over_x, over_y):
    px, py = lax.axis_size("px"), lax.axis_size("py")
    below = from_behind(rows, "px", -1)
    right = from_behind(field[:, :over_y], "py", -1)
    pairs = [
        (a * py + b, ((a - 1) % px) * py + (b - 1) % py) for a in range(px) for b in range(py)
    ]
    corner = lax.ppermute(rows[:, :over_y], ("px", "py"), pairs)
    return field, right, below, corner


def without_packs(along_x, count, slots, over, parts):
    body = count
    shifted = jnp.roll(along_x[:, :, body:], 1, axis=0)
    pieces = []
    for k in range(body):
        at = (k % slots) * over
        pieces.append(shifted[:, :, k // slots, :, at : at + over])
    body = along_x[:, :, :body].at[..., :over].add(jnp.stack(pieces, axis=2))
    body = jnp.transpose(body, (1, 2, 3, 0, 4))
    return body.reshape((1,) + body.shape[:3] + (-1,))


def on_device(eta_boxes, corners, grain_ids, misfit, green):
    px, py = lax.axis_size("px"), lax.axis_size("py")
    p = lax.axis_index("px")
    middle = px // 2
    box_count, extent, span, depth = eta_boxes.shape
    own, kx_rows, length_y = green.shape
    length_x = kx_rows * py
    rows_dev, cols_dev = length_x // px, length_y // py
    over_x, over_y = extent - STEP, span - STEP
    half = own // 2
    chunks = 2 if half % 2 == 0 else 1
    size = half // chunks
    slots = cols_dev // over_y
    first_x = corners[:, 0] * STEP
    start_x = first_x - p * rows_dev
    start_y = corners[:, 1] * STEP - lax.axis_index("py") * cols_dev
    place_here = jnp.stack([start_x, start_y], axis=1).reshape(-1)
    variant = jnp.arange(misfit.shape[0], dtype=jnp.int32)
    weights = jnp.sum(
        jnp.where(grain_ids[:, None] == variant[None, :], misfit[None, :], 0.0), axis=1
    )
    scale = 1.0 / (length_x * length_y * depth)
    depth_forward, depth_inverse = depth_tables(depth, px, chunks, scale)
    rows_forward, rows_inverse = row_tables(length_x)
    cols_forward, cols_inverse = column_tables(length_y)
    straight, mirrored, flip = mirror_tables(kx_rows, length_y)

    edge = from_behind(green[:, :1, :], "py", -1)
    place_send = jnp.stack([first_x, start_y], axis=1).reshape(-1)
    spectra = box_depth(eta_boxes, weights, place_send, depth_forward, px, ())
    arrived = exchange(spectra, "px")
    place = arrived[:, -STEP, : 2 * box_count].astype(jnp.int32).reshape(-1)

    lower = (p < middle).astype(jnp.int32)
    t = jnp.arange(half, dtype=jnp.int32)
    facing = [(i, py - 1 - i) for i in range(py)]
    zero_index = jnp.zeros((1,), jnp.int32)
    index = jnp.minimum(own - 1 - t + lower, own - 1)
    indices = [index[k * size : (k + 1) * size] for k in range(chunks)]
    indices.insert(1, zero_index)
    mirror = [spectra]
    for which in indices:
        mirror.append(mirror_planes(green, edge, which, mirrored, flip, (mirror[-1],)))
    own_index = jnp.concatenate([t + lower, zero_index])
    own_planes = order_planes(green, own_index, straight, (mirror[-1],))
    patch, first, last = occupancy_patch(
        eta_boxes, place_here, rows_dev + over_x, cols_dev + over_y, over_x, (own_planes,)
    )
    first_leg = [lax.ppermute(planes, "py", facing) for planes in mirror[1:]]
    mirror_zero = first_leg.pop(1)
    own_zero = own_planes[half:]
    middle_own = 0.5 * (own_zero + mirror_zero)
    payload = jnp.where(p == 0, middle_own, mirror_zero)
    pairs = [(0, middle)] + [(i, px - i) for i in range(1, middle)]
    from_zero = lax.ppermute(payload, "px", pairs)

    opposite = [(i, px - 1 - i) for i in range(px)]
    mirror = [lax.ppermute(planes, "px", opposite) for planes in first_leg]
    packs = -(-(half + 1) // slots)
    shape = (px, box_count, half, extent, span, length_x, cols_dev, over_y, slots, packs)
    after = (patch, mirror_zero, first_leg[-1], mirror[0])
    lines = box_rows(arrived, place, rows_forward, shape, py, after)
    along_x = exchange(lines, "py")
    first, last = from_behind(last, "px", 1), from_behind(first, "px", -1)
    first_gain = own_planes[:1] + jnp.where(p < middle, mirror[0][:1], from_zero)
    first_gain = jnp.where(p == middle, middle_own + from_zero, first_gain)
    conj_gain = jnp.where(p == middle, middle_own - from_zero, 0.0)
    gains = (first_gain[0], conj_gain[0])

    if cols_dev % LANES:
        along_x, packs = without_packs(along_x, half + 1, slots, over_y, py), 0
    me = lax.axis_index("py").astype(jnp.int32).reshape(1)
    pieces = []
    for k in range(chunks):
        lines = grid_columns(
            me,
            along_x,
            size,
            half,
            own_planes,
            k * size,
            mirror[k],
            gains if k == 0 else None,
            cols_forward,
            cols_inverse,
            slots,
            over_y,
            packs,
            (lines,) if k else (),
        )
        back = lines
        if cols_dev % LANES:
            lines = lines.reshape(2, size, kx_rows, py, cols_dev)
            lines = [exchange(jnp.transpose(lines, (3, 0, 1, 2, 4)), "py")]
        else:
            lines = send_round(lines, "py")
        if k == 0:
            patch, first, last = join_rows(patch, first, last, over_y, (back,))
        lines = back_rows(me, lines, rows_inverse, px, () if k else (patch, mirror[-1]))
        pieces.append(exchange(lines, "px"))
    first, last = from_behind(last, "py", 1), from_behind(first, "py", -1)

    window = patch.at[:, :over_y].add(first).at[:, cols_dev:].add(last)
    zero = jnp.zeros((), jnp.int32)
    results = []
    for b in range(box_count):
        position = (start_x[b], start_y[b], zero)
        total = lax.dynamic_slice(window, position, eta_boxes.shape[1:])
        results.append(advance(eta_boxes[b], total))
    base = jnp.stack(results)

    rows = back_depth(pieces, depth_inverse, (base,), over_x)
    potential = back_depth(pieces, depth_inverse, (rows,))
    pieces = potential_pieces(potential, rows, over_x, over_y)
    return (apply_potential(place_here, weights, base, eta_boxes, pieces), potential)


def solution(mesh):
    in_specs = (
        P(("px", "py"), None, None, None),
        P(("px", "py"), None),
        P(("px", "py")),
        P(),
        P("px", "py", None),
    )
    out_specs = (P(("px", "py"), None, None, None), P("px", "py", None))
    return jax.shard_map(
        on_device, mesh=mesh, in_specs=in_specs, out_specs=out_specs, check_vma=False
    )
```

time: 818 us -> 527 us (0.64)
  blocking collectives: 128 us -> 0 us
  waiting for transfers between devices: 355 us -> 250 us
  other arithmetic: 34.4 us -> 11.8 us
  local copies, waits for them, and re-layouts: 61.3 us -> 43.9 us
  Pallas kernels: 108 us -> 98.2 us
    ppermute x7 -> x13, waiting for transfers between devices: 200 us -> 89.8 us  [from_behind(): lax.ppermute(shard, axis, [(i, (i + by) % peers) for i in range(peers)])]
    all_to_all x1 -> x0, blocking collectives: 77.3 us -> none  [exchange(): return lax.all_to_all(shard, axis, split_axis=0, concat_axis=0, tiled=True)]
    all_gather x1 -> x0, blocking collectives: 50.9 us -> none  [on_device(): lax.all_gather(jnp.stack([first_x, start_y], axis=1), 'px', tiled=True)]
    all_to_all x3 -> x4, waiting for transfers between devices: 5.75 us -> 38.2 us  [exchange(): return lax.all_to_all(shard, axis, split_axis=0, concat_axis=0, tiled=True)]
    ppermute x7 -> x13, starting transfers between devices: 12 us -> 41.7 us  [from_behind(): lax.ppermute(shard, axis, [(i, (i + by) % peers) for i in range(peers)])]
    all_to_all x3 -> x4, starting transfers between devices: 80.6 us -> 51.9 us  [exchange(): return lax.all_to_all(shard, axis, split_axis=0, concat_axis=0, tiled=True)]
    ppermute x5 -> x7, waiting for transfers between devices: 149 us -> 122 us  [the longest x3 49.4 us: on_device(): first_leg = [lax.ppermute(planes, 'py', facing) for planes in mirror[1:]]]
    dynamic_update_slice x4 -> x0, local copies, waits for them, and re-layouts: 14.5 us -> none  [occupancy_window(): patch = lax.dynamic_update_slice(patch, current + squares[b], position)]
  transfers between devices with their start and end apart: 15 -> 24, of which waited for: 8 -> 17; matrix products, arithmetic and copies ran while one was open for 7% -> 5% of each run, Pallas kernels for 3% -> 11%
where the time goes in v2:
time: 527 us; the launch traced here: 525 us
  waiting for transfers between devices  250 us (47%)
  starting transfers between devices  106 us (20%)
  Pallas kernels  98.2 us (19%)
  local copies, waits for them, and re-layouts  43.9 us (8%)
  between operations  15.7 us (3%)
  other arithmetic  11.8 us (2%)
    ppermute x13, waiting for transfers between devices, from_behind(): lax.ppermute(shard, axis, [(i, (i + by) % peers) for i in range(peers)])  89.8 us
    all_to_all x4, starting transfers between devices, exchange(): return lax.all_to_all(shard, axis, split_axis=0, concat_axis=0, tiled=True)  51.9 us
    ppermute x3, waiting for transfers between devices, on_device(): first_leg = [lax.ppermute(planes, 'py', facing) for planes in mirror[1:]]  49.4 us
    ppermute x1, waiting for transfers between devices, on_device(): from_zero = lax.ppermute(payload, 'px', pairs)  42.9 us
    ppermute x13, starting transfers between devices, from_behind(): lax.ppermute(shard, axis, [(i, (i + by) % peers) for i in range(peers)])  41.7 us
    all_to_all x4, waiting for transfers between devices, exchange(): return lax.all_to_all(shard, axis, split_axis=0, concat_axis=0, tiled=True)  38.2 us
    unnamed x62, local copies, waits for them, and re-layouts  30.1 us
    ppermute x1, waiting for transfers between devices, potential_pieces(): corner = lax.ppermute(rows[:, :over_y], ('px', 'py'), pairs)  29.3 us
  transfers between devices with their start and end apart: 24, of which 17 were waited for; matrix products, arithmetic and copies ran while one was open for 5% of the time, Pallas kernels for 11%

profile of v2, /device:TPU:5, one launch (start us, length us, event | category | flops | bytes accessed | tf_op | source)
XLA Modules:
  0.0 525.2 jit_solution(9198599675767953087)
XLA Ops:
  2.5 1.6 copy-done.5
  5.6 4.4 box_depth.1.refs_5_
  10.0 5.9 %all-to-all-start = ((f32[8,520,128]{2,1,0:T(8,128)}), f32[8,520,128]{2,1,0:T(8,128)}, u32[]{:S(2)}, u32[]{:S(2)}) async-start(f32[8,520,128]{2,1,0:T(8,128)} %box_depth.1.refs_5_), calls=%async_computation | async-start | bytes 4259840 | tf_op jit(solution)/shard_map/all_to_all | solution.py:746
  16.9 1.3 collective-permute-start
  18.2 3.0 collective-permute-done.refs_2_
  21.2 2.8 copy-done
  24.0 2.5 mirror_planes.3.refs_5_
  26.7 1.2 mirror_planes.4.refs_5_
  27.9 3.6 mirror_planes.5.refs_3_
  31.5 1.7 collective-permute-start.4
  33.2 30.6 %collective-permute-done.5 = f32[4,192,512]{2,1,0:T(8,128)} collective-permute-done((f32[4,192,512]{2,1,0:T(8,128)S(1)}, f32[4,192,512]{2,1,0:T(8,128)}, u32[]{:S(2)}, u32[]{:S(2)}) %collective-permute-start.5) | collective-permute-done | bytes 1572896 | tf_op jit(solution)/shard_map/ppermute | solution.py:825
  63.8 3.0 collective-permute-start.6
  67.1 2.8 copy-done.1
  70.9 3.9 order_planes.1.refs_2_.refs_5_.refs_3_
  74.8 1.7 occupancy_patch.1
  76.6 3.6 copy-done.3
  80.2 1.3 copy-done.17
  81.5 1.2 copy-done.18
  82.7 1.4 fusion.57
  84.1 1.4 convert_element_type.17.refs_0_
  85.4 18.8 %collective-permute-done.3.refs_6_ = f32[1,192,512]{2,1,0:T(8,128)} collective-permute-done((f32[1,192,512]{2,1,0:T(8,128)}, f32[1,192,512]{2,1,0:T(8,128)}, u32[]{:S(2)}, u32[]{:S(2)}) %collective-permute-start.3) | collective-permute-done | bytes 393248 | tf_op jit(solution)/shard_map/ppermute | solution.py:825
  104.2 22.5 %box_rows.1 = f32[4,2,11,192,128]{4,3,2,1,0:T(8,128)} custom-call(s32[64]{0:T(128)} %convert_element_type.17.refs_0_, f32[8,520,128]{2,1,0:T(8,128)} %all-to-all-done.refs_1_.refs_2_, f32[8,520,128]{2,1,0:T(8,128)} %all-to-all-done.refs_1_.refs_2_, bf16[3,512,512]{2,1,0:T(8,128)(2,1)} %constant.127.clone.refs_3_, ...), custom_call_target="tpu_custom_call" | custom-call | bytes 53903360 | tf_op jit(solution)/shard_map/box_rows/pallas_call | solution.py:317
  126.7 5.7 %all-to-all-start.1 = ((f32[4,2,11,192,128]{4,3,2,1,0:T(8,128)}), f32[4,2,11,192,128]{4,3,2,1,0:T(8,128)}, u32[]{:S(2)}, u32[]{:S(2)}) async-start(f32[4,2,11,192,128]{4,3,2,1,0:T(8,128)} %box_rows.1), calls=%async_computation.1 | async-start | bytes 17301504 | tf_op jit(solution)/shard_map/all_to_all | solution.py:746
  132.4 31.0 %collective-permute-start.1 = (f32[24,152,128]{2,1,0:T(8,128)}, f32[24,152,128]{2,1,0:T(8,128)}, u32[]{:S(2)}, u32[]{:S(2)}) collective-permute-start(f32[24,152,128]{2,1,0:T(8,128)} %copy-done.18), channel_id=1, source_target_pairs={{0,4},{4,8},{8,12},{12,16},{16,20},{20,24},{24,28},{28,0},{1,5},{5... | collective-permute-start | bytes 5603336 | tf_op jit(solution)/shard_map/ppermute | solution.py:28
  163.4 1.9 broadcast_select_fusion
  165.3 2.0 collective-permute-start.7
  167.3 2.4 collective-permute-start.13
  169.7 42.9 %collective-permute-done.7 = f32[1,192,512]{2,1,0:T(8,128)} collective-permute-done((f32[1,192,512]{2,1,0:T(8,128)}, f32[1,192,512]{2,1,0:T(8,128)}, u32[]{:S(2)}, u32[]{:S(2)}) %collective-permute-start.7) | collective-permute-done | bytes 393248 | tf_op jit(solution)/shard_map/ppermute | solution.py:831
  212.6 2.4 select_bitcast_fusion
  214.9 12.2 %all-to-all-done.1.refs_1_.refs_2_.refs_3_.refs_4_ = f32[4,2,11,192,128]{4,3,2,1,0:T(8,128)} async-done(((f32[4,2,11,192,128]{4,3,2,1,0:T(8,128)}), f32[4,2,11,192,128]{4,3,2,1,0:T(8,128)}, u32[]{:S(2)}, u32[]{:S(2)}) %all-to-all-start.1) | async-done | bytes 8650784 | tf_op jit(solution)/shard_map/all_to_all | solution.py:746
  227.1 12.6 %grid_columns.2.refs_3_ = f32[4,2,4,192,128]{4,3,2,1,0:T(8,128)} custom-call(s32[1]{0:T(128)} %bitcast.1.refs_0_, f32[4,2,11,192,128]{4,3,2,1,0:T(8,128)} %all-to-all-done.1.refs_1_.refs_2_.refs_3_.refs_4_, f32[4,2,11,192,128]{4,3,2,1,0:T(8,128)} %all-to-all-done.1.refs_1_.refs_2_.refs_3_.refs_4_, ...), custom_call_target="tpu_custom_call" | custom-call | bytes 47185920 | tf_op jit(solution)/shard_map/grid_columns/pallas_call | solution.py:440
  239.7 3.3 slice_bitcast_fusion.4
  243.4 1.7 collective-permute-start.11
  245.1 3.8 collective-permute-done.1.refs_1_
  249.7 3.7 copy-done.4
  253.4 3.6 join_rows.1
  257.0 3.6 copy-done.10
  260.6 1.2 copy-done.19
  262.9 16.3 %collective-permute-done.11.refs_3_ = f32[2,4,192,128]{3,2,1,0:T(8,128)S(1)} collective-permute-done((f32[2,4,192,128]{3,2,1,0:T(8,128)S(1)}, f32[2,4,192,128]{3,2,1,0:T(8,128)S(1)}, u32[]{:S(2)}, u32[]{:S(2)}) %collective-permute-start.11) | collective-permute-done | bytes 786464 | tf_op jit(solution)/shard_map/ppermute | solution.py:28
  280.6 7.9 %back_rows.2.refs_9_ = f32[8,2,4,96,128]{4,3,2,1,0:T(8,128)} custom-call(s32[1]{0:T(128)} %bitcast.1.refs_0_, f32[2,4,192,128]{3,2,1,0:T(8,128)} %get-tuple-element.51.refs_1_, f32[2,4,192,128]{3,2,1,0:T(8,128)} %copy-done.22, f32[2,4,192,128]{3,2,1,0:T(8,128)} %copy-done.23, f32[2,4,192,128]{3,2,1,0:T(8,128)} %copy-done.24, ...), custom_call_target="tpu_custom_call" | custom-call | bytes 31457280 | tf_op jit(solution)/shard_map/back_rows/pallas_call | solution.py:497
  288.5 35.7 %all-to-all-start.2 = ((f32[8,2,4,96,128]{4,3,2,1,0:T(8,128)}), f32[8,2,4,96,128]{4,3,2,1,0:T(8,128)}, u32[]{:S(2)}, u32[]{:S(2)}) async-start(f32[8,2,4,96,128]{4,3,2,1,0:T(8,128)} %back_rows.2.refs_9_), calls=%async_computation.2 | async-start | bytes 6291456 | tf_op jit(solution)/shard_map/all_to_all | solution.py:746
  324.2 10.4 %grid_columns.3 = f32[4,2,4,192,128]{4,3,2,1,0:T(8,128)} custom-call(s32[1]{0:T(128)} %bitcast.1.refs_0_, f32[4,2,11,192,128]{4,3,2,1,0:T(8,128)} %all-to-all-done.1.refs_1_.refs_2_.refs_3_.refs_4_, f32[4,2,11,192,128]{4,3,2,1,0:T(8,128)} %all-to-all-done.1.refs_1_.refs_2_.refs_3_.refs_4_, f32[9,192,512]{2,1,0:T(8,128)} %copy-done.2, ...), custom_call_target="tpu_custom_call" | custom-call | bytes 47185920 | tf_op jit(solution)/shard_map/grid_columns/pallas_call | solution.py:440
  334.5 3.0 slice_bitcast_fusion
  337.9 1.7 collective-permute-start.15
  339.9 13.1 %collective-permute-done.14.refs_2_ = f32[2,4,192,128]{3,2,1,0:T(8,128)S(1)} collective-permute-done((f32[2,4,192,128]{3,2,1,0:T(8,128)S(1)}, f32[2,4,192,128]{3,2,1,0:T(8,128)S(1)}, u32[]{:S(2)}, u32[]{:S(2)}) %collective-permute-start.14) | collective-permute-done | bytes 786464 | tf_op jit(solution)/shard_map/ppermute | solution.py:28
  353.0 21.0 %collective-permute-done.15.refs_3_ = f32[2,4,192,128]{3,2,1,0:T(8,128)S(1)} collective-permute-done((f32[2,4,192,128]{3,2,1,0:T(8,128)S(1)}, f32[2,4,192,128]{3,2,1,0:T(8,128)S(1)}, u32[]{:S(2)}, u32[]{:S(2)}) %collective-permute-start.15) | collective-permute-done | bytes 786464 | tf_op jit(solution)/shard_map/ppermute | solution.py:28
  375.5 7.8 %back_rows.3 = f32[8,2,4,96,128]{4,3,2,1,0:T(8,128)} custom-call(s32[1]{0:T(128)} %bitcast.1.refs_0_, f32[2,4,192,128]{3,2,1,0:T(8,128)} %get-tuple-element.47.refs_1_, f32[2,4,192,128]{3,2,1,0:T(8,128)} %copy-done.25, f32[2,4,192,128]{3,2,1,0:T(8,128)} %copy-done.26, f32[2,4,192,128]{3,2,1,0:T(8,128)} %copy-done.27, ...), custom_call_target="tpu_custom_call" | custom-call | bytes 31457280 | tf_op jit(solution)/shard_map/back_rows/pallas_call | solution.py:497
  383.3 11.2 %all-to-all-done.2 = f32[8,2,4,96,128]{4,3,2,1,0:T(8,128)} async-done(((f32[8,2,4,96,128]{4,3,2,1,0:T(8,128)}), f32[8,2,4,96,128]{4,3,2,1,0:T(8,128)}, u32[]{:S(2)}, u32[]{:S(2)}) %all-to-all-start.2) | async-done | bytes 3145760 | tf_op jit(solution)/shard_map/all_to_all | solution.py:746
  394.5 4.6 all-to-all-start.3
  414.6 1.6 collective-permute-start.8
  418.9 27.7 %collective-permute-done.8 = f32[120,24,128]{2,1,0:T(8,128)S(1)} collective-permute-done((f32[120,24,128]{2,1,0:T(8,128)}, f32[120,24,128]{2,1,0:T(8,128)S(1)}, u32[]{:S(2)}, u32[]{:S(2)}) %collective-permute-start.8) | collective-permute-done | bytes 1474592 | tf_op jit(solution)/shard_map/ppermute | solution.py:28
  446.9 3.3 collective-permute-done.9
  450.5 1.2 fusion.12
  451.7 1.2 fusion.6
  452.9 1.5 pad_maximum_fusion.refs_4_.base
  454.4 14.8 %all-to-all-done.3 = f32[8,2,4,96,128]{4,3,2,1,0:T(8,128)} async-done(((f32[8,2,4,96,128]{4,3,2,1,0:T(8,128)}), f32[8,2,4,96,128]{4,3,2,1,0:T(8,128)}, u32[]{:S(2)}, u32[]{:S(2)}) %all-to-all-start.3) | async-done | bytes 3145760 | tf_op jit(solution)/shard_map/all_to_all | solution.py:746
  469.2 3.8 back_depth.2
  473.0 8.5 %back_depth.3 = f32[32,3,128,128]{3,2,1,0:T(8,128)} custom-call(f32[64,3,32,128]{3,2,1,0:T(8,128)} %bitcast.23.refs_0_, f32[64,3,32,128]{3,2,1,0:T(8,128)} %bitcast.28.refs_1_, bf16[128,128]{1,0:T(8,128)(2,1)} %constant.135.clone.refs_2_, bf16[128,128]{1,0:T(8,128)(2,1)} %constant.136.clone.refs_3_, f32[24,128,128]{2,1,0:T(8,128)} %bitcast.55), custom_call_target="tpu_custom_call" | custom-call | bytes 62914560 | tf_op jit(solution)/shard_map/back_depth/pallas_call | solution.py:541
  481.5 1.5 slice.343
  483.1 2.1 collective-permute-start.17
  486.1 3.3 collective-permute-start.19
  489.4 29.3 %collective-permute-done.19.corner = f32[24,24,128]{2,1,0:T(8,128)S(1)} collective-permute-done((f32[24,24,128]{2,1,0:T(8,128)S(1)}, f32[24,24,128]{2,1,0:T(8,128)S(1)}, u32[]{:S(2)}, u32[]{:S(2)}) %collective-permute-start.19) | collective-permute-done | bytes 294944 | tf_op jit(solution)/shard_map/ppermute | solution.py:761
  518.7 2.8 copy-done.8
  521.5 3.7 apply_potential.1
  (93 shorter events, 16.7 us)
Async XLA Ops:
  2.4 1.6 copy-start.5
  4.0 0.8 copy-start.15
  4.8 0.8 copy-start.16
  10.0 11.3 %copy-start.12 = (bf16[512,512]{1,0:T(8,128)(2,1)S(1)}, bf16[512,512]{1,0:T(8,128)(2,1)}, u32[]{:S(2)}) copy-start(bf16[512,512]{1,0:T(8,128)(2,1)} %constant.124.clone.refs_3_) | copy-start | bytes 1572868
  10.0 11.3 %copy-start.13 = (bf16[192,192]{1,0:T(8,128)(2,1)S(1)}, bf16[192,192]{1,0:T(8,128)(2,1)}, u32[]{:S(2)}) copy-start(bf16[192,192]{1,0:T(8,128)(2,1)} %constant.125.clone.refs_4_) | copy-start | bytes 221188
  10.0 72.7 %all-to-all-start = ((f32[8,520,128]{2,1,0:T(8,128)}), f32[8,520,128]{2,1,0:T(8,128)}, u32[]{:S(2)}, u32[]{:S(2)}) async-start(f32[8,520,128]{2,1,0:T(8,128)} %box_depth.1.refs_5_), calls=%async_computation | async-start | bytes 4259840 | tf_op jit(solution)/shard_map/all_to_all | solution.py:746
  16.9 4.4 collective-permute-start
  21.2 2.8 copy-start
  26.6 37.2 %collective-permute-start.5 = (f32[4,192,512]{2,1,0:T(8,128)S(1)}, f32[4,192,512]{2,1,0:T(8,128)}, u32[]{:S(2)}, u32[]{:S(2)}) collective-permute-start(f32[4,192,512]{2,1,0:T(8,128)S(1)} %mirror_planes.3.refs_5_), channel_id=1, source_target_pairs={{0,3},{1,2},{2,1},{3,0},{4,7},{5,6},{6,5},{7,4},{8,11},{9,10},{10,... | collective-permute-start | bytes 4718600 | tf_op jit(solution)/shard_map/ppermute | solution.py:825
  31.5 72.7 %collective-permute-start.4 = (f32[4,192,512]{2,1,0:T(8,128)}, f32[4,192,512]{2,1,0:T(8,128)}, u32[]{:S(2)}, u32[]{:S(2)}) collective-permute-start(f32[4,192,512]{2,1,0:T(8,128)} %mirror_planes.5.refs_3_), channel_id=1, source_target_pairs={{0,3},{1,2},{2,1},{3,0},{4,7},{5,6},{6,5},{7,4},{8,11},{9,10},{10,... | collective-permute-start | bytes 4718600 | tf_op jit(solution)/shard_map/ppermute | solution.py:825
  63.8 40.4 %collective-permute-start.6 = (f32[4,192,512]{2,1,0:T(8,128)}, f32[4,192,512]{2,1,0:T(8,128)}, u32[]{:S(2)}, u32[]{:S(2)}) collective-permute-start(f32[4,192,512]{2,1,0:T(8,128)} %collective-permute-done.5), channel_id=1, source_target_pairs={{0,28},{4,24},{8,20},{12,16},{16,12},{20,8},{24,4},{28,0},{1,29},{... | collective-permute-start | bytes 4718600 | tf_op jit(solution)/shard_map/ppermute | solution.py:834
  66.8 37.4 %collective-permute-start.3 = (f32[1,192,512]{2,1,0:T(8,128)}, f32[1,192,512]{2,1,0:T(8,128)}, u32[]{:S(2)}, u32[]{:S(2)}) collective-permute-start(f32[1,192,512]{2,1,0:T(8,128)} %mirror_planes.4.refs_5_), channel_id=1, source_target_pairs={{0,3},{1,2},{2,1},{3,0},{4,7},{5,6},{6,5},{7,4},{8,11},{9,10},{10,... | collective-permute-start | bytes 1179656 | tf_op jit(solution)/shard_map/ppermute | solution.py:825
  67.1 2.8 copy-start.1
  69.9 1.0 copy-start.14
  70.9 3.9 copy-start.6
  74.8 137.7 %copy-start.2 = (f32[9,192,512]{2,1,0:T(8,128)}, f32[9,192,512]{2,1,0:T(8,128)S(1)}, u32[]{:S(2)}) copy-start(f32[9,192,512]{2,1,0:T(8,128)S(1)} %order_planes.1.refs_2_.refs_5_.refs_3_) | copy-start | bytes 10616836
  76.6 3.6 copy-start.3
  80.2 1.3 copy-start.17
  81.5 1.2 copy-start.18
  126.7 100.4 %all-to-all-start.1 = ((f32[4,2,11,192,128]{4,3,2,1,0:T(8,128)}), f32[4,2,11,192,128]{4,3,2,1,0:T(8,128)}, u32[]{:S(2)}, u32[]{:S(2)}) async-start(f32[4,2,11,192,128]{4,3,2,1,0:T(8,128)} %box_rows.1), calls=%async_computation.1 | async-start | bytes 17301504 | tf_op jit(solution)/shard_map/all_to_all | solution.py:746
  132.4 116.5 %collective-permute-start.1 = (f32[24,152,128]{2,1,0:T(8,128)}, f32[24,152,128]{2,1,0:T(8,128)}, u32[]{:S(2)}, u32[]{:S(2)}) collective-permute-start(f32[24,152,128]{2,1,0:T(8,128)} %copy-done.18), channel_id=1, source_target_pairs={{0,4},{4,8},{8,12},{12,16},{16,20},{20,24},{24,28},{28,0},{1,5},{5... | collective-permute-start | bytes 5603336 | tf_op jit(solution)/shard_map/ppermute | solution.py:28
  163.4 86.3 %collective-permute-start.2 = (f32[24,152,128]{2,1,0:T(8,128)}, f32[24,152,128]{2,1,0:T(8,128)}, u32[]{:S(2)}, u32[]{:S(2)}) collective-permute-start(f32[24,152,128]{2,1,0:T(8,128)} %copy-done.17), channel_id=1, source_target_pairs={{0,28},{4,0},{8,4},{12,8},{16,12},{20,16},{24,20},{28,24},{1,29},{... | collective-permute-start | bytes 5603336 | tf_op jit(solution)/shard_map/ppermute | solution.py:28
  165.3 47.3 %collective-permute-start.7 = (f32[1,192,512]{2,1,0:T(8,128)}, f32[1,192,512]{2,1,0:T(8,128)}, u32[]{:S(2)}, u32[]{:S(2)}) collective-permute-start(f32[1,192,512]{2,1,0:T(8,128)} %broadcast_select_fusion), channel_id=1, source_target_pairs={{0,16},{4,28},{8,24},{12,20},{1,17},{5,29},{9,25},{13,21},{2,18},{... | collective-permute-start | bytes 1179656 | tf_op jit(solution)/shard_map/ppermute | solution.py:831
  167.3 95.5 %collective-permute-start.13 = (f32[4,192,512]{2,1,0:T(8,128)}, f32[4,192,512]{2,1,0:T(8,128)}, u32[]{:S(2)}, u32[]{:S(2)}) collective-permute-start(f32[4,192,512]{2,1,0:T(8,128)} %collective-permute-done.4.refs_7_), channel_id=1, source_target_pairs={{0,28},{4,24},{8,20},{12,16},{16,12},{20,8},{24,4},{28,0},{1,29},{... | collective-permute-start | bytes 4718600 | tf_op jit(solution)/shard_map/ppermute | solution.py:834
  239.7 10.0 %copy-start.9 = (f32[4,2,4,192,128]{4,3,2,1,0:T(8,128)S(1)}, f32[4,2,4,192,128]{4,3,2,1,0:T(8,128)}, u32[]{:S(2)}) copy-start(f32[4,2,4,192,128]{4,3,2,1,0:T(8,128)} %grid_columns.2.refs_3_) | copy-start | bytes 9437188
  243.0 19.9 %collective-permute-start.10 = (f32[2,4,192,128]{3,2,1,0:T(8,128)S(1)}, f32[2,4,192,128]{3,2,1,0:T(8,128)S(1)}, u32[]{:S(2)}, u32[]{:S(2)}) collective-permute-start(f32[2,4,192,128]{3,2,1,0:T(8,128)S(1)} %get-tuple-element.50), channel_id=1, source_target_pairs={{0,1},{1,2},{2,3},{3,0},{4,5},{5,6},{6,7},{7,4},{8,9},{9,10},{10,1... | collective-permute-start | bytes 2359304 | tf_op jit(solution)/shard_map/ppermute | solution.py:28
  243.4 35.8 %collective-permute-start.11 = (f32[2,4,192,128]{3,2,1,0:T(8,128)S(1)}, f32[2,4,192,128]{3,2,1,0:T(8,128)S(1)}, u32[]{:S(2)}, u32[]{:S(2)}) collective-permute-start(f32[2,4,192,128]{3,2,1,0:T(8,128)S(1)} %get-tuple-element.49), channel_id=1, source_target_pairs={{0,2},{1,3},{2,0},{3,1},{4,6},{5,7},{6,4},{7,5},{8,10},{9,11},{10,... | collective-permute-start | bytes 2359304 | tf_op jit(solution)/shard_map/ppermute | solution.py:28
  248.9 30.8 %collective-permute-start.12 = (f32[2,4,192,128]{3,2,1,0:T(8,128)S(1)}, f32[2,4,192,128]{3,2,1,0:T(8,128)S(1)}, u32[]{:S(2)}, u32[]{:S(2)}) collective-permute-start(f32[2,4,192,128]{3,2,1,0:T(8,128)S(1)} %get-tuple-element.48), channel_id=1, source_target_pairs={{0,3},{1,0},{2,1},{3,2},{4,7},{5,4},{6,5},{7,6},{8,11},{9,8},{10,9... | collective-permute-start | bytes 2359304 | tf_op jit(solution)/shard_map/ppermute | solution.py:28
  249.7 3.7 copy-start.4
  257.0 3.6 copy-start.10
  260.6 1.2 copy-start.19
  261.8 1.1 copy-start.21
  262.9 16.9 %copy-start.22 = (f32[2,4,192,128]{3,2,1,0:T(8,128)}, f32[2,4,192,128]{3,2,1,0:T(8,128)S(1)}, u32[]{:S(2)}) copy-start(f32[2,4,192,128]{3,2,1,0:T(8,128)S(1)} %collective-permute-done.10.refs_2_) | copy-start | bytes 2359300
  279.2 0.9 copy-start.23
  279.7 0.9 copy-start.24
  288.5 106.0 %all-to-all-start.2 = ((f32[8,2,4,96,128]{4,3,2,1,0:T(8,128)}), f32[8,2,4,96,128]{4,3,2,1,0:T(8,128)}, u32[]{:S(2)}, u32[]{:S(2)}) async-start(f32[8,2,4,96,128]{4,3,2,1,0:T(8,128)} %back_rows.2.refs_9_), calls=%async_computation.2 | async-start | bytes 6291456 | tf_op jit(solution)/shard_map/all_to_all | solution.py:746
  337.5 15.5 %collective-permute-start.14 = (f32[2,4,192,128]{3,2,1,0:T(8,128)S(1)}, f32[2,4,192,128]{3,2,1,0:T(8,128)S(1)}, u32[]{:S(2)}, u32[]{:S(2)}) collective-permute-start(f32[2,4,192,128]{3,2,1,0:T(8,128)S(1)} %get-tuple-element.46), channel_id=1, source_target_pairs={{0,1},{1,2},{2,3},{3,0},{4,5},{5,6},{6,7},{7,4},{8,9},{9,10},{10,1... | collective-permute-start | bytes 2359304 | tf_op jit(solution)/shard_map/ppermute | solution.py:28
  337.9 36.1 %collective-permute-start.15 = (f32[2,4,192,128]{3,2,1,0:T(8,128)S(1)}, f32[2,4,192,128]{3,2,1,0:T(8,128)S(1)}, u32[]{:S(2)}, u32[]{:S(2)}) collective-permute-start(f32[2,4,192,128]{3,2,1,0:T(8,128)S(1)} %get-tuple-element.45), channel_id=1, source_target_pairs={{0,2},{1,3},{2,0},{3,1},{4,6},{5,7},{6,4},{7,5},{8,10},{9,11},{10,... | collective-permute-start | bytes 2359304 | tf_op jit(solution)/shard_map/ppermute | solution.py:28
  339.5 35.0 %collective-permute-start.16 = (f32[2,4,192,128]{3,2,1,0:T(8,128)S(1)}, f32[2,4,192,128]{3,2,1,0:T(8,128)S(1)}, u32[]{:S(2)}, u32[]{:S(2)}) collective-permute-start(f32[2,4,192,128]{3,2,1,0:T(8,128)S(1)} %get-tuple-element.44), channel_id=1, source_target_pairs={{0,3},{1,0},{2,1},{3,2},{4,7},{5,4},{6,5},{7,6},{8,11},{9,8},{10,9... | collective-permute-start | bytes 2359304 | tf_op jit(solution)/shard_map/ppermute | solution.py:28
  353.0 21.6 %copy-start.25 = (f32[2,4,192,128]{3,2,1,0:T(8,128)}, f32[2,4,192,128]{3,2,1,0:T(8,128)S(1)}, u32[]{:S(2)}) copy-start(f32[2,4,192,128]{3,2,1,0:T(8,128)S(1)} %collective-permute-done.14.refs_2_) | copy-start | bytes 2359300
  374.0 0.9 copy-start.26
  374.6 0.9 copy-start.27
  383.3 32.9 %copy-start.7 = (f32[4,32,32,128]{3,2,1,0:T(8,128)S(1)}, f32[4,32,32,128]{3,2,1,0:T(8,128)}, u32[]{:S(2)}) copy-start(f32[4,32,32,128]{3,2,1,0:T(8,128)} %eta.1) | copy-start | bytes 6291460
  394.5 74.7 %all-to-all-start.3 = ((f32[8,2,4,96,128]{4,3,2,1,0:T(8,128)}), f32[8,2,4,96,128]{4,3,2,1,0:T(8,128)}, u32[]{:S(2)}, u32[]{:S(2)}) async-start(f32[8,2,4,96,128]{4,3,2,1,0:T(8,128)} %back_rows.3), calls=%async_computation.3 | async-start | bytes 6291456 | tf_op jit(solution)/shard_map/all_to_all | solution.py:746
  414.6 1.8 copy-start.20
  414.6 32.0 %collective-permute-start.8 = (f32[120,24,128]{2,1,0:T(8,128)}, f32[120,24,128]{2,1,0:T(8,128)S(1)}, u32[]{:S(2)}, u32[]{:S(2)}) collective-permute-start(f32[120,24,128]{2,1,0:T(8,128)} %copy-done.21), channel_id=1, source_target_pairs={{0,1},{1,2},{2,3},{3,0},{4,5},{5,6},{6,7},{7,4},{8,9},{9,10},{10,1... | collective-permute-start | bytes 4423688 | tf_op jit(solution)/shard_map/ppermute | solution.py:28
  416.2 30.4 %slice-start = ((s8[9338880]{0:T(1024)(128)(4,1)}), s8[4194304]{0:T(1024)(128)(4,1)S(1)}, s32[]{:S(2)}) async-start(s8[9338880]{0:T(1024)(128)(4,1)} %bitcast.52), calls=%async_computation.4 | async-start | bytes 8388608
  416.3 33.9 %collective-permute-start.9 = (f32[120,24,128]{2,1,0:T(8,128)S(1)}, f32[120,24,128]{2,1,0:T(8,128)S(1)}, u32[]{:S(2)}, u32[]{:S(2)}) collective-permute-start(f32[120,24,128]{2,1,0:T(8,128)S(1)} %copy-done.20), channel_id=1, source_target_pairs={{0,3},{1,0},{2,1},{3,2},{4,7},{5,4},{6,5},{7,6},{8,11},{9,8},{10,9... | collective-permute-start | bytes 4423688 | tf_op jit(solution)/shard_map/ppermute | solution.py:28
  417.4 29.2 %slice-start.1 = ((s8[9338880]{0:T(1024)(128)(4,1)}), s8[4194304]{0:T(1024)(128)(4,1)S(1)}, s32[]{:S(2)}) async-start(s8[9338880]{0:T(1024)(128)(4,1)} %bitcast.52), calls=%async_computation.5 | async-start | bytes 8388608
  418.2 28.4 %slice-start.2 = ((s8[9338880]{0:T(1024)(128)(4,1)}), s8[950272]{0:T(1024)(128)(4,1)S(1)}, s32[]{:S(2)}) async-start(s8[9338880]{0:T(1024)(128)(4,1)} %bitcast.52), calls=%async_computation.6 | async-start | bytes 1900544
  473.0 45.7 %collective-permute-start.18 = (f32[24,128,128]{2,1,0:T(8,128)}, f32[24,128,128]{2,1,0:T(8,128)S(1)}, u32[]{:S(2)}, u32[]{:S(2)}) collective-permute-start(f32[24,128,128]{2,1,0:T(8,128)} %bitcast.54), channel_id=1, source_target_pairs={{0,28},{4,0},{8,4},{12,8},{16,12},{20,16},{24,20},{28,24},{1,29},{... | collective-permute-start | bytes 4718600 | tf_op jit(solution)/shard_map/ppermute | solution.py:28
  481.5 37.2 %copy-start.11 = (f32[4,32,32,128]{3,2,1,0:T(8,128)S(1)}, f32[4,32,32,128]{3,2,1,0:T(8,128)}, u32[]{:S(2)}) copy-start(f32[4,32,32,128]{3,2,1,0:T(8,128)} %pad_maximum_fusion.refs_4_.base) | copy-start | bytes 6291460
  483.1 35.6 %collective-permute-start.17 = (f32[96,24,128]{2,1,0:T(8,128)S(1)}, f32[96,24,128]{2,1,0:T(8,128)S(1)}, u32[]{:S(2)}, u32[]{:S(2)}) collective-permute-start(f32[96,24,128]{2,1,0:T(8,128)S(1)} %slice.343), channel_id=1, source_target_pairs={{0,3},{1,0},{2,1},{3,2},{4,7},{5,4},{6,5},{7,6},{8,11},{9,8},{10,9... | collective-permute-start | bytes 3538952 | tf_op jit(solution)/shard_map/ppermute | solution.py:28
  486.1 32.6 %collective-permute-start.19 = (f32[24,24,128]{2,1,0:T(8,128)S(1)}, f32[24,24,128]{2,1,0:T(8,128)S(1)}, u32[]{:S(2)}, u32[]{:S(2)}) collective-permute-start(f32[24,24,128]{2,1,0:T(8,128)S(1)} %slice.344), channel_id=1, source_target_pairs={{0,31},{1,28},{2,29},{3,30},{4,3},{5,0},{6,1},{7,2},{8,7},{9,4},{1... | collective-permute-start | bytes 884744 | tf_op jit(solution)/shard_map/ppermute | solution.py:761
  518.7 2.8 copy-start.8

commit v3 on v2

--- a/solution.py
+++ b/solution.py
@@ -52,7 +52,7 @@
     return (index % length) * (2.0 * math.pi / length)
 
 
-def depth_tables(depth, owners, chunks, scale):
+def depth_tables(depth, owners, sizes, scale):
     own = depth // owners
     half = own // 2
     z = np.arange(depth)
@@ -74,10 +74,11 @@
     for p in range(owners):
         out += rows_of(p, range(half))[0]
     back = []
-    size = half // chunks
-    for k in range(chunks):
+    begin = 0
+    for size in sizes:
         for p in range(owners):
-            back += rows_of(p, range(k * size, (k + 1) * size))[1]
+            back += rows_of(p, range(begin, begin + size))[1]
+        begin += size
     return pair_of(np.array(out)), pair_of(np.array(back))
 
 
@@ -339,19 +340,22 @@
     )(place, pieces, pieces, high, low, *after)
 
 
-def columns_kernel(slots, over, has_packs, has_conj, begin, half, *refs):
+def columns_kernel(slots, over, has_packs, has_conj, begin, half, counts, *refs):
     refs = list(refs)
     me = refs.pop(0)[0]
     main = refs.pop(0)
     pack = refs.pop(0) if has_packs else None
     conj = refs.pop(0) if has_conj else None
     conj_pack = refs.pop(0) if has_conj and has_packs else None
-    own, mirror = refs.pop(0), refs.pop(0)
+    own = refs.pop(0)
+    mirrors = [refs.pop(0) for _ in counts]
     first_gain, conj_gain = (refs.pop(0), refs.pop(0)) if has_conj else (None, None)
     fwd_high, fwd_low, inv_high, inv_low = refs[:4]
-    out, scratch = refs[-2:]
+    parts = main.shape[0]
+    outs = refs[-2 - parts : -2]
+    scratch, lines = refs[-2:]
     step = pl.program_id(0)
-    parts, rows, cols = out.shape[0], out.shape[3], out.shape[4]
+    rows, cols = main.shape[3], main.shape[4]
     half_length = fwd_high.shape[1] // 2
 
     def gathered(body, overhang, slot):
@@ -387,7 +391,10 @@
         right = jnp.concatenate([right, right], axis=1)
         return even * left, odd * right
 
-    gain = own[0] + mirror[0]
+    mirror = mirrors[0][0]
+    for k in range(1, len(counts)):
+        mirror = jnp.where(step >= sum(counts[:k]), mirrors[k][0], mirror)
+    gain = own[0] + mirror
     if has_conj:
         gain = jnp.where(step == 0, first_gain[...], gain)
     even, odd = scaled(forward(main, pack, lax.rem(step + begin, slots)), gain)
@@ -409,7 +416,9 @@
         take = slice(ri * half_length, (ri + 1) * half_length)
         line = jnp.concatenate([lower[:, take], upper[:, take]], axis=1)
         for q in range(parts):
-            out[lax.rem(q - me + parts, parts), ri, 0] = line[:, q * cols : (q + 1) * cols]
+            lines[q] = line[:, q * cols : (q + 1) * cols]
+        for r, out in enumerate(outs):
+            out[ri, 0] = lines[lax.rem(me + r, parts)]
 
 
 def grid_columns(me, arrived, count, half, own, begin, mirror, gains, forward, inverse, slots, over, packs, after):
@@ -431,19 +440,28 @@
         if has_packs:
             operands += [arrived]
             specs += [pl.BlockSpec(one, lambda t: (0, 0, half + 1 + half // slots, 0, 0))]
-    operands += [own, mirror]
-    specs += [
-        pl.BlockSpec((1, rows, length), lambda t: (begin + t, 0, 0)),
-        pl.BlockSpec((1, rows, length), lambda t: (t, 0, 0)),
-    ]
+    operands += [own, *mirror]
+    specs += [pl.BlockSpec((1, rows, length), lambda t: (begin + t, 0, 0))]
+    counts = [m.shape[0] for m in mirror]
+    for k, many in enumerate(counts):
+        skip = sum(counts[:k])
+        specs += [
+            pl.BlockSpec(
+                (1, rows, length),
+                lambda t, skip=skip, many=many: (jnp.clip(t - skip, 0, many - 1), 0, 0),
+            )
+        ]
     fixed = [*(gains or ()), *forward, *inverse]
     return pl.pallas_call(
-        functools.partial(columns_kernel, slots, over, has_packs, has_conj, begin, half),
-        out_shape=jax.ShapeDtypeStruct((parts, 2, count, rows, cols), F32),
+        functools.partial(columns_kernel, slots, over, has_packs, has_conj, begin, half, counts),
+        out_shape=[jax.ShapeDtypeStruct((2, count, rows, cols), F32)] * parts,
         grid=(count,),
         in_specs=specs + [whole(t) for t in fixed] + [ANYWHERE] * len(after),
-        out_specs=pl.BlockSpec(one, lambda t: (0, 0, t, 0, 0)),
-        scratch_shapes=[pltpu.VMEM((2, rows, length), F32)],
+        out_specs=[pl.BlockSpec((2, 1, rows, cols), lambda t: (0, t, 0, 0))] * parts,
+        scratch_shapes=[
+            pltpu.VMEM((2, rows, length), F32),
+            pltpu.VMEM((parts, rows, cols), F32),
+        ],
         compiler_params=params(56),
         cost_estimate=cost(jax.ShapeDtypeStruct((parts, 6, count, rows, cols), F32)),
         name="grid_columns",
@@ -515,7 +533,6 @@
     high, low = refs[chunks : chunks + 2]
     out = refs[-1]
     group = out.shape[0]
-    planes = bodies[0].shape[0]
     dims = (((0,), (0,)), ((), ()))
     for g in range(group):
         for l in range(RADIX):
@@ -532,17 +549,16 @@
     high, low = tables
     chunks = len(arrived)
     depth = high.shape[1]
-    planes = high.shape[0] // chunks
     rows, cols = arrived[0].shape[-2:]
     group = rows // RADIX
     take = group if only is None else only // RADIX
-    bodies = [piece.reshape(planes, RADIX, group, cols) for piece in arrived]
-    block = (planes, RADIX, STEP, cols)
+    bodies = [piece.reshape(-1, RADIX, group, cols) for piece in arrived]
+    blocks = [(body.shape[0], RADIX, STEP, cols) for body in bodies]
     found = pl.pallas_call(
         functools.partial(back_depth_kernel, chunks),
         out_shape=jax.ShapeDtypeStruct((take, RADIX, cols, depth), F32),
         grid=(take // STEP,),
-        in_specs=[pl.BlockSpec(block, lambda g: (0, 0, g, 0)) for _ in bodies]
+        in_specs=[pl.BlockSpec(block, lambda g: (0, 0, g, 0)) for block in blocks]
         + [whole(high), whole(low)]
         + [ANYWHERE] * len(after),
         out_specs=pl.BlockSpec((STEP, RADIX, cols, depth), lambda g: (g, 0, 0, 0)),
@@ -695,9 +711,11 @@
     )(patch, behind, ahead, *after)
 
 
-def apply_kernel(place, weights, base, eta, main, right, below, corner, out):
+def apply_kernel(inside, place, weights, base, eta, *refs):
+    sources, out = refs[:-1], refs[-1]
     boxes, extent, span = eta.shape[0], eta.shape[1], eta.shape[2]
-    rows, cols = main.shape[0], main.shape[1]
+    rows, cols = inside
+    out[...] = base[...]
 
     def one_box(b, carry):
         first, column = place[2 * b], place[2 * b + 1]
@@ -706,33 +724,31 @@
             x = first + i
             for j in range(0, span, STEP):
                 y = pl.multiple_of(column + j, STEP)
-                for source, take in (
-                    (main, (x < rows) & (y < cols)),
-                    (right, (x < rows) & (y >= cols)),
-                    (below, (x >= rows) & (y < cols)),
-                    (corner, (x >= rows) & (y >= cols)),
-                ):
+                places = [
+                    ((x < rows) & (y < cols), x, y),
+                    ((x < rows) & (y >= cols), x, y - cols),
+                    ((x >= rows) & (y < cols), x - rows, y),
+                    ((x >= rows) & (y >= cols), x - rows, y - cols),
+                ]
+                places = places[:1] if len(sources) == 1 else places[1:]
+                for source, (take, at_x, at_y) in zip(sources, places):
 
                     @pl.when(take)
-                    def _(source=source, i=i, j=j, x=x, y=y):
-                        low = source is below or source is corner
-                        side = source is right or source is corner
-                        at_x = x - rows if low else x
-                        at_y = pl.multiple_of(y - cols if side else y, STEP)
+                    def _(source=source, i=i, j=j, at_x=at_x, at_y=pl.multiple_of(at_y, STEP)):
                         mu = source[pl.ds(at_x, STEP), pl.ds(at_y, STEP), :]
                         here = (b, pl.ds(i, STEP), pl.ds(j, STEP), slice(None))
-                        out[here] = base[here] + factor * eta[here] * mu
+                        out[here] += factor * eta[here] * mu
 
         return carry
 
     lax.fori_loop(0, boxes, one_box, 0)
 
 
-def apply_potential(place, weights, base, eta_boxes, pieces):
-    arrays = [base, eta_boxes, *pieces]
+def apply_potential(place, weights, base, eta_boxes, sources, inside):
+    arrays = [base, eta_boxes, *sources]
     smem = pl.BlockSpec(memory_space=pltpu.SMEM)
     return pl.pallas_call(
-        apply_kernel,
+        functools.partial(apply_kernel, inside),
         out_shape=jax.ShapeDtypeStruct(eta_boxes.shape, F32),
         in_specs=[smem, smem] + [whole(v) for v in arrays],
         out_specs=whole(eta_boxes),
@@ -742,13 +758,16 @@
     )(place, weights, *arrays)
 
 
+def halved(count):
+    return [count // 2, count - count // 2] if count > 1 else [1]
+
+
 def exchange(shard, axis):
     return lax.all_to_all(shard, axis, split_axis=0, concat_axis=0, tiled=True)
 
 
 def send_round(lines, axis):
-    count = lines.shape[0]
-    return [lines[0]] + [from_behind(lines[r], axis, r) for r in range(1, count)]
+    return [lines[0]] + [from_behind(lines[r], axis, r) for r in range(1, len(lines))]
 
 
 def potential_pieces(field, rows, over_x, over_y):
@@ -759,7 +778,7 @@
         (a * py + b, ((a - 1) % px) * py + (b - 1) % py) for a in range(px) for b in range(py)
     ]
     corner = lax.ppermute(rows[:, :over_y], ("px", "py"), pairs)
-    return field, right, below, corner
+    return right, below, corner
 
 
 def without_packs(along_x, count, slots, over, parts):
@@ -784,8 +803,9 @@
     rows_dev, cols_dev = length_x // px, length_y // py
     over_x, over_y = extent - STEP, span - STEP
     half = own // 2
-    chunks = 2 if half % 2 == 0 else 1
-    size = half // chunks
+    sizes = halved(half)
+    begins = [sum(sizes[:k]) for k in range(len(sizes))]
+    pieces = [halved(sizes[0]), *([size] for size in sizes[1:])]
     slots = cols_dev // over_y
     first_x = corners[:, 0] * STEP
     start_x = first_x - p * rows_dev
@@ -796,7 +816,7 @@
         jnp.where(grain_ids[:, None] == variant[None, :], misfit[None, :], 0.0), axis=1
     )
     scale = 1.0 / (length_x * length_y * depth)
-    depth_forward, depth_inverse = depth_tables(depth, px, chunks, scale)
+    depth_forward, depth_inverse = depth_tables(depth, px, sizes, scale)
     rows_forward, rows_inverse = row_tables(length_x)
     cols_forward, cols_inverse = column_tables(length_y)
     straight, mirrored, flip = mirror_tables(kx_rows, length_y)
@@ -812,19 +832,18 @@
     facing = [(i, py - 1 - i) for i in range(py)]
     zero_index = jnp.zeros((1,), jnp.int32)
     index = jnp.minimum(own - 1 - t + lower, own - 1)
-    indices = [index[k * size : (k + 1) * size] for k in range(chunks)]
-    indices.insert(1, zero_index)
-    mirror = [spectra]
+    indices = jnp.split(index, np.cumsum(sum(pieces, []))[:-1].tolist())
+    indices[0] = jnp.concatenate([zero_index, indices[0]])
+    own_zero = order_planes(green, zero_index, straight, (spectra,))
+    mirror = [own_zero]
     for which in indices:
         mirror.append(mirror_planes(green, edge, which, mirrored, flip, (mirror[-1],)))
-    own_index = jnp.concatenate([t + lower, zero_index])
-    own_planes = order_planes(green, own_index, straight, (mirror[-1],))
+    own_planes = order_planes(green, t + lower, straight, (mirror[-1],))
     patch, first, last = occupancy_patch(
         eta_boxes, place_here, rows_dev + over_x, cols_dev + over_y, over_x, (own_planes,)
     )
     first_leg = [lax.ppermute(planes, "py", facing) for planes in mirror[1:]]
-    mirror_zero = first_leg.pop(1)
-    own_zero = own_planes[half:]
+    mirror_zero, first_leg[0] = first_leg[0][:1], first_leg[0][1:]
     middle_own = 0.5 * (own_zero + mirror_zero)
     payload = jnp.where(p == 0, middle_own, mirror_zero)
     pairs = [(0, middle)] + [(i, px - i) for i in range(1, middle)]
@@ -834,11 +853,12 @@
     mirror = [lax.ppermute(planes, "px", opposite) for planes in first_leg]
     packs = -(-(half + 1) // slots)
     shape = (px, box_count, half, extent, span, length_x, cols_dev, over_y, slots, packs)
-    after = (patch, mirror_zero, first_leg[-1], mirror[0])
+    after = (patch, from_zero, *first_leg, mirror[0])
     lines = box_rows(arrived, place, rows_forward, shape, py, after)
     along_x = exchange(lines, "py")
     first, last = from_behind(last, "px", 1), from_behind(first, "px", -1)
-    first_gain = own_planes[:1] + jnp.where(p < middle, mirror[0][:1], from_zero)
+    mirror = [mirror[: len(pieces[0])], *([m] for m in mirror[len(pieces[0]) :])]
+    first_gain = own_planes[:1] + jnp.where(p < middle, mirror[0][0][:1], from_zero)
     first_gain = jnp.where(p == middle, middle_own + from_zero, first_gain)
     conj_gain = jnp.where(p == middle, middle_own - from_zero, 0.0)
     gains = (first_gain[0], conj_gain[0])
@@ -846,15 +866,15 @@
     if cols_dev % LANES:
         along_x, packs = without_packs(along_x, half + 1, slots, over_y, py), 0
     me = lax.axis_index("py").astype(jnp.int32).reshape(1)
-    pieces = []
-    for k in range(chunks):
+    arrays = []
+    for k, size in enumerate(sizes):
         lines = grid_columns(
             me,
             along_x,
             size,
             half,
             own_planes,
-            k * size,
+            begins[k],
             mirror[k],
             gains if k == 0 else None,
             cols_forward,
@@ -864,16 +884,16 @@
             packs,
             (lines,) if k else (),
         )
-        back = lines
+        back = lines[0]
         if cols_dev % LANES:
-            lines = lines.reshape(2, size, kx_rows, py, cols_dev)
+            lines = lines[0].reshape(2, size, kx_rows, py, cols_dev)
             lines = [exchange(jnp.transpose(lines, (3, 0, 1, 2, 4)), "py")]
         else:
             lines = send_round(lines, "py")
         if k == 0:
             patch, first, last = join_rows(patch, first, last, over_y, (back,))
-        lines = back_rows(me, lines, rows_inverse, px, () if k else (patch, mirror[-1]))
-        pieces.append(exchange(lines, "px"))
+        lines = back_rows(me, lines, rows_inverse, px, () if k else (patch, *sum(mirror, [])))
+        arrays.append(exchange(lines, "px"))
     first, last = from_behind(last, "py", 1), from_behind(first, "py", -1)
 
     window = patch.at[:, :over_y].add(first).at[:, cols_dev:].add(last)
@@ -885,10 +905,12 @@
         results.append(advance(eta_boxes[b], total))
     base = jnp.stack(results)
 
-    rows = back_depth(pieces, depth_inverse, (base,), over_x)
-    potential = back_depth(pieces, depth_inverse, (rows,))
+    rows = back_depth(arrays, depth_inverse, (base,), over_x)
+    potential = back_depth(arrays, depth_inverse, (rows,))
     pieces = potential_pieces(potential, rows, over_x, over_y)
-    return (apply_potential(place_here, weights, base, eta_boxes, pieces), potential)
+    inside = (rows_dev, cols_dev)
+    base = apply_potential(place_here, weights, base, eta_boxes, [potential], inside)
+    return (apply_potential(place_here, weights, base, eta_boxes, pieces, inside), potential)
 
 
 def solution(mesh):

time: 527 us -> 516 us (0.979)
  starting transfers between devices: 106 us -> 85.1 us
  waiting for transfers between devices: 250 us -> 261 us
    ppermute x2 -> x3, waiting for transfers between devices: 0.01 us -> 55.5 us  [on_device(): mirror = [lax.ppermute(planes, 'px', opposite) for planes in first_leg]]
    ppermute x1, waiting for transfers between devices: 42.9 us -> 0.01 us  [on_device(): from_zero = lax.ppermute(payload, 'px', pairs)]
    ppermute x13, starting transfers between devices: 41.7 us -> 23.9 us  [from_behind(): lax.ppermute(shard, axis, [(i, (i + by) % peers) for i in range(peers)])]
    all_to_all x4, waiting for transfers between devices: 38.2 us -> 52.7 us  [exchange(): return lax.all_to_all(shard, axis, split_axis=0, concat_axis=0, tiled=True)]
    ppermute x3, waiting for transfers between devices: 49.4 us -> 39.1 us  [on_device(): first_leg = [lax.ppermute(planes, 'py', facing) for planes in mirror[1:]]]
    all_to_all x4, starting transfers between devices: 51.9 us -> 43.8 us  [exchange(): return lax.all_to_all(shard, axis, split_axis=0, concat_axis=0, tiled=True)]
    squeeze x2 -> x0, local copies, waits for them, and re-layouts: 6.27 us -> none  [send_round(): lines[r]]
    unnamed x62 -> x66, local copies, waits for them, and re-layouts: 30.1 us -> 32.3 us
  transfers between devices with their start and end apart: 24 -> 25, of which waited for: 17 -> 15; matrix products, arithmetic and copies ran while one was open for 5% -> 3% of each run, Pallas kernels for 11% -> 11%
where the time goes in v3:
time: 516 us; the launch traced here: 514 us
  waiting for transfers between devices  261 us (51%)
  Pallas kernels  101 us (20%)
  starting transfers between devices  85.1 us (16%)
  local copies, waits for them, and re-layouts  40.9 us (8%)
  between operations  16 us (3%)
  other arithmetic  10.7 us (2%)
    ppermute x13, waiting for transfers between devices, from_behind(): lax.ppermute(shard, axis, [(i, (i + by) % peers) for i in range(peers)])  88.8 us
    ppermute x3, waiting for transfers between devices, on_device(): mirror = [lax.ppermute(planes, 'px', opposite) for planes in first_leg]  55.5 us
    all_to_all x4, waiting for transfers between devices, exchange(): return lax.all_to_all(shard, axis, split_axis=0, concat_axis=0, tiled=True)  52.7 us
    all_to_all x4, starting transfers between devices, exchange(): return lax.all_to_all(shard, axis, split_axis=0, concat_axis=0, tiled=True)  43.8 us
    ppermute x3, waiting for transfers between devices, on_device(): first_leg = [lax.ppermute(planes, 'py', facing) for planes in mirror[1:]]  39.1 us
    unnamed x66, local copies, waits for them, and re-layouts  32.3 us
    ppermute x1, waiting for transfers between devices, potential_pieces(): corner = lax.ppermute(rows[:, :over_y], ('px', 'py'), pairs)  24.8 us
    pallas_call x2, Pallas kernels, grid_columns(): pl.pallas_call(functools.partial(columns_kernel, slots, over, has_packs,...  24 us
  transfers between devices with their start and end apart: 25, of which 15 were waited for; matrix products, arithmetic and copies ran while one was open for 3% of the time, Pallas kernels for 11%

profile of v3, /device:TPU:5, one launch (start us, length us, event | category | flops | bytes accessed | tf_op | source)
XLA Modules:
  0.0 514.3 jit_solution(8214608840838830308)
XLA Ops:
  2.5 1.6 copy-done.3
  5.6 4.4 box_depth.1.refs_3_
  10.0 5.9 %all-to-all-start = ((f32[8,520,128]{2,1,0:T(8,128)}), f32[8,520,128]{2,1,0:T(8,128)}, u32[]{:S(2)}, u32[]{:S(2)}) async-start(f32[8,520,128]{2,1,0:T(8,128)} %box_depth.1.refs_3_), calls=%async_computation | async-start | bytes 4259840 | tf_op jit(solution)/shard_map/all_to_all | solution.py:766
  16.9 1.3 collective-permute-start
  18.3 2.8 copy-done
  22.1 2.1 mirror_planes.3.refs_5_
  24.2 1.2 collective-permute-start.3
  25.5 2.3 mirror_planes.4.refs_5_
  27.8 3.6 mirror_planes.5.refs_3_
  32.0 1.1 collective-permute-start.5
  33.1 19.8 %collective-permute-done.3 = f32[3,192,512]{2,1,0:T(8,128)S(1)} collective-permute-done((f32[3,192,512]{2,1,0:T(8,128)S(1)}, f32[3,192,512]{2,1,0:T(8,128)S(1)}, u32[]{:S(2)}, u32[]{:S(2)}) %collective-permute-start.3) | collective-permute-done | bytes 1179680 | tf_op jit(solution)/shard_map/ppermute | solution.py:845
  54.0 3.0 collective-permute-start.7
  57.8 2.7 collective-permute-start.4
  60.7 2.8 copy-done.1
  64.5 3.5 order_planes.3.refs_2_.refs_5_.refs_3_
  68.0 1.7 occupancy_patch.1
  69.8 3.6 copy-done.6
  73.4 1.3 copy-done.18
  74.7 1.2 copy-done.19
  75.9 5.1 all-to-all-done.refs_1_.refs_2_
  81.0 1.4 fusion.56
  82.4 1.3 convert_element_type.17.refs_0_
  83.6 19.3 %collective-permute-done.5.refs_8_ = f32[2,192,512]{2,1,0:T(8,128)} collective-permute-done((f32[2,192,512]{2,1,0:T(8,128)}, f32[2,192,512]{2,1,0:T(8,128)}, u32[]{:S(2)}, u32[]{:S(2)}) %collective-permute-start.5) | collective-permute-done | bytes 786464 | tf_op jit(solution)/shard_map/ppermute | solution.py:845
  102.9 22.5 %box_rows.1 = f32[4,2,11,192,128]{4,3,2,1,0:T(8,128)} custom-call(s32[64]{0:T(128)} %convert_element_type.17.refs_0_, f32[8,520,128]{2,1,0:T(8,128)} %all-to-all-done.refs_1_.refs_2_, f32[8,520,128]{2,1,0:T(8,128)} %all-to-all-done.refs_1_.refs_2_, bf16[3,512,512]{2,1,0:T(8,128)(2,1)} %constant.127.clone.refs_3_, ...), custom_call_target="tpu_custom_call" | custom-call | bytes 53903360 | tf_op jit(solution)/shard_map/box_rows/pallas_call | solution.py:318
  125.4 6.0 %all-to-all-start.1 = ((f32[4,2,11,192,128]{4,3,2,1,0:T(8,128)}), f32[4,2,11,192,128]{4,3,2,1,0:T(8,128)}, u32[]{:S(2)}, u32[]{:S(2)}) async-start(f32[4,2,11,192,128]{4,3,2,1,0:T(8,128)} %box_rows.1), calls=%async_computation.1 | async-start | bytes 17301504 | tf_op jit(solution)/shard_map/all_to_all | solution.py:766
  131.4 12.1 %collective-permute-start.1 = (f32[24,152,128]{2,1,0:T(8,128)}, f32[24,152,128]{2,1,0:T(8,128)}, u32[]{:S(2)}, u32[]{:S(2)}) collective-permute-start(f32[24,152,128]{2,1,0:T(8,128)} %copy-done.19), channel_id=1, source_target_pairs={{0,4},{4,8},{8,12},{12,16},{16,20},{20,24},{24,28},{28,0},{1,5},{5... | collective-permute-start | bytes 5603336 | tf_op jit(solution)/shard_map/ppermute | solution.py:28
  143.5 5.2 %collective-permute-start.8 = (f32[2,192,512]{2,1,0:T(8,128)}, f32[2,192,512]{2,1,0:T(8,128)}, u32[]{:S(2)}, u32[]{:S(2)}) collective-permute-start(f32[2,192,512]{2,1,0:T(8,128)} %collective-permute-done.5.refs_8_), channel_id=1, source_target_pairs={{0,28},{4,24},{8,20},{12,16},{16,12},{20,8},{24,4},{28,0},{1,29},{... | collective-permute-start | bytes 2359304 | tf_op jit(solution)/shard_map/ppermute | solution.py:853
  148.7 2.3 select_bitcast_fusion
  151.0 55.5 %collective-permute-done.8.refs_7_.refs_9_ = f32[2,192,512]{2,1,0:T(8,128)} collective-permute-done((f32[2,192,512]{2,1,0:T(8,128)}, f32[2,192,512]{2,1,0:T(8,128)}, u32[]{:S(2)}, u32[]{:S(2)}) %collective-permute-start.8) | collective-permute-done | bytes 786464 | tf_op jit(solution)/shard_map/ppermute | solution.py:853
  206.5 20.1 %all-to-all-done.1.refs_1_.refs_2_.refs_3_.refs_4_ = f32[4,2,11,192,128]{4,3,2,1,0:T(8,128)} async-done(((f32[4,2,11,192,128]{4,3,2,1,0:T(8,128)}), f32[4,2,11,192,128]{4,3,2,1,0:T(8,128)}, u32[]{:S(2)}, u32[]{:S(2)}) %all-to-all-start.1) | async-done | bytes 8650784 | tf_op jit(solution)/shard_map/all_to_all | solution.py:766
  226.6 13.2 %grid_columns.2 = (f32[2,4,192,128]{3,2,1,0:T(8,128)}, f32[2,4,192,128]{3,2,1,0:T(8,128)}, f32[2,4,192,128]{3,2,1,0:T(8,128)}, f32[2,4,192,128]{3,2,1,0:T(8,128)}) custom-call(s32[1]{0:T(128)} %bitcast.1.refs_0_, f32[4,2,11,192,128]{4,3,2,1,0:T(8,128)} %all-to-all-done.1.refs_1_.refs_2_.refs_3_.refs_4_, ...), custom_call_target="tpu_custom_call" | custom-call | bytes 47185920 | tf_op jit(solution)/shard_map/grid_columns/pallas_call | solution.py:455
  240.7 1.4 collective-permute-start.12
  242.1 22.5 %collective-permute-done.1.refs_1_ = f32[24,152,128]{2,1,0:T(8,128)} collective-permute-done((f32[24,152,128]{2,1,0:T(8,128)}, f32[24,152,128]{2,1,0:T(8,128)}, u32[]{:S(2)}, u32[]{:S(2)}) %collective-permute-start.1) | collective-permute-done | bytes 1867808 | tf_op jit(solution)/shard_map/ppermute | solution.py:28
  265.8 3.6 copy-done.7
  269.4 1.1 copy-done.12
  270.6 3.6 join_rows.1
  274.2 3.6 copy-done.9
  277.8 1.2 copy-done.20
  279.0 1.1 copy-done.22
  281.5 7.9 %back_rows.2.refs_9_ = f32[8,2,4,96,128]{4,3,2,1,0:T(8,128)} custom-call(s32[1]{0:T(128)} %bitcast.1.refs_0_, f32[2,4,192,128]{3,2,1,0:T(8,128)} %get-tuple-element.43.refs_3_.refs_1_, f32[2,4,192,128]{3,2,1,0:T(8,128)} %copy-done.24, f32[2,4,192,128]{3,2,1,0:T(8,128)} %copy-done.25, f32[2,4,192,128]{3,2,1,0:T(8,128)} %copy-done.26, ...), custom_call_target="tpu_custom_call" | custom-call | bytes 31457280 | tf_op jit(solution)/shard_map/back_rows/pallas_call | solution.py:515
  289.4 27.3 %all-to-all-start.2 = ((f32[8,2,4,96,128]{4,3,2,1,0:T(8,128)}), f32[8,2,4,96,128]{4,3,2,1,0:T(8,128)}, u32[]{:S(2)}, u32[]{:S(2)}) async-start(f32[8,2,4,96,128]{4,3,2,1,0:T(8,128)} %back_rows.2.refs_9_), calls=%async_computation.2 | async-start | bytes 6291456 | tf_op jit(solution)/shard_map/all_to_all | solution.py:766
  316.7 10.8 %grid_columns.3 = (f32[2,4,192,128]{3,2,1,0:T(8,128)}, f32[2,4,192,128]{3,2,1,0:T(8,128)}, f32[2,4,192,128]{3,2,1,0:T(8,128)}, f32[2,4,192,128]{3,2,1,0:T(8,128)}) custom-call(s32[1]{0:T(128)} %bitcast.1.refs_0_, f32[4,2,11,192,128]{4,3,2,1,0:T(8,128)} %all-to-all-done.1.refs_1_.refs_2_.refs_3_.refs_4_, ...), custom_call_target="tpu_custom_call" | custom-call | bytes 47185920 | tf_op jit(solution)/shard_map/grid_columns/pallas_call | solution.py:455
  328.0 1.7 collective-permute-start.16
  330.0 13.5 %collective-permute-done.15.refs_2_ = f32[2,4,192,128]{3,2,1,0:T(8,128)S(1)} collective-permute-done((f32[2,4,192,128]{3,2,1,0:T(8,128)}, f32[2,4,192,128]{3,2,1,0:T(8,128)S(1)}, u32[]{:S(2)}, u32[]{:S(2)}) %collective-permute-start.15) | collective-permute-done | bytes 786464 | tf_op jit(solution)/shard_map/ppermute | solution.py:28
  343.5 20.9 %collective-permute-done.16.refs_3_ = f32[2,4,192,128]{3,2,1,0:T(8,128)S(1)} collective-permute-done((f32[2,4,192,128]{3,2,1,0:T(8,128)}, f32[2,4,192,128]{3,2,1,0:T(8,128)S(1)}, u32[]{:S(2)}, u32[]{:S(2)}) %collective-permute-start.16) | collective-permute-done | bytes 786464 | tf_op jit(solution)/shard_map/ppermute | solution.py:28
  365.9 7.8 %back_rows.3 = f32[8,2,4,96,128]{4,3,2,1,0:T(8,128)} custom-call(s32[1]{0:T(128)} %bitcast.1.refs_0_, f32[2,4,192,128]{3,2,1,0:T(8,128)} %get-tuple-element.50.refs_1_, f32[2,4,192,128]{3,2,1,0:T(8,128)} %copy-done.27, f32[2,4,192,128]{3,2,1,0:T(8,128)} %copy-done.28, f32[2,4,192,128]{3,2,1,0:T(8,128)} %copy-done.29, ...), custom_call_target="tpu_custom_call" | custom-call | bytes 31457280 | tf_op jit(solution)/shard_map/back_rows/pallas_call | solution.py:515
  373.7 13.2 %all-to-all-done.2 = f32[8,2,4,96,128]{4,3,2,1,0:T(8,128)} async-done(((f32[8,2,4,96,128]{4,3,2,1,0:T(8,128)}), f32[8,2,4,96,128]{4,3,2,1,0:T(8,128)}, u32[]{:S(2)}, u32[]{:S(2)}) %all-to-all-start.2) | async-done | bytes 3145760 | tf_op jit(solution)/shard_map/all_to_all | solution.py:766
  386.8 4.6 all-to-all-start.3
  407.2 1.9 collective-permute-start.9
  411.7 28.0 %collective-permute-done.9 = f32[120,24,128]{2,1,0:T(8,128)S(1)} collective-permute-done((f32[120,24,128]{2,1,0:T(8,128)}, f32[120,24,128]{2,1,0:T(8,128)S(1)}, u32[]{:S(2)}, u32[]{:S(2)}) %collective-permute-start.9) | collective-permute-done | bytes 1474592 | tf_op jit(solution)/shard_map/ppermute | solution.py:28
  440.1 3.0 collective-permute-done.10
  443.3 1.2 fusion.12
  444.5 1.2 fusion.6
  445.7 1.5 pad_maximum_fusion.refs_4_.base
  447.1 14.4 %all-to-all-done.3 = f32[8,2,4,96,128]{4,3,2,1,0:T(8,128)} async-done(((f32[8,2,4,96,128]{4,3,2,1,0:T(8,128)}), f32[8,2,4,96,128]{4,3,2,1,0:T(8,128)}, u32[]{:S(2)}, u32[]{:S(2)}) %all-to-all-start.3) | async-done | bytes 3145760 | tf_op jit(solution)/shard_map/all_to_all | solution.py:766
  461.5 3.8 back_depth.2
  465.3 8.5 %back_depth.3 = f32[32,3,128,128]{3,2,1,0:T(8,128)} custom-call(f32[64,3,32,128]{3,2,1,0:T(8,128)} %bitcast.19.refs_0_, f32[64,3,32,128]{3,2,1,0:T(8,128)} %bitcast.20.refs_1_, bf16[128,128]{1,0:T(8,128)(2,1)} %constant.135.clone.refs_2_, bf16[128,128]{1,0:T(8,128)(2,1)} %constant.136.clone.refs_3_, f32[24,128,128]{2,1,0:T(8,128)} %bitcast.39), custom_call_target="tpu_custom_call" | custom-call | bytes 62914560 | tf_op jit(solution)/shard_map/back_depth/pallas_call | solution.py:557
  473.9 1.5 slice.300
  475.4 2.1 collective-permute-start.18
  478.5 3.6 collective-permute-start.20
  482.0 2.8 copy-done.8
  484.8 1.7 apply_potential.2.base
  486.5 24.8 %collective-permute-done.20.refs_2_ = f32[24,24,128]{2,1,0:T(8,128)S(1)} collective-permute-done((f32[24,24,128]{2,1,0:T(8,128)S(1)}, f32[24,24,128]{2,1,0:T(8,128)S(1)}, u32[]{:S(2)}, u32[]{:S(2)}) %collective-permute-start.20) | collective-permute-done | bytes 294944 | tf_op jit(solution)/shard_map/ppermute | solution.py:780
  511.3 3.0 apply_potential.3
  (101 shorter events, 20.0 us)
Async XLA Ops:
  2.4 1.6 copy-start.3
  4.0 0.8 copy-start.16
  4.8 0.8 copy-start.17
  10.0 8.3 %copy-start.13 = (bf16[512,512]{1,0:T(8,128)(2,1)S(1)}, bf16[512,512]{1,0:T(8,128)(2,1)}, u32[]{:S(2)}) copy-start(bf16[512,512]{1,0:T(8,128)(2,1)} %constant.124.clone.refs_2_) | copy-start | bytes 1572868
  10.0 71.0 %all-to-all-start = ((f32[8,520,128]{2,1,0:T(8,128)}), f32[8,520,128]{2,1,0:T(8,128)}, u32[]{:S(2)}, u32[]{:S(2)}) async-start(f32[8,520,128]{2,1,0:T(8,128)} %box_depth.1.refs_3_), calls=%async_computation | async-start | bytes 4259840 | tf_op jit(solution)/shard_map/all_to_all | solution.py:766
  16.9 4.6 collective-permute-start
  18.3 2.8 copy-start
  21.1 1.0 copy-start.11
  21.1 1.0 copy-start.15
  24.2 28.7 %collective-permute-start.3 = (f32[3,192,512]{2,1,0:T(8,128)S(1)}, f32[3,192,512]{2,1,0:T(8,128)S(1)}, u32[]{:S(2)}, u32[]{:S(2)}) collective-permute-start(f32[3,192,512]{2,1,0:T(8,128)S(1)} %mirror_planes.3.refs_5_), channel_id=1, source_target_pairs={{0,3},{1,2},{2,1},{3,0},{4,7},{5,6},{6,5},{7,4},{8,11},{9,10},{10,... | collective-permute-start | bytes 3538952 | tf_op jit(solution)/shard_map/ppermute | solution.py:845
  31.4 71.6 %collective-permute-start.6 = (f32[4,192,512]{2,1,0:T(8,128)}, f32[4,192,512]{2,1,0:T(8,128)}, u32[]{:S(2)}, u32[]{:S(2)}) collective-permute-start(f32[4,192,512]{2,1,0:T(8,128)} %mirror_planes.5.refs_3_), channel_id=1, source_target_pairs={{0,3},{1,2},{2,1},{3,0},{4,7},{5,6},{6,5},{7,4},{8,11},{9,10},{10,... | collective-permute-start | bytes 4718600 | tf_op jit(solution)/shard_map/ppermute | solution.py:845
  32.0 70.9 %collective-permute-start.5 = (f32[2,192,512]{2,1,0:T(8,128)}, f32[2,192,512]{2,1,0:T(8,128)}, u32[]{:S(2)}, u32[]{:S(2)}) collective-permute-start(f32[2,192,512]{2,1,0:T(8,128)} %mirror_planes.4.refs_5_), channel_id=1, source_target_pairs={{0,3},{1,2},{2,1},{3,0},{4,7},{5,6},{6,5},{7,4},{8,11},{9,10},{10,... | collective-permute-start | bytes 2359304 | tf_op jit(solution)/shard_map/ppermute | solution.py:845
  52.9 7.7 %copy-start.23 = (f32[3,192,512]{2,1,0:T(8,128)}, f32[3,192,512]{2,1,0:T(8,128)S(1)}, u32[]{:S(2)}) copy-start(f32[3,192,512]{2,1,0:T(8,128)S(1)} %collective-permute-done.3) | copy-start | bytes 3538948
  54.0 48.9 %collective-permute-start.7 = (f32[2,192,512]{2,1,0:T(8,128)}, f32[2,192,512]{2,1,0:T(8,128)}, u32[]{:S(2)}, u32[]{:S(2)}) collective-permute-start(f32[2,192,512]{2,1,0:T(8,128)} %slice.280.refs_7_), channel_id=1, source_target_pairs={{0,28},{4,24},{8,20},{12,16},{16,12},{20,8},{24,4},{28,0},{1,29},{... | collective-permute-start | bytes 2359304 | tf_op jit(solution)/shard_map/ppermute | solution.py:853
  57.8 45.1 %collective-permute-start.4 = (f32[1,192,512]{2,1,0:T(8,128)}, f32[1,192,512]{2,1,0:T(8,128)}, u32[]{:S(2)}, u32[]{:S(2)}) collective-permute-start(f32[1,192,512]{2,1,0:T(8,128)} %slice_select_fusion.1), channel_id=1, source_target_pairs={{0,16},{4,28},{8,24},{12,20},{1,17},{5,29},{9,25},{13,21},{2,18},{... | collective-permute-start | bytes 1179656 | tf_op jit(solution)/shard_map/ppermute | solution.py:850
  60.7 2.8 copy-start.1
  63.5 1.0 copy-start.14
  64.5 3.5 copy-start.4
  68.0 80.7 %copy-start.2 = (f32[8,192,512]{2,1,0:T(8,128)}, f32[8,192,512]{2,1,0:T(8,128)S(1)}, u32[]{:S(2)}) copy-start(f32[8,192,512]{2,1,0:T(8,128)S(1)} %order_planes.3.refs_2_.refs_5_.refs_3_) | copy-start | bytes 9437188
  69.8 3.6 copy-start.6
  73.4 1.3 copy-start.18
  74.7 1.2 copy-start.19
  125.4 101.2 %all-to-all-start.1 = ((f32[4,2,11,192,128]{4,3,2,1,0:T(8,128)}), f32[4,2,11,192,128]{4,3,2,1,0:T(8,128)}, u32[]{:S(2)}, u32[]{:S(2)}) async-start(f32[4,2,11,192,128]{4,3,2,1,0:T(8,128)} %box_rows.1), calls=%async_computation.1 | async-start | bytes 17301504 | tf_op jit(solution)/shard_map/all_to_all | solution.py:766
  131.4 133.2 %collective-permute-start.1 = (f32[24,152,128]{2,1,0:T(8,128)}, f32[24,152,128]{2,1,0:T(8,128)}, u32[]{:S(2)}, u32[]{:S(2)}) collective-permute-start(f32[24,152,128]{2,1,0:T(8,128)} %copy-done.19), channel_id=1, source_target_pairs={{0,4},{4,8},{8,12},{12,16},{16,20},{20,24},{24,28},{28,0},{1,5},{5... | collective-permute-start | bytes 5603336 | tf_op jit(solution)/shard_map/ppermute | solution.py:28
  143.5 122.3 %collective-permute-start.2 = (f32[24,152,128]{2,1,0:T(8,128)}, f32[24,152,128]{2,1,0:T(8,128)}, u32[]{:S(2)}, u32[]{:S(2)}) collective-permute-start(f32[24,152,128]{2,1,0:T(8,128)} %copy-done.18), channel_id=1, source_target_pairs={{0,28},{4,0},{8,4},{12,8},{16,12},{20,16},{24,20},{28,24},{1,29},{... | collective-permute-start | bytes 5603336 | tf_op jit(solution)/shard_map/ppermute | solution.py:28
  143.5 63.0 %collective-permute-start.8 = (f32[2,192,512]{2,1,0:T(8,128)}, f32[2,192,512]{2,1,0:T(8,128)}, u32[]{:S(2)}, u32[]{:S(2)}) collective-permute-start(f32[2,192,512]{2,1,0:T(8,128)} %collective-permute-done.5.refs_8_), channel_id=1, source_target_pairs={{0,28},{4,24},{8,20},{12,16},{16,12},{20,8},{24,4},{28,0},{1,29},{... | collective-permute-start | bytes 2359304 | tf_op jit(solution)/shard_map/ppermute | solution.py:853
  148.7 131.4 %collective-permute-start.14 = (f32[4,192,512]{2,1,0:T(8,128)}, f32[4,192,512]{2,1,0:T(8,128)}, u32[]{:S(2)}, u32[]{:S(2)}) collective-permute-start(f32[4,192,512]{2,1,0:T(8,128)} %collective-permute-done.6.refs_9_), channel_id=1, source_target_pairs={{0,28},{4,24},{8,20},{12,16},{16,12},{20,8},{24,4},{28,0},{1,29},{... | collective-permute-start | bytes 4718600 | tf_op jit(solution)/shard_map/ppermute | solution.py:853
  239.8 40.3 %collective-permute-start.11 = (f32[2,4,192,128]{3,2,1,0:T(8,128)}, f32[2,4,192,128]{3,2,1,0:T(8,128)S(1)}, u32[]{:S(2)}, u32[]{:S(2)}) collective-permute-start(f32[2,4,192,128]{3,2,1,0:T(8,128)} %get-tuple-element.47), channel_id=1, source_target_pairs={{0,1},{1,2},{2,3},{3,0},{4,5},{5,6},{6,7},{7,4},{8,9},{9,10},{10,1... | collective-permute-start | bytes 2359304 | tf_op jit(solution)/shard_map/ppermute | solution.py:28
  240.7 39.4 %collective-permute-start.12 = (f32[2,4,192,128]{3,2,1,0:T(8,128)}, f32[2,4,192,128]{3,2,1,0:T(8,128)S(1)}, u32[]{:S(2)}, u32[]{:S(2)}) collective-permute-start(f32[2,4,192,128]{3,2,1,0:T(8,128)} %get-tuple-element.48), channel_id=1, source_target_pairs={{0,2},{1,3},{2,0},{3,1},{4,6},{5,7},{6,4},{7,5},{8,10},{9,11},{10,... | collective-permute-start | bytes 2359304 | tf_op jit(solution)/shard_map/ppermute | solution.py:28
  264.6 15.5 %collective-permute-start.13 = (f32[2,4,192,128]{3,2,1,0:T(8,128)}, f32[2,4,192,128]{3,2,1,0:T(8,128)S(1)}, u32[]{:S(2)}, u32[]{:S(2)}) collective-permute-start(f32[2,4,192,128]{3,2,1,0:T(8,128)} %get-tuple-element.49), channel_id=1, source_target_pairs={{0,3},{1,0},{2,1},{3,2},{4,7},{5,4},{6,5},{7,6},{8,11},{9,8},{10,9... | collective-permute-start | bytes 2359304 | tf_op jit(solution)/shard_map/ppermute | solution.py:28
  265.8 3.7 copy-start.7
  269.4 1.1 copy-start.12
  274.2 3.6 copy-start.9
  277.8 1.2 copy-start.20
  279.0 1.1 copy-start.22
  280.1 0.9 copy-start.24
  280.1 1.1 copy-start.25
  280.1 1.4 copy-start.26
  289.4 97.4 %all-to-all-start.2 = ((f32[8,2,4,96,128]{4,3,2,1,0:T(8,128)}), f32[8,2,4,96,128]{4,3,2,1,0:T(8,128)}, u32[]{:S(2)}, u32[]{:S(2)}) async-start(f32[8,2,4,96,128]{4,3,2,1,0:T(8,128)} %back_rows.2.refs_9_), calls=%async_computation.2 | async-start | bytes 6291456 | tf_op jit(solution)/shard_map/all_to_all | solution.py:766
  327.5 16.0 %collective-permute-start.15 = (f32[2,4,192,128]{3,2,1,0:T(8,128)}, f32[2,4,192,128]{3,2,1,0:T(8,128)S(1)}, u32[]{:S(2)}, u32[]{:S(2)}) collective-permute-start(f32[2,4,192,128]{3,2,1,0:T(8,128)} %get-tuple-element.51), channel_id=1, source_target_pairs={{0,1},{1,2},{2,3},{3,0},{4,5},{5,6},{6,7},{7,4},{8,9},{9,10},{10,1... | collective-permute-start | bytes 2359304 | tf_op jit(solution)/shard_map/ppermute | solution.py:28
  328.0 36.3 %collective-permute-start.16 = (f32[2,4,192,128]{3,2,1,0:T(8,128)}, f32[2,4,192,128]{3,2,1,0:T(8,128)S(1)}, u32[]{:S(2)}, u32[]{:S(2)}) collective-permute-start(f32[2,4,192,128]{3,2,1,0:T(8,128)} %get-tuple-element.52), channel_id=1, source_target_pairs={{0,2},{1,3},{2,0},{3,1},{4,6},{5,7},{6,4},{7,5},{8,10},{9,11},{10,... | collective-permute-start | bytes 2359304 | tf_op jit(solution)/shard_map/ppermute | solution.py:28
  329.7 35.3 %collective-permute-start.17 = (f32[2,4,192,128]{3,2,1,0:T(8,128)}, f32[2,4,192,128]{3,2,1,0:T(8,128)S(1)}, u32[]{:S(2)}, u32[]{:S(2)}) collective-permute-start(f32[2,4,192,128]{3,2,1,0:T(8,128)} %get-tuple-element.53), channel_id=1, source_target_pairs={{0,3},{1,0},{2,1},{3,2},{4,7},{5,4},{6,5},{7,6},{8,11},{9,8},{10,9... | collective-permute-start | bytes 2359304 | tf_op jit(solution)/shard_map/ppermute | solution.py:28
  343.5 21.5 %copy-start.27 = (f32[2,4,192,128]{3,2,1,0:T(8,128)}, f32[2,4,192,128]{3,2,1,0:T(8,128)S(1)}, u32[]{:S(2)}) copy-start(f32[2,4,192,128]{3,2,1,0:T(8,128)S(1)} %collective-permute-done.15.refs_2_) | copy-start | bytes 2359300
  364.4 0.9 copy-start.28
  365.0 0.9 copy-start.29
  373.7 35.4 %copy-start.5 = (f32[4,32,32,128]{3,2,1,0:T(8,128)S(1)}, f32[4,32,32,128]{3,2,1,0:T(8,128)}, u32[]{:S(2)}) copy-start(f32[4,32,32,128]{3,2,1,0:T(8,128)} %eta.3) | copy-start | bytes 6291460
  386.8 74.7 %all-to-all-start.3 = ((f32[8,2,4,96,128]{4,3,2,1,0:T(8,128)}), f32[8,2,4,96,128]{4,3,2,1,0:T(8,128)}, u32[]{:S(2)}, u32[]{:S(2)}) async-start(f32[8,2,4,96,128]{4,3,2,1,0:T(8,128)} %back_rows.3), calls=%async_computation.3 | async-start | bytes 6291456 | tf_op jit(solution)/shard_map/all_to_all | solution.py:766
  407.2 2.1 copy-start.21
  407.2 32.5 %collective-permute-start.9 = (f32[120,24,128]{2,1,0:T(8,128)}, f32[120,24,128]{2,1,0:T(8,128)S(1)}, u32[]{:S(2)}, u32[]{:S(2)}) collective-permute-start(f32[120,24,128]{2,1,0:T(8,128)} %copy-done.22), channel_id=1, source_target_pairs={{0,1},{1,2},{2,3},{3,0},{4,5},{5,6},{6,7},{7,4},{8,9},{9,10},{10,1... | collective-permute-start | bytes 4423688 | tf_op jit(solution)/shard_map/ppermute | solution.py:28
  409.1 30.6 %slice-start = ((s8[9338880]{0:T(1024)(128)(4,1)}), s8[4194304]{0:T(1024)(128)(4,1)S(1)}, s32[]{:S(2)}) async-start(s8[9338880]{0:T(1024)(128)(4,1)} %bitcast.36), calls=%async_computation.4 | async-start | bytes 8388608
  409.3 33.7 %collective-permute-start.10 = (f32[120,24,128]{2,1,0:T(8,128)S(1)}, f32[120,24,128]{2,1,0:T(8,128)S(1)}, u32[]{:S(2)}, u32[]{:S(2)}) collective-permute-start(f32[120,24,128]{2,1,0:T(8,128)S(1)} %copy-done.21), channel_id=1, source_target_pairs={{0,3},{1,0},{2,1},{3,2},{4,7},{5,4},{6,5},{7,6},{8,11},{9,8},{10,9... | collective-permute-start | bytes 4423688 | tf_op jit(solution)/shard_map/ppermute | solution.py:28
  410.2 29.5 %slice-start.1 = ((s8[9338880]{0:T(1024)(128)(4,1)}), s8[4194304]{0:T(1024)(128)(4,1)S(1)}, s32[]{:S(2)}) async-start(s8[9338880]{0:T(1024)(128)(4,1)} %bitcast.36), calls=%async_computation.5 | async-start | bytes 8388608
  411.0 28.8 %slice-start.2 = ((s8[9338880]{0:T(1024)(128)(4,1)}), s8[950272]{0:T(1024)(128)(4,1)S(1)}, s32[]{:S(2)}) async-start(s8[9338880]{0:T(1024)(128)(4,1)} %bitcast.36), calls=%async_computation.6 | async-start | bytes 1900544
  465.3 46.0 %collective-permute-start.19 = (f32[24,128,128]{2,1,0:T(8,128)}, f32[24,128,128]{2,1,0:T(8,128)S(1)}, u32[]{:S(2)}, u32[]{:S(2)}) collective-permute-start(f32[24,128,128]{2,1,0:T(8,128)} %bitcast.38), channel_id=1, source_target_pairs={{0,28},{4,0},{8,4},{12,8},{16,12},{20,16},{24,20},{28,24},{1,29},{... | collective-permute-start | bytes 4718600 | tf_op jit(solution)/shard_map/ppermute | solution.py:28
  473.9 8.2 %copy-start.10 = (f32[4,32,32,128]{3,2,1,0:T(8,128)S(1)}, f32[4,32,32,128]{3,2,1,0:T(8,128)}, u32[]{:S(2)}) copy-start(f32[4,32,32,128]{3,2,1,0:T(8,128)} %pad_maximum_fusion.refs_4_.base) | copy-start | bytes 6291460
  475.4 35.9 %collective-permute-start.18 = (f32[96,24,128]{2,1,0:T(8,128)S(1)}, f32[96,24,128]{2,1,0:T(8,128)S(1)}, u32[]{:S(2)}, u32[]{:S(2)}) collective-permute-start(f32[96,24,128]{2,1,0:T(8,128)S(1)} %slice.300), channel_id=1, source_target_pairs={{0,3},{1,0},{2,1},{3,2},{4,7},{5,4},{6,5},{7,6},{8,11},{9,8},{10,9... | collective-permute-start | bytes 3538952 | tf_op jit(solution)/shard_map/ppermute | solution.py:28
  478.5 32.8 %collective-permute-start.20 = (f32[24,24,128]{2,1,0:T(8,128)S(1)}, f32[24,24,128]{2,1,0:T(8,128)S(1)}, u32[]{:S(2)}, u32[]{:S(2)}) collective-permute-start(f32[24,24,128]{2,1,0:T(8,128)S(1)} %slice.301), channel_id=1, source_target_pairs={{0,31},{1,28},{2,29},{3,30},{4,3},{5,0},{6,1},{7,2},{8,7},{9,4},{1... | collective-permute-start | bytes 884744 | tf_op jit(solution)/shard_map/ppermute | solution.py:780
  482.0 2.8 copy-start.8

commit v4 on v3

--- a/solution.py
+++ b/solution.py
@@ -89,9 +89,8 @@
     for l in range(RADIX):
         angles = angle_of(m[:, None] * (RADIX * m[None, :] + l), length)
         c, s = np.cos(angles), np.sin(angles)
-        forward.append(np.block([[c, s], [-s, c]]))
-        c, s = c.T, s.T
-        inverse.append(np.block([[c, -s], [s, c]]))
+        forward.append(np.stack([c, s - c, c + s]))
+        inverse.append(np.stack([c.T, (s - c).T, (c + s).T]))
     return pair_of(np.array(forward)), pair_of(np.array(inverse))
 
 
@@ -288,9 +287,15 @@
     terms = []
     for l in range(RADIX):
         take = pl.ds(l, part, stride=RADIX)
-        values = jnp.concatenate([lines[0, 0, take, :], lines[0, 1, take, :] * sign], axis=0)
-        terms.append(table_first(high[l], low[l], values))
-    real, imag = [v[:part] for v in terms], [v[part:] for v in terms]
+        re, im = lines[0, 0, take, :], lines[0, 1, take, :] * sign
+        both = table_first(high[l, 0], low[l, 0], re + im)
+        terms.append(
+            (
+                both + table_first(high[l, 1], low[l, 1], im),
+                both - table_first(high[l, 2], low[l, 2], re),
+            )
+        )
+    real, imag = [v[0] for v in terms], [v[1] for v in terms]
     root = math.sqrt(0.75)
     sum_re, sum_im = real[1] + real[2], imag[1] + imag[2]
     dif_re, dif_im = root * (real[1] - real[2]), root * (imag[1] - imag[2])
@@ -495,9 +500,14 @@
         (mid_re + dif_im, mid_im - dif_re),
     ]
     for l in range(RADIX):
-        result = table_first(high[l], low[l], jnp.concatenate(terms[l], axis=0))
+        re, im = terms[l]
+        both = table_first(high[l, 0], low[l, 0], re + im)
+        result = (
+            both - table_first(high[l, 2], low[l, 2], im),
+            both + table_first(high[l, 1], low[l, 1], re),
+        )
         for ri in range(2):
-            values = result[ri * part : (ri + 1) * part].reshape(owners, group, cols)
+            values = result[ri].reshape(owners, group, cols)
             out[:, ri, 0, l * group : (l + 1) * group, :] = values
 
 

time: 516 us -> 513 us (level)
  no operation moved by 1% of the time
where the time goes in v4:
time: 513 us; the launch traced here: 511 us
  waiting for transfers between devices  262 us (51%)
  Pallas kernels  96.9 us (19%)
  starting transfers between devices  85.2 us (17%)
  local copies, waits for them, and re-layouts  40.9 us (8%)
  between operations  16 us (3%)
  other arithmetic  10.7 us (2%)
    ppermute x13, waiting for transfers between devices, from_behind(): lax.ppermute(shard, axis, [(i, (i + by) % peers) for i in range(peers)])  88.8 us
    ppermute x3, waiting for transfers between devices, on_device(): mirror = [lax.ppermute(planes, 'px', opposite) for planes in first_leg]  55.5 us
    all_to_all x4, waiting for transfers between devices, exchange(): return lax.all_to_all(shard, axis, split_axis=0, concat_axis=0, tiled=True)  53.4 us
    all_to_all x4, starting transfers between devices, exchange(): return lax.all_to_all(shard, axis, split_axis=0, concat_axis=0, tiled=True)  43.9 us
    ppermute x3, waiting for transfers between devices, on_device(): first_leg = [lax.ppermute(planes, 'py', facing) for planes in mirror[1:]]  39.1 us
    unnamed x66, local copies, waits for them, and re-layouts  32.3 us
    ppermute x1, waiting for transfers between devices, potential_pieces(): corner = lax.ppermute(rows[:, :over_y], ('px', 'py'), pairs)  24.9 us
    pallas_call x2, Pallas kernels, grid_columns(): pl.pallas_call(functools.partial(columns_kernel, slots, over, has_packs,...  24 us
  transfers between devices with their start and end apart: 25, of which 15 were waited for; matrix products, arithmetic and copies ran while one was open for 3% of the time, Pallas kernels for 11%

profile of v4, /device:TPU:5, one launch (start us, length us, event | category | flops | bytes accessed | tf_op | source)
XLA Modules:
  0.0 511.3 jit_solution(12045731880056963170)
XLA Ops:
  2.5 1.6 copy-done.3
  5.6 4.4 box_depth.1.refs_3_
  10.0 5.9 %all-to-all-start = ((f32[8,520,128]{2,1,0:T(8,128)}), f32[8,520,128]{2,1,0:T(8,128)}, u32[]{:S(2)}, u32[]{:S(2)}) async-start(f32[8,520,128]{2,1,0:T(8,128)} %box_depth.1.refs_3_), calls=%async_computation | async-start | bytes 4259840 | tf_op jit(solution)/shard_map/all_to_all | solution.py:776
  16.9 1.3 collective-permute-start
  18.3 2.8 copy-done
  22.1 2.1 mirror_planes.3.refs_5_
  24.2 1.2 collective-permute-start.3
  25.5 2.3 mirror_planes.4.refs_5_
  27.8 3.6 mirror_planes.5.refs_3_
  32.0 1.1 collective-permute-start.5
  33.1 19.8 %collective-permute-done.3 = f32[3,192,512]{2,1,0:T(8,128)S(1)} collective-permute-done((f32[3,192,512]{2,1,0:T(8,128)S(1)}, f32[3,192,512]{2,1,0:T(8,128)S(1)}, u32[]{:S(2)}, u32[]{:S(2)}) %collective-permute-start.3) | collective-permute-done | bytes 1179680 | tf_op jit(solution)/shard_map/ppermute | solution.py:855
  54.0 3.0 collective-permute-start.7
  57.8 2.7 collective-permute-start.4
  60.7 2.8 copy-done.1
  64.5 3.5 order_planes.3.refs_2_.refs_5_.refs_3_
  68.0 1.7 occupancy_patch.1
  69.8 3.6 copy-done.6
  73.4 1.3 copy-done.18
  74.7 1.2 copy-done.19
  75.9 5.1 all-to-all-done.refs_1_.refs_2_
  81.0 1.4 fusion.56
  82.4 1.3 convert_element_type.17.refs_0_
  83.6 19.3 %collective-permute-done.5.refs_8_ = f32[2,192,512]{2,1,0:T(8,128)} collective-permute-done((f32[2,192,512]{2,1,0:T(8,128)}, f32[2,192,512]{2,1,0:T(8,128)}, u32[]{:S(2)}, u32[]{:S(2)}) %collective-permute-start.5) | collective-permute-done | bytes 786464 | tf_op jit(solution)/shard_map/ppermute | solution.py:855
  102.9 20.0 %box_rows.1 = f32[4,2,11,192,128]{4,3,2,1,0:T(8,128)} custom-call(s32[64]{0:T(128)} %convert_element_type.17.refs_0_, f32[8,520,128]{2,1,0:T(8,128)} %all-to-all-done.refs_1_.refs_2_, f32[8,520,128]{2,1,0:T(8,128)} %all-to-all-done.refs_1_.refs_2_, bf16[3,3,256,256]{3,2,1,0:T(8,128)(2,1)} %constant.127.clone.refs_3_, ...), custom_call_target="tpu_custom_call" | custom-call | bytes 53903360 | tf_op jit(solution)/shard_map/box_rows/pallas_call | solution.py:323
  123.0 6.0 %all-to-all-start.1 = ((f32[4,2,11,192,128]{4,3,2,1,0:T(8,128)}), f32[4,2,11,192,128]{4,3,2,1,0:T(8,128)}, u32[]{:S(2)}, u32[]{:S(2)}) async-start(f32[4,2,11,192,128]{4,3,2,1,0:T(8,128)} %box_rows.1), calls=%async_computation.1 | async-start | bytes 17301504 | tf_op jit(solution)/shard_map/all_to_all | solution.py:776
  129.0 12.1 %collective-permute-start.1 = (f32[24,152,128]{2,1,0:T(8,128)}, f32[24,152,128]{2,1,0:T(8,128)}, u32[]{:S(2)}, u32[]{:S(2)}) collective-permute-start(f32[24,152,128]{2,1,0:T(8,128)} %copy-done.19), channel_id=1, source_target_pairs={{0,4},{4,8},{8,12},{12,16},{16,20},{20,24},{24,28},{28,0},{1,5},{5... | collective-permute-start | bytes 5603336 | tf_op jit(solution)/shard_map/ppermute | solution.py:28
  141.1 5.2 %collective-permute-start.8 = (f32[2,192,512]{2,1,0:T(8,128)}, f32[2,192,512]{2,1,0:T(8,128)}, u32[]{:S(2)}, u32[]{:S(2)}) collective-permute-start(f32[2,192,512]{2,1,0:T(8,128)} %collective-permute-done.5.refs_8_), channel_id=1, source_target_pairs={{0,28},{4,24},{8,20},{12,16},{16,12},{20,8},{24,4},{28,0},{1,29},{... | collective-permute-start | bytes 2359304 | tf_op jit(solution)/shard_map/ppermute | solution.py:863
  146.3 2.3 select_bitcast_fusion
  148.6 55.5 %collective-permute-done.8.refs_7_.refs_9_ = f32[2,192,512]{2,1,0:T(8,128)} collective-permute-done((f32[2,192,512]{2,1,0:T(8,128)}, f32[2,192,512]{2,1,0:T(8,128)}, u32[]{:S(2)}, u32[]{:S(2)}) %collective-permute-start.8) | collective-permute-done | bytes 786464 | tf_op jit(solution)/shard_map/ppermute | solution.py:863
  204.1 20.1 %all-to-all-done.1.refs_1_.refs_2_.refs_3_.refs_4_ = f32[4,2,11,192,128]{4,3,2,1,0:T(8,128)} async-done(((f32[4,2,11,192,128]{4,3,2,1,0:T(8,128)}), f32[4,2,11,192,128]{4,3,2,1,0:T(8,128)}, u32[]{:S(2)}, u32[]{:S(2)}) %all-to-all-start.1) | async-done | bytes 8650784 | tf_op jit(solution)/shard_map/all_to_all | solution.py:776
  224.1 13.2 %grid_columns.2 = (f32[2,4,192,128]{3,2,1,0:T(8,128)}, f32[2,4,192,128]{3,2,1,0:T(8,128)}, f32[2,4,192,128]{3,2,1,0:T(8,128)}, f32[2,4,192,128]{3,2,1,0:T(8,128)}) custom-call(s32[1]{0:T(128)} %bitcast.1.refs_0_, f32[4,2,11,192,128]{4,3,2,1,0:T(8,128)} %all-to-all-done.1.refs_1_.refs_2_.refs_3_.refs_4_, ...), custom_call_target="tpu_custom_call" | custom-call | bytes 47185920 | tf_op jit(solution)/shard_map/grid_columns/pallas_call | solution.py:460
  238.3 1.4 collective-permute-start.12
  239.6 22.5 %collective-permute-done.1.refs_1_ = f32[24,152,128]{2,1,0:T(8,128)} collective-permute-done((f32[24,152,128]{2,1,0:T(8,128)}, f32[24,152,128]{2,1,0:T(8,128)}, u32[]{:S(2)}, u32[]{:S(2)}) %collective-permute-start.1) | collective-permute-done | bytes 1867808 | tf_op jit(solution)/shard_map/ppermute | solution.py:28
  263.4 3.6 copy-done.7
  267.0 1.1 copy-done.12
  268.1 3.6 join_rows.1
  271.8 3.6 copy-done.9
  275.4 1.2 copy-done.20
  276.6 1.1 copy-done.22
  279.1 7.2 %back_rows.2.refs_9_ = f32[8,2,4,96,128]{4,3,2,1,0:T(8,128)} custom-call(s32[1]{0:T(128)} %bitcast.1.refs_0_, f32[2,4,192,128]{3,2,1,0:T(8,128)} %get-tuple-element.43.refs_3_.refs_1_, f32[2,4,192,128]{3,2,1,0:T(8,128)} %copy-done.24, f32[2,4,192,128]{3,2,1,0:T(8,128)} %copy-done.25, f32[2,4,192,128]{3,2,1,0:T(8,128)} %copy-done.26, ...), custom_call_target="tpu_custom_call" | custom-call | bytes 31457280 | tf_op jit(solution)/shard_map/back_rows/pallas_call | solution.py:525
  286.2 27.3 %all-to-all-start.2 = ((f32[8,2,4,96,128]{4,3,2,1,0:T(8,128)}), f32[8,2,4,96,128]{4,3,2,1,0:T(8,128)}, u32[]{:S(2)}, u32[]{:S(2)}) async-start(f32[8,2,4,96,128]{4,3,2,1,0:T(8,128)} %back_rows.2.refs_9_), calls=%async_computation.2 | async-start | bytes 6291456 | tf_op jit(solution)/shard_map/all_to_all | solution.py:776
  313.6 10.8 %grid_columns.3 = (f32[2,4,192,128]{3,2,1,0:T(8,128)}, f32[2,4,192,128]{3,2,1,0:T(8,128)}, f32[2,4,192,128]{3,2,1,0:T(8,128)}, f32[2,4,192,128]{3,2,1,0:T(8,128)}) custom-call(s32[1]{0:T(128)} %bitcast.1.refs_0_, f32[4,2,11,192,128]{4,3,2,1,0:T(8,128)} %all-to-all-done.1.refs_1_.refs_2_.refs_3_.refs_4_, ...), custom_call_target="tpu_custom_call" | custom-call | bytes 47185920 | tf_op jit(solution)/shard_map/grid_columns/pallas_call | solution.py:460
  324.9 1.7 collective-permute-start.16
  326.9 13.5 %collective-permute-done.15.refs_2_ = f32[2,4,192,128]{3,2,1,0:T(8,128)S(1)} collective-permute-done((f32[2,4,192,128]{3,2,1,0:T(8,128)}, f32[2,4,192,128]{3,2,1,0:T(8,128)S(1)}, u32[]{:S(2)}, u32[]{:S(2)}) %collective-permute-start.15) | collective-permute-done | bytes 786464 | tf_op jit(solution)/shard_map/ppermute | solution.py:28
  340.3 20.9 %collective-permute-done.16.refs_3_ = f32[2,4,192,128]{3,2,1,0:T(8,128)S(1)} collective-permute-done((f32[2,4,192,128]{3,2,1,0:T(8,128)}, f32[2,4,192,128]{3,2,1,0:T(8,128)S(1)}, u32[]{:S(2)}, u32[]{:S(2)}) %collective-permute-start.16) | collective-permute-done | bytes 786464 | tf_op jit(solution)/shard_map/ppermute | solution.py:28
  362.7 7.1 %back_rows.3 = f32[8,2,4,96,128]{4,3,2,1,0:T(8,128)} custom-call(s32[1]{0:T(128)} %bitcast.1.refs_0_, f32[2,4,192,128]{3,2,1,0:T(8,128)} %get-tuple-element.50.refs_1_, f32[2,4,192,128]{3,2,1,0:T(8,128)} %copy-done.27, f32[2,4,192,128]{3,2,1,0:T(8,128)} %copy-done.28, f32[2,4,192,128]{3,2,1,0:T(8,128)} %copy-done.29, ...), custom_call_target="tpu_custom_call" | custom-call | bytes 31457280 | tf_op jit(solution)/shard_map/back_rows/pallas_call | solution.py:525
  369.8 13.9 %all-to-all-done.2 = f32[8,2,4,96,128]{4,3,2,1,0:T(8,128)} async-done(((f32[8,2,4,96,128]{4,3,2,1,0:T(8,128)}), f32[8,2,4,96,128]{4,3,2,1,0:T(8,128)}, u32[]{:S(2)}, u32[]{:S(2)}) %all-to-all-start.2) | async-done | bytes 3145760 | tf_op jit(solution)/shard_map/all_to_all | solution.py:776
  383.7 4.6 all-to-all-start.3
  404.0 1.9 collective-permute-start.9
  408.6 28.0 %collective-permute-done.9 = f32[120,24,128]{2,1,0:T(8,128)S(1)} collective-permute-done((f32[120,24,128]{2,1,0:T(8,128)}, f32[120,24,128]{2,1,0:T(8,128)S(1)}, u32[]{:S(2)}, u32[]{:S(2)}) %collective-permute-start.9) | collective-permute-done | bytes 1474592 | tf_op jit(solution)/shard_map/ppermute | solution.py:28
  436.9 2.9 collective-permute-done.10
  440.2 1.2 fusion.12
  441.3 1.2 fusion.6
  442.5 1.5 pad_maximum_fusion.refs_4_.base
  444.0 14.4 %all-to-all-done.3 = f32[8,2,4,96,128]{4,3,2,1,0:T(8,128)} async-done(((f32[8,2,4,96,128]{4,3,2,1,0:T(8,128)}), f32[8,2,4,96,128]{4,3,2,1,0:T(8,128)}, u32[]{:S(2)}, u32[]{:S(2)}) %all-to-all-start.3) | async-done | bytes 3145760 | tf_op jit(solution)/shard_map/all_to_all | solution.py:776
  458.3 3.8 back_depth.2
  462.2 8.5 %back_depth.3 = f32[32,3,128,128]{3,2,1,0:T(8,128)} custom-call(f32[64,3,32,128]{3,2,1,0:T(8,128)} %bitcast.19.refs_0_, f32[64,3,32,128]{3,2,1,0:T(8,128)} %bitcast.20.refs_1_, bf16[128,128]{1,0:T(8,128)(2,1)} %constant.135.clone.refs_2_, bf16[128,128]{1,0:T(8,128)(2,1)} %constant.136.clone.refs_3_, f32[24,128,128]{2,1,0:T(8,128)} %bitcast.39), custom_call_target="tpu_custom_call" | custom-call | bytes 62914560 | tf_op jit(solution)/shard_map/back_depth/pallas_call | solution.py:567
  470.7 1.5 slice.300
  472.2 2.1 collective-permute-start.18
  475.3 3.6 collective-permute-start.20
  478.9 2.8 copy-done.8
  481.7 1.6 apply_potential.2.base
  483.3 24.9 %collective-permute-done.20.refs_2_ = f32[24,24,128]{2,1,0:T(8,128)S(1)} collective-permute-done((f32[24,24,128]{2,1,0:T(8,128)S(1)}, f32[24,24,128]{2,1,0:T(8,128)S(1)}, u32[]{:S(2)}, u32[]{:S(2)}) %collective-permute-start.20) | collective-permute-done | bytes 294944 | tf_op jit(solution)/shard_map/ppermute | solution.py:790
  508.2 3.1 apply_potential.3
  (101 shorter events, 20.0 us)
Async XLA Ops:
  2.4 1.6 copy-start.3
  4.0 0.8 copy-start.16
  4.8 0.8 copy-start.17
  10.0 8.3 %copy-start.13 = (bf16[512,512]{1,0:T(8,128)(2,1)S(1)}, bf16[512,512]{1,0:T(8,128)(2,1)}, u32[]{:S(2)}) copy-start(bf16[512,512]{1,0:T(8,128)(2,1)} %constant.124.clone.refs_2_) | copy-start | bytes 1572868
  10.0 71.0 %all-to-all-start = ((f32[8,520,128]{2,1,0:T(8,128)}), f32[8,520,128]{2,1,0:T(8,128)}, u32[]{:S(2)}, u32[]{:S(2)}) async-start(f32[8,520,128]{2,1,0:T(8,128)} %box_depth.1.refs_3_), calls=%async_computation | async-start | bytes 4259840 | tf_op jit(solution)/shard_map/all_to_all | solution.py:776
  16.9 4.6 collective-permute-start
  18.3 2.8 copy-start
  21.1 1.0 copy-start.11
  21.1 1.0 copy-start.15
  24.2 28.7 %collective-permute-start.3 = (f32[3,192,512]{2,1,0:T(8,128)S(1)}, f32[3,192,512]{2,1,0:T(8,128)S(1)}, u32[]{:S(2)}, u32[]{:S(2)}) collective-permute-start(f32[3,192,512]{2,1,0:T(8,128)S(1)} %mirror_planes.3.refs_5_), channel_id=1, source_target_pairs={{0,3},{1,2},{2,1},{3,0},{4,7},{5,6},{6,5},{7,4},{8,11},{9,10},{10,... | collective-permute-start | bytes 3538952 | tf_op jit(solution)/shard_map/ppermute | solution.py:855
  31.4 71.6 %collective-permute-start.6 = (f32[4,192,512]{2,1,0:T(8,128)}, f32[4,192,512]{2,1,0:T(8,128)}, u32[]{:S(2)}, u32[]{:S(2)}) collective-permute-start(f32[4,192,512]{2,1,0:T(8,128)} %mirror_planes.5.refs_3_), channel_id=1, source_target_pairs={{0,3},{1,2},{2,1},{3,0},{4,7},{5,6},{6,5},{7,4},{8,11},{9,10},{10,... | collective-permute-start | bytes 4718600 | tf_op jit(solution)/shard_map/ppermute | solution.py:855
  32.0 70.9 %collective-permute-start.5 = (f32[2,192,512]{2,1,0:T(8,128)}, f32[2,192,512]{2,1,0:T(8,128)}, u32[]{:S(2)}, u32[]{:S(2)}) collective-permute-start(f32[2,192,512]{2,1,0:T(8,128)} %mirror_planes.4.refs_5_), channel_id=1, source_target_pairs={{0,3},{1,2},{2,1},{3,0},{4,7},{5,6},{6,5},{7,4},{8,11},{9,10},{10,... | collective-permute-start | bytes 2359304 | tf_op jit(solution)/shard_map/ppermute | solution.py:855
  52.9 7.7 %copy-start.23 = (f32[3,192,512]{2,1,0:T(8,128)}, f32[3,192,512]{2,1,0:T(8,128)S(1)}, u32[]{:S(2)}) copy-start(f32[3,192,512]{2,1,0:T(8,128)S(1)} %collective-permute-done.3) | copy-start | bytes 3538948
  54.0 48.9 %collective-permute-start.7 = (f32[2,192,512]{2,1,0:T(8,128)}, f32[2,192,512]{2,1,0:T(8,128)}, u32[]{:S(2)}, u32[]{:S(2)}) collective-permute-start(f32[2,192,512]{2,1,0:T(8,128)} %slice.280.refs_7_), channel_id=1, source_target_pairs={{0,28},{4,24},{8,20},{12,16},{16,12},{20,8},{24,4},{28,0},{1,29},{... | collective-permute-start | bytes 2359304 | tf_op jit(solution)/shard_map/ppermute | solution.py:863
  57.8 45.1 %collective-permute-start.4 = (f32[1,192,512]{2,1,0:T(8,128)}, f32[1,192,512]{2,1,0:T(8,128)}, u32[]{:S(2)}, u32[]{:S(2)}) collective-permute-start(f32[1,192,512]{2,1,0:T(8,128)} %slice_select_fusion.1), channel_id=1, source_target_pairs={{0,16},{4,28},{8,24},{12,20},{1,17},{5,29},{9,25},{13,21},{2,18},{... | collective-permute-start | bytes 1179656 | tf_op jit(solution)/shard_map/ppermute | solution.py:860
  60.7 2.8 copy-start.1
  63.5 1.0 copy-start.14
  64.5 3.5 copy-start.4
  68.0 78.2 %copy-start.2 = (f32[8,192,512]{2,1,0:T(8,128)}, f32[8,192,512]{2,1,0:T(8,128)S(1)}, u32[]{:S(2)}) copy-start(f32[8,192,512]{2,1,0:T(8,128)S(1)} %order_planes.3.refs_2_.refs_5_.refs_3_) | copy-start | bytes 9437188
  69.8 3.6 copy-start.6
  73.4 1.3 copy-start.18
  74.7 1.2 copy-start.19
  123.0 101.2 %all-to-all-start.1 = ((f32[4,2,11,192,128]{4,3,2,1,0:T(8,128)}), f32[4,2,11,192,128]{4,3,2,1,0:T(8,128)}, u32[]{:S(2)}, u32[]{:S(2)}) async-start(f32[4,2,11,192,128]{4,3,2,1,0:T(8,128)} %box_rows.1), calls=%async_computation.1 | async-start | bytes 17301504 | tf_op jit(solution)/shard_map/all_to_all | solution.py:776
  129.0 133.2 %collective-permute-start.1 = (f32[24,152,128]{2,1,0:T(8,128)}, f32[24,152,128]{2,1,0:T(8,128)}, u32[]{:S(2)}, u32[]{:S(2)}) collective-permute-start(f32[24,152,128]{2,1,0:T(8,128)} %copy-done.19), channel_id=1, source_target_pairs={{0,4},{4,8},{8,12},{12,16},{16,20},{20,24},{24,28},{28,0},{1,5},{5... | collective-permute-start | bytes 5603336 | tf_op jit(solution)/shard_map/ppermute | solution.py:28
  141.1 122.3 %collective-permute-start.2 = (f32[24,152,128]{2,1,0:T(8,128)}, f32[24,152,128]{2,1,0:T(8,128)}, u32[]{:S(2)}, u32[]{:S(2)}) collective-permute-start(f32[24,152,128]{2,1,0:T(8,128)} %copy-done.18), channel_id=1, source_target_pairs={{0,28},{4,0},{8,4},{12,8},{16,12},{20,16},{24,20},{28,24},{1,29},{... | collective-permute-start | bytes 5603336 | tf_op jit(solution)/shard_map/ppermute | solution.py:28
  141.1 63.0 %collective-permute-start.8 = (f32[2,192,512]{2,1,0:T(8,128)}, f32[2,192,512]{2,1,0:T(8,128)}, u32[]{:S(2)}, u32[]{:S(2)}) collective-permute-start(f32[2,192,512]{2,1,0:T(8,128)} %collective-permute-done.5.refs_8_), channel_id=1, source_target_pairs={{0,28},{4,24},{8,20},{12,16},{16,12},{20,8},{24,4},{28,0},{1,29},{... | collective-permute-start | bytes 2359304 | tf_op jit(solution)/shard_map/ppermute | solution.py:863
  146.2 131.4 %collective-permute-start.14 = (f32[4,192,512]{2,1,0:T(8,128)}, f32[4,192,512]{2,1,0:T(8,128)}, u32[]{:S(2)}, u32[]{:S(2)}) collective-permute-start(f32[4,192,512]{2,1,0:T(8,128)} %collective-permute-done.6.refs_9_), channel_id=1, source_target_pairs={{0,28},{4,24},{8,20},{12,16},{16,12},{20,8},{24,4},{28,0},{1,29},{... | collective-permute-start | bytes 4718600 | tf_op jit(solution)/shard_map/ppermute | solution.py:863
  237.4 40.3 %collective-permute-start.11 = (f32[2,4,192,128]{3,2,1,0:T(8,128)}, f32[2,4,192,128]{3,2,1,0:T(8,128)S(1)}, u32[]{:S(2)}, u32[]{:S(2)}) collective-permute-start(f32[2,4,192,128]{3,2,1,0:T(8,128)} %get-tuple-element.47), channel_id=1, source_target_pairs={{0,1},{1,2},{2,3},{3,0},{4,5},{5,6},{6,7},{7,4},{8,9},{9,10},{10,1... | collective-permute-start | bytes 2359304 | tf_op jit(solution)/shard_map/ppermute | solution.py:28
  238.3 39.4 %collective-permute-start.12 = (f32[2,4,192,128]{3,2,1,0:T(8,128)}, f32[2,4,192,128]{3,2,1,0:T(8,128)S(1)}, u32[]{:S(2)}, u32[]{:S(2)}) collective-permute-start(f32[2,4,192,128]{3,2,1,0:T(8,128)} %get-tuple-element.48), channel_id=1, source_target_pairs={{0,2},{1,3},{2,0},{3,1},{4,6},{5,7},{6,4},{7,5},{8,10},{9,11},{10,... | collective-permute-start | bytes 2359304 | tf_op jit(solution)/shard_map/ppermute | solution.py:28
  262.2 15.5 %collective-permute-start.13 = (f32[2,4,192,128]{3,2,1,0:T(8,128)}, f32[2,4,192,128]{3,2,1,0:T(8,128)S(1)}, u32[]{:S(2)}, u32[]{:S(2)}) collective-permute-start(f32[2,4,192,128]{3,2,1,0:T(8,128)} %get-tuple-element.49), channel_id=1, source_target_pairs={{0,3},{1,0},{2,1},{3,2},{4,7},{5,4},{6,5},{7,6},{8,11},{9,8},{10,9... | collective-permute-start | bytes 2359304 | tf_op jit(solution)/shard_map/ppermute | solution.py:28
  263.4 3.7 copy-start.7
  267.0 1.1 copy-start.12
  271.8 3.6 copy-start.9
  275.4 1.2 copy-start.20
  276.6 1.1 copy-start.22
  277.7 0.9 copy-start.24
  277.7 1.1 copy-start.25
  277.7 1.4 copy-start.26
  286.2 97.4 %all-to-all-start.2 = ((f32[8,2,4,96,128]{4,3,2,1,0:T(8,128)}), f32[8,2,4,96,128]{4,3,2,1,0:T(8,128)}, u32[]{:S(2)}, u32[]{:S(2)}) async-start(f32[8,2,4,96,128]{4,3,2,1,0:T(8,128)} %back_rows.2.refs_9_), calls=%async_computation.2 | async-start | bytes 6291456 | tf_op jit(solution)/shard_map/all_to_all | solution.py:776
  324.3 16.0 %collective-permute-start.15 = (f32[2,4,192,128]{3,2,1,0:T(8,128)}, f32[2,4,192,128]{3,2,1,0:T(8,128)S(1)}, u32[]{:S(2)}, u32[]{:S(2)}) collective-permute-start(f32[2,4,192,128]{3,2,1,0:T(8,128)} %get-tuple-element.51), channel_id=1, source_target_pairs={{0,1},{1,2},{2,3},{3,0},{4,5},{5,6},{6,7},{7,4},{8,9},{9,10},{10,1... | collective-permute-start | bytes 2359304 | tf_op jit(solution)/shard_map/ppermute | solution.py:28
  324.9 36.3 %collective-permute-start.16 = (f32[2,4,192,128]{3,2,1,0:T(8,128)}, f32[2,4,192,128]{3,2,1,0:T(8,128)S(1)}, u32[]{:S(2)}, u32[]{:S(2)}) collective-permute-start(f32[2,4,192,128]{3,2,1,0:T(8,128)} %get-tuple-element.52), channel_id=1, source_target_pairs={{0,2},{1,3},{2,0},{3,1},{4,6},{5,7},{6,4},{7,5},{8,10},{9,11},{10,... | collective-permute-start | bytes 2359304 | tf_op jit(solution)/shard_map/ppermute | solution.py:28
  326.6 35.3 %collective-permute-start.17 = (f32[2,4,192,128]{3,2,1,0:T(8,128)}, f32[2,4,192,128]{3,2,1,0:T(8,128)S(1)}, u32[]{:S(2)}, u32[]{:S(2)}) collective-permute-start(f32[2,4,192,128]{3,2,1,0:T(8,128)} %get-tuple-element.53), channel_id=1, source_target_pairs={{0,3},{1,0},{2,1},{3,2},{4,7},{5,4},{6,5},{7,6},{8,11},{9,8},{10,9... | collective-permute-start | bytes 2359304 | tf_op jit(solution)/shard_map/ppermute | solution.py:28
  340.3 21.5 %copy-start.27 = (f32[2,4,192,128]{3,2,1,0:T(8,128)}, f32[2,4,192,128]{3,2,1,0:T(8,128)S(1)}, u32[]{:S(2)}) copy-start(f32[2,4,192,128]{3,2,1,0:T(8,128)S(1)} %collective-permute-done.15.refs_2_) | copy-start | bytes 2359300
  361.2 0.9 copy-start.28
  361.8 0.9 copy-start.29
  369.8 36.2 %copy-start.5 = (f32[4,32,32,128]{3,2,1,0:T(8,128)S(1)}, f32[4,32,32,128]{3,2,1,0:T(8,128)}, u32[]{:S(2)}) copy-start(f32[4,32,32,128]{3,2,1,0:T(8,128)} %eta.3) | copy-start | bytes 6291460
  383.7 74.7 %all-to-all-start.3 = ((f32[8,2,4,96,128]{4,3,2,1,0:T(8,128)}), f32[8,2,4,96,128]{4,3,2,1,0:T(8,128)}, u32[]{:S(2)}, u32[]{:S(2)}) async-start(f32[8,2,4,96,128]{4,3,2,1,0:T(8,128)} %back_rows.3), calls=%async_computation.3 | async-start | bytes 6291456 | tf_op jit(solution)/shard_map/all_to_all | solution.py:776
  404.0 2.1 copy-start.21
  404.0 32.5 %collective-permute-start.9 = (f32[120,24,128]{2,1,0:T(8,128)}, f32[120,24,128]{2,1,0:T(8,128)S(1)}, u32[]{:S(2)}, u32[]{:S(2)}) collective-permute-start(f32[120,24,128]{2,1,0:T(8,128)} %copy-done.22), channel_id=1, source_target_pairs={{0,1},{1,2},{2,3},{3,0},{4,5},{5,6},{6,7},{7,4},{8,9},{9,10},{10,1... | collective-permute-start | bytes 4423688 | tf_op jit(solution)/shard_map/ppermute | solution.py:28
  406.0 30.6 %slice-start = ((s8[9338880]{0:T(1024)(128)(4,1)}), s8[4194304]{0:T(1024)(128)(4,1)S(1)}, s32[]{:S(2)}) async-start(s8[9338880]{0:T(1024)(128)(4,1)} %bitcast.36), calls=%async_computation.4 | async-start | bytes 8388608
  406.2 33.7 %collective-permute-start.10 = (f32[120,24,128]{2,1,0:T(8,128)S(1)}, f32[120,24,128]{2,1,0:T(8,128)S(1)}, u32[]{:S(2)}, u32[]{:S(2)}) collective-permute-start(f32[120,24,128]{2,1,0:T(8,128)S(1)} %copy-done.21), channel_id=1, source_target_pairs={{0,3},{1,0},{2,1},{3,2},{4,7},{5,4},{6,5},{7,6},{8,11},{9,8},{10,9... | collective-permute-start | bytes 4423688 | tf_op jit(solution)/shard_map/ppermute | solution.py:28
  407.1 29.5 %slice-start.1 = ((s8[9338880]{0:T(1024)(128)(4,1)}), s8[4194304]{0:T(1024)(128)(4,1)S(1)}, s32[]{:S(2)}) async-start(s8[9338880]{0:T(1024)(128)(4,1)} %bitcast.36), calls=%async_computation.5 | async-start | bytes 8388608
  407.8 28.8 %slice-start.2 = ((s8[9338880]{0:T(1024)(128)(4,1)}), s8[950272]{0:T(1024)(128)(4,1)S(1)}, s32[]{:S(2)}) async-start(s8[9338880]{0:T(1024)(128)(4,1)} %bitcast.36), calls=%async_computation.6 | async-start | bytes 1900544
  462.2 46.0 %collective-permute-start.19 = (f32[24,128,128]{2,1,0:T(8,128)}, f32[24,128,128]{2,1,0:T(8,128)S(1)}, u32[]{:S(2)}, u32[]{:S(2)}) collective-permute-start(f32[24,128,128]{2,1,0:T(8,128)} %bitcast.38), channel_id=1, source_target_pairs={{0,28},{4,0},{8,4},{12,8},{16,12},{20,16},{24,20},{28,24},{1,29},{... | collective-permute-start | bytes 4718600 | tf_op jit(solution)/shard_map/ppermute | solution.py:28
  470.7 8.2 %copy-start.10 = (f32[4,32,32,128]{3,2,1,0:T(8,128)S(1)}, f32[4,32,32,128]{3,2,1,0:T(8,128)}, u32[]{:S(2)}) copy-start(f32[4,32,32,128]{3,2,1,0:T(8,128)} %pad_maximum_fusion.refs_4_.base) | copy-start | bytes 6291460
  472.2 35.9 %collective-permute-start.18 = (f32[96,24,128]{2,1,0:T(8,128)S(1)}, f32[96,24,128]{2,1,0:T(8,128)S(1)}, u32[]{:S(2)}, u32[]{:S(2)}) collective-permute-start(f32[96,24,128]{2,1,0:T(8,128)S(1)} %slice.300), channel_id=1, source_target_pairs={{0,3},{1,0},{2,1},{3,2},{4,7},{5,4},{6,5},{7,6},{8,11},{9,8},{10,9... | collective-permute-start | bytes 3538952 | tf_op jit(solution)/shard_map/ppermute | solution.py:28
  475.3 32.9 %collective-permute-start.20 = (f32[24,24,128]{2,1,0:T(8,128)S(1)}, f32[24,24,128]{2,1,0:T(8,128)S(1)}, u32[]{:S(2)}, u32[]{:S(2)}) collective-permute-start(f32[24,24,128]{2,1,0:T(8,128)S(1)} %slice.301), channel_id=1, source_target_pairs={{0,31},{1,28},{2,29},{3,30},{4,3},{5,0},{6,1},{7,2},{8,7},{9,4},{1... | collective-permute-start | bytes 884744 | tf_op jit(solution)/shard_map/ppermute | solution.py:790
  478.9 2.8 copy-start.8

commit v5 on v4

--- a/solution.py
+++ b/solution.py
@@ -101,9 +101,8 @@
     for parity in range(2):
         angles = angle_of(m[:, None] * (2 * m[None, :] + parity), length)
         c, s = np.cos(angles), np.sin(angles)
-        forward.append(np.block([[c, -s], [s, c]]))
-        c, s = c.T, s.T
-        inverse.append(np.block([[c, s], [-s, c]]))
+        forward.append(np.stack([c, s - c, c + s]))
+        inverse.append(np.stack([c.T, (s - c).T, (c + s).T]))
     return pair_of(np.array(forward)), pair_of(np.array(inverse))
 
 
@@ -152,6 +151,17 @@
 def cost(*arrays):
     size = sum(math.prod(array.shape) * 4 for array in arrays)
     return pl.CostEstimate(flops=0, bytes_accessed=5 * size, transcendentals=0)
+
+
+def complex_last(values, high, low, back):
+    middle = values.shape[1] // 2
+    re, im = values[:, :middle], values[:, middle:]
+    both = table_last(re + im, high[0], low[0])
+    if back:
+        pair = both - table_last(im, high[2], low[2]), both + table_last(re, high[1], low[1])
+    else:
+        pair = both + table_last(im, high[1], low[1]), both - table_last(re, high[2], low[2])
+    return jnp.concatenate(pair, axis=1)
 
 
 def params(mib):
@@ -361,7 +371,7 @@
     scratch, lines = refs[-2:]
     step = pl.program_id(0)
     rows, cols = main.shape[3], main.shape[4]
-    half_length = fwd_high.shape[1] // 2
+    half_length = fwd_high.shape[2]
 
     def gathered(body, overhang, slot):
         pieces = []
@@ -385,8 +395,8 @@
     def forward(body, overhang, slot):
         even, odd = gathered(body, overhang, slot)
         return (
-            table_last(even, fwd_high[0], fwd_low[0]),
-            table_last(odd, fwd_high[1], fwd_low[1]),
+            complex_last(even, fwd_high[0], fwd_low[0], False),
+            complex_last(odd, fwd_high[1], fwd_low[1], False),
         )
 
     def scaled(spectrum, gain):
@@ -414,8 +424,8 @@
             scratch[0] += even
             scratch[1] += odd
 
-    even = table_last(scratch[0], inv_high[0], inv_low[0])
-    odd = table_last(scratch[1], inv_high[1], inv_low[1])
+    even = complex_last(scratch[0], inv_high[0], inv_low[0], True)
+    odd = complex_last(scratch[1], inv_high[1], inv_low[1], True)
     lower, upper = even + odd, even - odd
     for ri in range(2):
         take = slice(ri * half_length, (ri + 1) * half_length)

time: 513 us -> 512 us (level)
  no operation moved by 1% of the time
where the time goes in v5:
time: 512 us; the launch traced here: 510 us
  waiting for transfers between devices  264 us (52%)
  Pallas kernels  94.6 us (18%)
  starting transfers between devices  84.1 us (16%)
  local copies, waits for them, and re-layouts  40.9 us (8%)
  between operations  16 us (3%)
  other arithmetic  10.7 us (2%)
    ppermute x13, waiting for transfers between devices, from_behind(): lax.ppermute(shard, axis, [(i, (i + by) % peers) for i in range(peers)])  89.8 us
    ppermute x3, waiting for transfers between devices, on_device(): mirror = [lax.ppermute(planes, 'px', opposite) for planes in first_leg]  55.5 us
    all_to_all x4, waiting for transfers between devices, exchange(): return lax.all_to_all(shard, axis, split_axis=0, concat_axis=0, tiled=True)  54.6 us
    all_to_all x4, starting transfers between devices, exchange(): return lax.all_to_all(shard, axis, split_axis=0, concat_axis=0, tiled=True)  42.7 us
    ppermute x3, waiting for transfers between devices, on_device(): first_leg = [lax.ppermute(planes, 'py', facing) for planes in mirror[1:]]  39.1 us
    unnamed x66, local copies, waits for them, and re-layouts  32.3 us
    ppermute x1, waiting for transfers between devices, potential_pieces(): corner = lax.ppermute(rows[:, :over_y], ('px', 'py'), pairs)  24.8 us
    ppermute x13, starting transfers between devices, from_behind(): lax.ppermute(shard, axis, [(i, (i + by) % peers) for i in range(peers)])  23.9 us
  transfers between devices with their start and end apart: 25, of which 15 were waited for; matrix products, arithmetic and copies ran while one was open for 3% of the time, Pallas kernels for 11%

profile of v5, /device:TPU:5, one launch (start us, length us, event | category | flops | bytes accessed | tf_op | source)
XLA Modules:
  0.0 510.1 jit_solution(10650003115808553692)
XLA Ops:
  2.5 1.6 copy-done.3
  5.6 4.4 box_depth.1.refs_3_
  10.0 5.9 %all-to-all-start = ((f32[8,520,128]{2,1,0:T(8,128)}), f32[8,520,128]{2,1,0:T(8,128)}, u32[]{:S(2)}, u32[]{:S(2)}) async-start(f32[8,520,128]{2,1,0:T(8,128)} %box_depth.1.refs_3_), calls=%async_computation | async-start | bytes 4259840 | tf_op jit(solution)/shard_map/all_to_all | solution.py:786
  16.9 1.3 collective-permute-start
  18.3 2.8 copy-done
  22.1 2.1 mirror_planes.3.refs_5_
  24.2 1.2 collective-permute-start.3
  25.5 2.3 mirror_planes.4.refs_5_
  27.8 3.6 mirror_planes.5.refs_3_
  32.0 1.1 collective-permute-start.5
  33.1 19.8 %collective-permute-done.3 = f32[3,192,512]{2,1,0:T(8,128)S(1)} collective-permute-done((f32[3,192,512]{2,1,0:T(8,128)S(1)}, f32[3,192,512]{2,1,0:T(8,128)S(1)}, u32[]{:S(2)}, u32[]{:S(2)}) %collective-permute-start.3) | collective-permute-done | bytes 1179680 | tf_op jit(solution)/shard_map/ppermute | solution.py:865
  54.0 3.0 collective-permute-start.7
  57.8 2.7 collective-permute-start.4
  60.7 2.8 copy-done.1
  64.5 3.5 order_planes.3.refs_2_.refs_5_.refs_3_
  68.0 1.7 occupancy_patch.1
  69.8 3.6 copy-done.6
  73.4 1.3 copy-done.18
  74.7 1.2 copy-done.19
  75.9 5.1 all-to-all-done.refs_1_.refs_2_
  81.0 1.4 fusion.56
  82.4 1.3 convert_element_type.17.refs_0_
  83.6 19.3 %collective-permute-done.5.refs_8_ = f32[2,192,512]{2,1,0:T(8,128)} collective-permute-done((f32[2,192,512]{2,1,0:T(8,128)}, f32[2,192,512]{2,1,0:T(8,128)}, u32[]{:S(2)}, u32[]{:S(2)}) %collective-permute-start.5) | collective-permute-done | bytes 786464 | tf_op jit(solution)/shard_map/ppermute | solution.py:865
  102.9 20.0 %box_rows.1 = f32[4,2,11,192,128]{4,3,2,1,0:T(8,128)} custom-call(s32[64]{0:T(128)} %convert_element_type.17.refs_0_, f32[8,520,128]{2,1,0:T(8,128)} %all-to-all-done.refs_1_.refs_2_, f32[8,520,128]{2,1,0:T(8,128)} %all-to-all-done.refs_1_.refs_2_, bf16[3,3,256,256]{3,2,1,0:T(8,128)(2,1)} %constant.127.clone.refs_3_, ...), custom_call_target="tpu_custom_call" | custom-call | bytes 53903360 | tf_op jit(solution)/shard_map/box_rows/pallas_call | solution.py:333
  123.0 6.0 %all-to-all-start.1 = ((f32[4,2,11,192,128]{4,3,2,1,0:T(8,128)}), f32[4,2,11,192,128]{4,3,2,1,0:T(8,128)}, u32[]{:S(2)}, u32[]{:S(2)}) async-start(f32[4,2,11,192,128]{4,3,2,1,0:T(8,128)} %box_rows.1), calls=%async_computation.1 | async-start | bytes 17301504 | tf_op jit(solution)/shard_map/all_to_all | solution.py:786
  129.0 12.1 %collective-permute-start.1 = (f32[24,152,128]{2,1,0:T(8,128)}, f32[24,152,128]{2,1,0:T(8,128)}, u32[]{:S(2)}, u32[]{:S(2)}) collective-permute-start(f32[24,152,128]{2,1,0:T(8,128)} %copy-done.19), channel_id=1, source_target_pairs={{0,4},{4,8},{8,12},{12,16},{16,20},{20,24},{24,28},{28,0},{1,5},{5... | collective-permute-start | bytes 5603336 | tf_op jit(solution)/shard_map/ppermute | solution.py:28
  141.0 5.2 %collective-permute-start.8 = (f32[2,192,512]{2,1,0:T(8,128)}, f32[2,192,512]{2,1,0:T(8,128)}, u32[]{:S(2)}, u32[]{:S(2)}) collective-permute-start(f32[2,192,512]{2,1,0:T(8,128)} %collective-permute-done.5.refs_8_), channel_id=1, source_target_pairs={{0,28},{4,24},{8,20},{12,16},{16,12},{20,8},{24,4},{28,0},{1,29},{... | collective-permute-start | bytes 2359304 | tf_op jit(solution)/shard_map/ppermute | solution.py:873
  146.3 2.3 select_bitcast_fusion
  148.6 55.5 %collective-permute-done.8.refs_7_.refs_9_ = f32[2,192,512]{2,1,0:T(8,128)} collective-permute-done((f32[2,192,512]{2,1,0:T(8,128)}, f32[2,192,512]{2,1,0:T(8,128)}, u32[]{:S(2)}, u32[]{:S(2)}) %collective-permute-start.8) | collective-permute-done | bytes 786464 | tf_op jit(solution)/shard_map/ppermute | solution.py:873
  204.1 20.1 %all-to-all-done.1.refs_1_.refs_2_.refs_3_.refs_4_ = f32[4,2,11,192,128]{4,3,2,1,0:T(8,128)} async-done(((f32[4,2,11,192,128]{4,3,2,1,0:T(8,128)}), f32[4,2,11,192,128]{4,3,2,1,0:T(8,128)}, u32[]{:S(2)}, u32[]{:S(2)}) %all-to-all-start.1) | async-done | bytes 8650784 | tf_op jit(solution)/shard_map/all_to_all | solution.py:786
  224.1 12.1 %grid_columns.2 = (f32[2,4,192,128]{3,2,1,0:T(8,128)}, f32[2,4,192,128]{3,2,1,0:T(8,128)}, f32[2,4,192,128]{3,2,1,0:T(8,128)}, f32[2,4,192,128]{3,2,1,0:T(8,128)}) custom-call(s32[1]{0:T(128)} %bitcast.1.refs_0_, f32[4,2,11,192,128]{4,3,2,1,0:T(8,128)} %all-to-all-done.1.refs_1_.refs_2_.refs_3_.refs_4_, ...), custom_call_target="tpu_custom_call" | custom-call | bytes 47185920 | tf_op jit(solution)/shard_map/grid_columns/pallas_call | solution.py:470
  237.1 1.4 collective-permute-start.12
  238.5 23.6 %collective-permute-done.1.refs_1_ = f32[24,152,128]{2,1,0:T(8,128)} collective-permute-done((f32[24,152,128]{2,1,0:T(8,128)}, f32[24,152,128]{2,1,0:T(8,128)}, u32[]{:S(2)}, u32[]{:S(2)}) %collective-permute-start.1) | collective-permute-done | bytes 1867808 | tf_op jit(solution)/shard_map/ppermute | solution.py:28
  263.3 3.6 copy-done.7
  267.0 1.1 copy-done.12
  268.1 3.6 join_rows.1
  271.7 3.6 copy-done.9
  275.4 1.2 copy-done.20
  276.5 1.1 copy-done.22
  279.1 7.2 %back_rows.2.refs_9_ = f32[8,2,4,96,128]{4,3,2,1,0:T(8,128)} custom-call(s32[1]{0:T(128)} %bitcast.1.refs_0_, f32[2,4,192,128]{3,2,1,0:T(8,128)} %get-tuple-element.43.refs_3_.refs_1_, f32[2,4,192,128]{3,2,1,0:T(8,128)} %copy-done.24, f32[2,4,192,128]{3,2,1,0:T(8,128)} %copy-done.25, f32[2,4,192,128]{3,2,1,0:T(8,128)} %copy-done.26, ...), custom_call_target="tpu_custom_call" | custom-call | bytes 31457280 | tf_op jit(solution)/shard_map/back_rows/pallas_call | solution.py:535
  286.2 26.2 %all-to-all-start.2 = ((f32[8,2,4,96,128]{4,3,2,1,0:T(8,128)}), f32[8,2,4,96,128]{4,3,2,1,0:T(8,128)}, u32[]{:S(2)}, u32[]{:S(2)}) async-start(f32[8,2,4,96,128]{4,3,2,1,0:T(8,128)} %back_rows.2.refs_9_), calls=%async_computation.2 | async-start | bytes 6291456 | tf_op jit(solution)/shard_map/all_to_all | solution.py:786
  312.4 9.6 %grid_columns.3 = (f32[2,4,192,128]{3,2,1,0:T(8,128)}, f32[2,4,192,128]{3,2,1,0:T(8,128)}, f32[2,4,192,128]{3,2,1,0:T(8,128)}, f32[2,4,192,128]{3,2,1,0:T(8,128)}) custom-call(s32[1]{0:T(128)} %bitcast.1.refs_0_, f32[4,2,11,192,128]{4,3,2,1,0:T(8,128)} %all-to-all-done.1.refs_1_.refs_2_.refs_3_.refs_4_, ...), custom_call_target="tpu_custom_call" | custom-call | bytes 47185920 | tf_op jit(solution)/shard_map/grid_columns/pallas_call | solution.py:470
  322.6 1.7 collective-permute-start.16
  324.6 13.5 %collective-permute-done.15.refs_2_ = f32[2,4,192,128]{3,2,1,0:T(8,128)S(1)} collective-permute-done((f32[2,4,192,128]{3,2,1,0:T(8,128)}, f32[2,4,192,128]{3,2,1,0:T(8,128)S(1)}, u32[]{:S(2)}, u32[]{:S(2)}) %collective-permute-start.15) | collective-permute-done | bytes 786464 | tf_op jit(solution)/shard_map/ppermute | solution.py:28
  338.0 20.9 %collective-permute-done.16.refs_3_ = f32[2,4,192,128]{3,2,1,0:T(8,128)S(1)} collective-permute-done((f32[2,4,192,128]{3,2,1,0:T(8,128)}, f32[2,4,192,128]{3,2,1,0:T(8,128)S(1)}, u32[]{:S(2)}, u32[]{:S(2)}) %collective-permute-start.16) | collective-permute-done | bytes 786464 | tf_op jit(solution)/shard_map/ppermute | solution.py:28
  360.4 7.1 %back_rows.3 = f32[8,2,4,96,128]{4,3,2,1,0:T(8,128)} custom-call(s32[1]{0:T(128)} %bitcast.1.refs_0_, f32[2,4,192,128]{3,2,1,0:T(8,128)} %get-tuple-element.50.refs_1_, f32[2,4,192,128]{3,2,1,0:T(8,128)} %copy-done.27, f32[2,4,192,128]{3,2,1,0:T(8,128)} %copy-done.28, f32[2,4,192,128]{3,2,1,0:T(8,128)} %copy-done.29, ...), custom_call_target="tpu_custom_call" | custom-call | bytes 31457280 | tf_op jit(solution)/shard_map/back_rows/pallas_call | solution.py:535
  367.5 15.1 %all-to-all-done.2 = f32[8,2,4,96,128]{4,3,2,1,0:T(8,128)} async-done(((f32[8,2,4,96,128]{4,3,2,1,0:T(8,128)}), f32[8,2,4,96,128]{4,3,2,1,0:T(8,128)}, u32[]{:S(2)}, u32[]{:S(2)}) %all-to-all-start.2) | async-done | bytes 3145760 | tf_op jit(solution)/shard_map/all_to_all | solution.py:786
  382.6 4.6 all-to-all-start.3
  402.9 1.9 collective-permute-start.9
  407.4 28.0 %collective-permute-done.9 = f32[120,24,128]{2,1,0:T(8,128)S(1)} collective-permute-done((f32[120,24,128]{2,1,0:T(8,128)}, f32[120,24,128]{2,1,0:T(8,128)S(1)}, u32[]{:S(2)}, u32[]{:S(2)}) %collective-permute-start.9) | collective-permute-done | bytes 1474592 | tf_op jit(solution)/shard_map/ppermute | solution.py:28
  435.8 2.9 collective-permute-done.10
  439.0 1.1 fusion.12
  440.2 1.2 fusion.6
  441.4 1.5 pad_maximum_fusion.refs_4_.base
  442.9 14.4 %all-to-all-done.3 = f32[8,2,4,96,128]{4,3,2,1,0:T(8,128)} async-done(((f32[8,2,4,96,128]{4,3,2,1,0:T(8,128)}), f32[8,2,4,96,128]{4,3,2,1,0:T(8,128)}, u32[]{:S(2)}, u32[]{:S(2)}) %all-to-all-start.3) | async-done | bytes 3145760 | tf_op jit(solution)/shard_map/all_to_all | solution.py:786
  457.2 3.8 back_depth.2
  461.1 8.5 %back_depth.3 = f32[32,3,128,128]{3,2,1,0:T(8,128)} custom-call(f32[64,3,32,128]{3,2,1,0:T(8,128)} %bitcast.19.refs_0_, f32[64,3,32,128]{3,2,1,0:T(8,128)} %bitcast.20.refs_1_, bf16[128,128]{1,0:T(8,128)(2,1)} %constant.135.clone.refs_2_, bf16[128,128]{1,0:T(8,128)(2,1)} %constant.136.clone.refs_3_, f32[24,128,128]{2,1,0:T(8,128)} %bitcast.39), custom_call_target="tpu_custom_call" | custom-call | bytes 62914560 | tf_op jit(solution)/shard_map/back_depth/pallas_call | solution.py:577
  469.6 1.5 slice.300
  471.1 2.1 collective-permute-start.18
  474.2 3.6 collective-permute-start.20
  477.8 2.8 copy-done.8
  480.6 1.7 apply_potential.2.base
  482.2 24.8 %collective-permute-done.20.refs_2_ = f32[24,24,128]{2,1,0:T(8,128)S(1)} collective-permute-done((f32[24,24,128]{2,1,0:T(8,128)S(1)}, f32[24,24,128]{2,1,0:T(8,128)S(1)}, u32[]{:S(2)}, u32[]{:S(2)}) %collective-permute-start.20) | collective-permute-done | bytes 294944 | tf_op jit(solution)/shard_map/ppermute | solution.py:800
  507.0 3.0 apply_potential.3
  (101 shorter events, 20.0 us)
Async XLA Ops:
  2.4 1.6 copy-start.3
  4.0 0.8 copy-start.16
  4.8 0.8 copy-start.17
  10.0 8.3 %copy-start.13 = (bf16[512,512]{1,0:T(8,128)(2,1)S(1)}, bf16[512,512]{1,0:T(8,128)(2,1)}, u32[]{:S(2)}) copy-start(bf16[512,512]{1,0:T(8,128)(2,1)} %constant.124.clone.refs_2_) | copy-start | bytes 1572868
  10.0 71.0 %all-to-all-start = ((f32[8,520,128]{2,1,0:T(8,128)}), f32[8,520,128]{2,1,0:T(8,128)}, u32[]{:S(2)}, u32[]{:S(2)}) async-start(f32[8,520,128]{2,1,0:T(8,128)} %box_depth.1.refs_3_), calls=%async_computation | async-start | bytes 4259840 | tf_op jit(solution)/shard_map/all_to_all | solution.py:786
  16.9 4.6 collective-permute-start
  18.3 2.8 copy-start
  21.1 1.0 copy-start.11
  21.1 1.0 copy-start.15
  24.2 28.7 %collective-permute-start.3 = (f32[3,192,512]{2,1,0:T(8,128)S(1)}, f32[3,192,512]{2,1,0:T(8,128)S(1)}, u32[]{:S(2)}, u32[]{:S(2)}) collective-permute-start(f32[3,192,512]{2,1,0:T(8,128)S(1)} %mirror_planes.3.refs_5_), channel_id=1, source_target_pairs={{0,3},{1,2},{2,1},{3,0},{4,7},{5,6},{6,5},{7,4},{8,11},{9,10},{10,... | collective-permute-start | bytes 3538952 | tf_op jit(solution)/shard_map/ppermute | solution.py:865
  31.4 71.6 %collective-permute-start.6 = (f32[4,192,512]{2,1,0:T(8,128)}, f32[4,192,512]{2,1,0:T(8,128)}, u32[]{:S(2)}, u32[]{:S(2)}) collective-permute-start(f32[4,192,512]{2,1,0:T(8,128)} %mirror_planes.5.refs_3_), channel_id=1, source_target_pairs={{0,3},{1,2},{2,1},{3,0},{4,7},{5,6},{6,5},{7,4},{8,11},{9,10},{10,... | collective-permute-start | bytes 4718600 | tf_op jit(solution)/shard_map/ppermute | solution.py:865
  32.0 70.9 %collective-permute-start.5 = (f32[2,192,512]{2,1,0:T(8,128)}, f32[2,192,512]{2,1,0:T(8,128)}, u32[]{:S(2)}, u32[]{:S(2)}) collective-permute-start(f32[2,192,512]{2,1,0:T(8,128)} %mirror_planes.4.refs_5_), channel_id=1, source_target_pairs={{0,3},{1,2},{2,1},{3,0},{4,7},{5,6},{6,5},{7,4},{8,11},{9,10},{10,... | collective-permute-start | bytes 2359304 | tf_op jit(solution)/shard_map/ppermute | solution.py:865
  52.9 7.7 %copy-start.23 = (f32[3,192,512]{2,1,0:T(8,128)}, f32[3,192,512]{2,1,0:T(8,128)S(1)}, u32[]{:S(2)}) copy-start(f32[3,192,512]{2,1,0:T(8,128)S(1)} %collective-permute-done.3) | copy-start | bytes 3538948
  54.0 48.9 %collective-permute-start.7 = (f32[2,192,512]{2,1,0:T(8,128)}, f32[2,192,512]{2,1,0:T(8,128)}, u32[]{:S(2)}, u32[]{:S(2)}) collective-permute-start(f32[2,192,512]{2,1,0:T(8,128)} %slice.280.refs_7_), channel_id=1, source_target_pairs={{0,28},{4,24},{8,20},{12,16},{16,12},{20,8},{24,4},{28,0},{1,29},{... | collective-permute-start | bytes 2359304 | tf_op jit(solution)/shard_map/ppermute | solution.py:873
  57.8 45.1 %collective-permute-start.4 = (f32[1,192,512]{2,1,0:T(8,128)}, f32[1,192,512]{2,1,0:T(8,128)}, u32[]{:S(2)}, u32[]{:S(2)}) collective-permute-start(f32[1,192,512]{2,1,0:T(8,128)} %slice_select_fusion.1), channel_id=1, source_target_pairs={{0,16},{4,28},{8,24},{12,20},{1,17},{5,29},{9,25},{13,21},{2,18},{... | collective-permute-start | bytes 1179656 | tf_op jit(solution)/shard_map/ppermute | solution.py:870
  60.7 2.8 copy-start.1
  63.5 1.0 copy-start.14
  64.5 3.5 copy-start.4
  68.0 78.2 %copy-start.2 = (f32[8,192,512]{2,1,0:T(8,128)}, f32[8,192,512]{2,1,0:T(8,128)S(1)}, u32[]{:S(2)}) copy-start(f32[8,192,512]{2,1,0:T(8,128)S(1)} %order_planes.3.refs_2_.refs_5_.refs_3_) | copy-start | bytes 9437188
  69.8 3.6 copy-start.6
  73.4 1.3 copy-start.18
  74.7 1.2 copy-start.19
  123.0 101.2 %all-to-all-start.1 = ((f32[4,2,11,192,128]{4,3,2,1,0:T(8,128)}), f32[4,2,11,192,128]{4,3,2,1,0:T(8,128)}, u32[]{:S(2)}, u32[]{:S(2)}) async-start(f32[4,2,11,192,128]{4,3,2,1,0:T(8,128)} %box_rows.1), calls=%async_computation.1 | async-start | bytes 17301504 | tf_op jit(solution)/shard_map/all_to_all | solution.py:786
  129.0 133.2 %collective-permute-start.1 = (f32[24,152,128]{2,1,0:T(8,128)}, f32[24,152,128]{2,1,0:T(8,128)}, u32[]{:S(2)}, u32[]{:S(2)}) collective-permute-start(f32[24,152,128]{2,1,0:T(8,128)} %copy-done.19), channel_id=1, source_target_pairs={{0,4},{4,8},{8,12},{12,16},{16,20},{20,24},{24,28},{28,0},{1,5},{5... | collective-permute-start | bytes 5603336 | tf_op jit(solution)/shard_map/ppermute | solution.py:28
  141.0 122.3 %collective-permute-start.2 = (f32[24,152,128]{2,1,0:T(8,128)}, f32[24,152,128]{2,1,0:T(8,128)}, u32[]{:S(2)}, u32[]{:S(2)}) collective-permute-start(f32[24,152,128]{2,1,0:T(8,128)} %copy-done.18), channel_id=1, source_target_pairs={{0,28},{4,0},{8,4},{12,8},{16,12},{20,16},{24,20},{28,24},{1,29},{... | collective-permute-start | bytes 5603336 | tf_op jit(solution)/shard_map/ppermute | solution.py:28
  141.0 63.0 %collective-permute-start.8 = (f32[2,192,512]{2,1,0:T(8,128)}, f32[2,192,512]{2,1,0:T(8,128)}, u32[]{:S(2)}, u32[]{:S(2)}) collective-permute-start(f32[2,192,512]{2,1,0:T(8,128)} %collective-permute-done.5.refs_8_), channel_id=1, source_target_pairs={{0,28},{4,24},{8,20},{12,16},{16,12},{20,8},{24,4},{28,0},{1,29},{... | collective-permute-start | bytes 2359304 | tf_op jit(solution)/shard_map/ppermute | solution.py:873
  146.2 131.4 %collective-permute-start.14 = (f32[4,192,512]{2,1,0:T(8,128)}, f32[4,192,512]{2,1,0:T(8,128)}, u32[]{:S(2)}, u32[]{:S(2)}) collective-permute-start(f32[4,192,512]{2,1,0:T(8,128)} %collective-permute-done.6.refs_9_), channel_id=1, source_target_pairs={{0,28},{4,24},{8,20},{12,16},{16,12},{20,8},{24,4},{28,0},{1,29},{... | collective-permute-start | bytes 4718600 | tf_op jit(solution)/shard_map/ppermute | solution.py:873
  236.3 41.4 %collective-permute-start.11 = (f32[2,4,192,128]{3,2,1,0:T(8,128)}, f32[2,4,192,128]{3,2,1,0:T(8,128)S(1)}, u32[]{:S(2)}, u32[]{:S(2)}) collective-permute-start(f32[2,4,192,128]{3,2,1,0:T(8,128)} %get-tuple-element.47), channel_id=1, source_target_pairs={{0,1},{1,2},{2,3},{3,0},{4,5},{5,6},{6,7},{7,4},{8,9},{9,10},{10,1... | collective-permute-start | bytes 2359304 | tf_op jit(solution)/shard_map/ppermute | solution.py:28
  237.1 40.5 %collective-permute-start.12 = (f32[2,4,192,128]{3,2,1,0:T(8,128)}, f32[2,4,192,128]{3,2,1,0:T(8,128)S(1)}, u32[]{:S(2)}, u32[]{:S(2)}) collective-permute-start(f32[2,4,192,128]{3,2,1,0:T(8,128)} %get-tuple-element.48), channel_id=1, source_target_pairs={{0,2},{1,3},{2,0},{3,1},{4,6},{5,7},{6,4},{7,5},{8,10},{9,11},{10,... | collective-permute-start | bytes 2359304 | tf_op jit(solution)/shard_map/ppermute | solution.py:28
  262.2 15.5 %collective-permute-start.13 = (f32[2,4,192,128]{3,2,1,0:T(8,128)}, f32[2,4,192,128]{3,2,1,0:T(8,128)S(1)}, u32[]{:S(2)}, u32[]{:S(2)}) collective-permute-start(f32[2,4,192,128]{3,2,1,0:T(8,128)} %get-tuple-element.49), channel_id=1, source_target_pairs={{0,3},{1,0},{2,1},{3,2},{4,7},{5,4},{6,5},{7,6},{8,11},{9,8},{10,9... | collective-permute-start | bytes 2359304 | tf_op jit(solution)/shard_map/ppermute | solution.py:28
  263.3 3.7 copy-start.7
  267.0 1.1 copy-start.12
  271.7 3.6 copy-start.9
  275.4 1.2 copy-start.20
  276.5 1.1 copy-start.22
  277.6 0.9 copy-start.24
  277.7 1.1 copy-start.25
  277.7 1.4 copy-start.26
  286.2 96.3 %all-to-all-start.2 = ((f32[8,2,4,96,128]{4,3,2,1,0:T(8,128)}), f32[8,2,4,96,128]{4,3,2,1,0:T(8,128)}, u32[]{:S(2)}, u32[]{:S(2)}) async-start(f32[8,2,4,96,128]{4,3,2,1,0:T(8,128)} %back_rows.2.refs_9_), calls=%async_computation.2 | async-start | bytes 6291456 | tf_op jit(solution)/shard_map/all_to_all | solution.py:786
  322.1 16.0 %collective-permute-start.15 = (f32[2,4,192,128]{3,2,1,0:T(8,128)}, f32[2,4,192,128]{3,2,1,0:T(8,128)S(1)}, u32[]{:S(2)}, u32[]{:S(2)}) collective-permute-start(f32[2,4,192,128]{3,2,1,0:T(8,128)} %get-tuple-element.51), channel_id=1, source_target_pairs={{0,1},{1,2},{2,3},{3,0},{4,5},{5,6},{6,7},{7,4},{8,9},{9,10},{10,1... | collective-permute-start | bytes 2359304 | tf_op jit(solution)/shard_map/ppermute | solution.py:28
  322.6 36.3 %collective-permute-start.16 = (f32[2,4,192,128]{3,2,1,0:T(8,128)}, f32[2,4,192,128]{3,2,1,0:T(8,128)S(1)}, u32[]{:S(2)}, u32[]{:S(2)}) collective-permute-start(f32[2,4,192,128]{3,2,1,0:T(8,128)} %get-tuple-element.52), channel_id=1, source_target_pairs={{0,2},{1,3},{2,0},{3,1},{4,6},{5,7},{6,4},{7,5},{8,10},{9,11},{10,... | collective-permute-start | bytes 2359304 | tf_op jit(solution)/shard_map/ppermute | solution.py:28
  324.3 35.3 %collective-permute-start.17 = (f32[2,4,192,128]{3,2,1,0:T(8,128)}, f32[2,4,192,128]{3,2,1,0:T(8,128)S(1)}, u32[]{:S(2)}, u32[]{:S(2)}) collective-permute-start(f32[2,4,192,128]{3,2,1,0:T(8,128)} %get-tuple-element.53), channel_id=1, source_target_pairs={{0,3},{1,0},{2,1},{3,2},{4,7},{5,4},{6,5},{7,6},{8,11},{9,8},{10,9... | collective-permute-start | bytes 2359304 | tf_op jit(solution)/shard_map/ppermute | solution.py:28
  338.0 21.5 %copy-start.27 = (f32[2,4,192,128]{3,2,1,0:T(8,128)}, f32[2,4,192,128]{3,2,1,0:T(8,128)S(1)}, u32[]{:S(2)}) copy-start(f32[2,4,192,128]{3,2,1,0:T(8,128)S(1)} %collective-permute-done.15.refs_2_) | copy-start | bytes 2359300
  358.9 0.9 copy-start.28
  359.5 0.9 copy-start.29
  367.5 37.3 %copy-start.5 = (f32[4,32,32,128]{3,2,1,0:T(8,128)S(1)}, f32[4,32,32,128]{3,2,1,0:T(8,128)}, u32[]{:S(2)}) copy-start(f32[4,32,32,128]{3,2,1,0:T(8,128)} %eta.3) | copy-start | bytes 6291460
  382.6 74.7 %all-to-all-start.3 = ((f32[8,2,4,96,128]{4,3,2,1,0:T(8,128)}), f32[8,2,4,96,128]{4,3,2,1,0:T(8,128)}, u32[]{:S(2)}, u32[]{:S(2)}) async-start(f32[8,2,4,96,128]{4,3,2,1,0:T(8,128)} %back_rows.3), calls=%async_computation.3 | async-start | bytes 6291456 | tf_op jit(solution)/shard_map/all_to_all | solution.py:786
  402.9 2.1 copy-start.21
  402.9 32.5 %collective-permute-start.9 = (f32[120,24,128]{2,1,0:T(8,128)}, f32[120,24,128]{2,1,0:T(8,128)S(1)}, u32[]{:S(2)}, u32[]{:S(2)}) collective-permute-start(f32[120,24,128]{2,1,0:T(8,128)} %copy-done.22), channel_id=1, source_target_pairs={{0,1},{1,2},{2,3},{3,0},{4,5},{5,6},{6,7},{7,4},{8,9},{9,10},{10,1... | collective-permute-start | bytes 4423688 | tf_op jit(solution)/shard_map/ppermute | solution.py:28
  404.8 30.6 %slice-start = ((s8[9338880]{0:T(1024)(128)(4,1)}), s8[4194304]{0:T(1024)(128)(4,1)S(1)}, s32[]{:S(2)}) async-start(s8[9338880]{0:T(1024)(128)(4,1)} %bitcast.36), calls=%async_computation.4 | async-start | bytes 8388608
  405.0 33.7 %collective-permute-start.10 = (f32[120,24,128]{2,1,0:T(8,128)S(1)}, f32[120,24,128]{2,1,0:T(8,128)S(1)}, u32[]{:S(2)}, u32[]{:S(2)}) collective-permute-start(f32[120,24,128]{2,1,0:T(8,128)S(1)} %copy-done.21), channel_id=1, source_target_pairs={{0,3},{1,0},{2,1},{3,2},{4,7},{5,4},{6,5},{7,6},{8,11},{9,8},{10,9... | collective-permute-start | bytes 4423688 | tf_op jit(solution)/shard_map/ppermute | solution.py:28
  405.9 29.5 %slice-start.1 = ((s8[9338880]{0:T(1024)(128)(4,1)}), s8[4194304]{0:T(1024)(128)(4,1)S(1)}, s32[]{:S(2)}) async-start(s8[9338880]{0:T(1024)(128)(4,1)} %bitcast.36), calls=%async_computation.5 | async-start | bytes 8388608
  406.7 28.8 %slice-start.2 = ((s8[9338880]{0:T(1024)(128)(4,1)}), s8[950272]{0:T(1024)(128)(4,1)S(1)}, s32[]{:S(2)}) async-start(s8[9338880]{0:T(1024)(128)(4,1)} %bitcast.36), calls=%async_computation.6 | async-start | bytes 1900544
  461.1 46.0 %collective-permute-start.19 = (f32[24,128,128]{2,1,0:T(8,128)}, f32[24,128,128]{2,1,0:T(8,128)S(1)}, u32[]{:S(2)}, u32[]{:S(2)}) collective-permute-start(f32[24,128,128]{2,1,0:T(8,128)} %bitcast.38), channel_id=1, source_target_pairs={{0,28},{4,0},{8,4},{12,8},{16,12},{20,16},{24,20},{28,24},{1,29},{... | collective-permute-start | bytes 4718600 | tf_op jit(solution)/shard_map/ppermute | solution.py:28
  469.6 8.2 %copy-start.10 = (f32[4,32,32,128]{3,2,1,0:T(8,128)S(1)}, f32[4,32,32,128]{3,2,1,0:T(8,128)}, u32[]{:S(2)}) copy-start(f32[4,32,32,128]{3,2,1,0:T(8,128)} %pad_maximum_fusion.refs_4_.base) | copy-start | bytes 6291460
  471.1 35.9 %collective-permute-start.18 = (f32[96,24,128]{2,1,0:T(8,128)S(1)}, f32[96,24,128]{2,1,0:T(8,128)S(1)}, u32[]{:S(2)}, u32[]{:S(2)}) collective-permute-start(f32[96,24,128]{2,1,0:T(8,128)S(1)} %slice.300), channel_id=1, source_target_pairs={{0,3},{1,0},{2,1},{3,2},{4,7},{5,4},{6,5},{7,6},{8,11},{9,8},{10,9... | collective-permute-start | bytes 3538952 | tf_op jit(solution)/shard_map/ppermute | solution.py:28
  474.2 32.9 %collective-permute-start.20 = (f32[24,24,128]{2,1,0:T(8,128)S(1)}, f32[24,24,128]{2,1,0:T(8,128)S(1)}, u32[]{:S(2)}, u32[]{:S(2)}) collective-permute-start(f32[24,24,128]{2,1,0:T(8,128)S(1)} %slice.301), channel_id=1, source_target_pairs={{0,31},{1,28},{2,29},{3,30},{4,3},{5,0},{6,1},{7,2},{8,7},{9,4},{1... | collective-permute-start | bytes 884744 | tf_op jit(solution)/shard_map/ppermute | solution.py:800
  477.8 2.8 copy-start.8
